TPU v7x, 32 devices: a whole 2x2x4 slice. The times are simulated.
32 devices in a mesh: section: 2 (over core), ctx: 4 (over z), tensor: 4 (over y, x).
Axes of the slice: x: 2, y: 2, z: 4, core: 2. Of those that a mesh axis runs over, the one named last changes fastest.
Arguments:
- inputs: bfloat16 [2, 4, 2, 512, 1536], P(None, 'ctx', None, 'tensor', 'section'), may hold values from -6 to 6
- cotangent: bfloat16 [2, 4, 2, 512, 1536], P(None, 'ctx', None, 'tensor', 'section'), may hold values from -6 to 6
- block_order: int32 [8], replicated, may hold values from 0 to 7, as said below
- attn_gain: float32 [2, 1536], P('section'), may hold values from 0.1 to 1.9
- w_query: bfloat16 [2, 1536, 1536], P('section', None, 'tensor'), may hold values from -0.15625 to 0.15625
- key_weight: bfloat16 [2, 1536, 768], P('section', None, 'tensor'), may hold values from -0.15625 to 0.15625
- value_weight: bfloat16 [2, 1536, 768], P('section', None, 'tensor'), may hold values from -0.15625 to 0.15625
- w_out: bfloat16 [2, 1536, 1536], P('section', 'tensor'), may hold values from -3 to 3
- mlp_gain: float32 [2, 1536], P('section'), may hold values from 0.1 to 1.9
- w_gate: bfloat16 [2, 1536, 4096], P('section', None, 'tensor'), may hold values from -0.15625 to 0.15625
- w_up: bfloat16 [2, 1536, 4096], P('section', None, 'tensor'), may hold values from -0.15625 to 0.15625
- w_down: bfloat16 [2, 4096, 1536], P('section', 'tensor'), may hold values from -0.09375 to 0.09375
Outputs:
- block_output: bfloat16 [2, 4, 2, 512, 1536], P(None, 'ctx', None, 'tensor', 'section')
- input_grad: float32 [2, 4, 2, 512, 1536], P(None, 'ctx', None, 'tensor', 'section')
- grad_attn_gain: float32 [2, 1536], P('section')
- grad_w_query: float32 [2, 1536, 1536], P('section', None, 'tensor')
- grad_w_key: float32 [2, 1536, 768], P('section', None, 'tensor')
- grad_w_value: float32 [2, 1536, 768], P('section', None, 'tensor')
- grad_w_out: float32 [2, 1536, 1536], P('section', 'tensor')
- grad_mlp_gain: float32 [2, 1536], P('section')
- grad_w_gate: float32 [2, 1536, 4096], P('section', None, 'tensor')
- grad_w_up: float32 [2, 1536, 4096], P('section', None, 'tensor')
- grad_w_down: float32 [2, 4096, 1536], P('section', 'tensor')
Inputs may be any that keep to these rules, and one draw needn't show every extreme that they name: Mirrored pairs: block_order[2 c] and block_order[2 c + 1] are c and 7 - c, in either order, so context rank c stores one early and one late block of positions (each 512 long); every block occurs once.
All inputs are finite; a program needn't handle non-finite values.
Results may differ from a plain program's by a relative error of at most 0.039.
Values may be sent and summed in bfloat16 or wider, within the bound.
A program may use at most 512 MiB of HBM per device.

v0:
```python
import jax
import jax.numpy as jnp
from jax import lax
from jax.sharding import PartitionSpec as P

HEAD_DIM = 96


EPSILON = 1e-05
ROPE_BASE = 100000.0


def partner(value, axis, stride):
    mask = 2**stride
    pairs = [(source, source ^ mask) for source in range(lax.axis_size(axis))]
    return lax.ppermute(value, axis, pairs)


def rms_norm(operand, gain_vec):
    return (
        operand
        * lax.rsqrt(jnp.mean(operand * operand, axis=-1, keepdims=True) + EPSILON)
        * gain_vec
    )


def rope_tables(positions):
    exponent = jnp.arange(0, HEAD_DIM, 2).astype(jnp.float32) / HEAD_DIM
    frequency = ROPE_BASE ** (-exponent)
    phases = positions.astype(jnp.float32)[:, None] * frequency[None, :]
    phases = jnp.concatenate([phases, phases], axis=-1)
    return (jnp.cos(phases), jnp.sin(phases))


def rotate(operand, cosine, sine):
    half_size = operand.shape[-1] // 2
    turned = jnp.concatenate([-operand[..., half_size:], operand[..., :half_size]], axis=-1)
    return operand * cosine[:, None, :] + turned * sine[:, None, :]


def rotate_back(operand, cosine, sine):
    half_size = operand.shape[-1] // 2
    scaled = operand * sine[:, None, :]
    turned = jnp.concatenate([scaled[..., half_size:], -scaled[..., :half_size]], axis=-1)
    return operand * cosine[:, None, :] + turned


def matmul(left, right):
    return jnp.dot(left, right, preferred_element_type=jnp.float32)


def matmul_back(left, right):
    return lax.dot_general(
        left, right, (((1,), (1,)), ((), ())), preferred_element_type=jnp.float32
    )


def outer_sum(left, right):
    return lax.dot_general(
        left, right, (((0,), (0,)), ((), ())), preferred_element_type=jnp.float32
    )


def hand_over(operand):
    return partner(operand, "section", 0)


def gather_rows(normalized_input):
    return lax.all_gather(normalized_input, "tensor", axis=0, tiled=True)


def gather_grads(grad_rows):
    return lax.all_gather(grad_rows, "tensor", axis=0, tiled=True)


def reduce_rows(full_rows, weight, sp_rows):

    def term_rows(row_start, row_count):
        return jnp.einsum("rjf,fd->rjd", full_rows, weight, preferred_element_type=jnp.float32)

    return lax.psum_scatter(
        term_rows(jnp.int32(0), sp_rows * lax.axis_size("tensor")).astype(jnp.bfloat16),
        "tensor",
        scatter_dimension=0,
        tiled=True,
    ).astype(jnp.float32)


def reduce_grads(operand_pairs, sp_rows):

    def term_rows(row_start, row_count):
        summed_terms = None
        for rows_full, weight in operand_pairs:
            addend = jnp.einsum(
                "rjf,df->rjd", rows_full, weight, preferred_element_type=jnp.float32
            )
            summed_terms = addend if summed_terms is None else summed_terms + addend
        return summed_terms

    return lax.psum_scatter(
        term_rows(jnp.int32(0), sp_rows * lax.axis_size("tensor")).astype(jnp.bfloat16),
        "tensor",
        scatter_dimension=0,
        tiled=True,
    ).astype(jnp.float32)


def attention_probs(query_rows, key_all, row_pos, key_pos):
    row_total = query_rows.shape[0]
    key_heads = key_all.reshape(-1, key_all.shape[-1] // HEAD_DIM, HEAD_DIM)
    kv_local = key_heads.shape[1]
    grouped = query_rows.reshape(row_total, kv_local, -1, HEAD_DIM)
    raw_scores = jnp.einsum(
        "rhgd,khd->hgrk", grouped, key_heads, preferred_element_type=jnp.float32
    ) * HEAD_DIM ** (-0.5)
    visible = row_pos[:, None] >= key_pos[None, :]
    masked = jnp.where(visible[None, None], raw_scores, -1e30)
    largest = jnp.max(masked, axis=-1, keepdims=True)
    powers = jnp.exp(masked - largest)
    return (powers / jnp.sum(powers, axis=-1, keepdims=True), grouped, key_heads)


def layer_forward(stream, params, tables):
    attn_gain, w_query, key_weight, value_weight, w_out, mlp_gain, w_gate, w_up, w_down = params
    row_cos, row_sin, row_pos, key_pos = tables
    sp_rows, pair_count, model_width = stream.shape
    normalized_input = rms_norm(stream, attn_gain).astype(jnp.bfloat16)
    normed_full = gather_rows(normalized_input)
    span_rows = normed_full.shape[0]
    flat_in = normed_full.reshape(-1, model_width)
    row_total = flat_in.shape[0]
    query_raw = matmul(flat_in, w_query).reshape(row_total, -1, HEAD_DIM)
    query_rows = rotate(query_raw, row_cos, row_sin).astype(jnp.bfloat16)
    key_raw = matmul(flat_in, key_weight).reshape(row_total, -1, HEAD_DIM)
    key_own = (
        rotate(key_raw, row_cos, row_sin).astype(jnp.bfloat16).reshape(span_rows, pair_count, -1)
    )
    value_own = (
        matmul(flat_in, value_weight).astype(jnp.bfloat16).reshape(span_rows, pair_count, -1)
    )
    key_all, value_all = (
        lax.all_gather(key_own, "ctx", axis=1, tiled=True),
        lax.all_gather(value_own, "ctx", axis=1, tiled=True),
    )
    attn_probs, grouped, key_heads = attention_probs(query_rows, key_all, row_pos, key_pos)
    value_heads = value_all.reshape(-1, key_heads.shape[1], HEAD_DIM)
    mixed_heads = jnp.einsum(
        "hgrk,khd->rhgd",
        attn_probs.astype(jnp.bfloat16),
        value_heads,
        preferred_element_type=jnp.float32,
    )
    mixed_full = mixed_heads.astype(jnp.bfloat16).reshape(span_rows, pair_count, -1)
    middle = stream + reduce_rows(mixed_full, w_out, sp_rows)
    normed_two = rms_norm(middle, mlp_gain).astype(jnp.bfloat16)
    normed_two_full = gather_rows(normed_two)
    flat_two = normed_two_full.reshape(-1, model_width)
    gate_value = matmul(flat_two, w_gate)
    up_value = matmul(flat_two, w_up)
    activated = (gate_value * jax.nn.sigmoid(gate_value) * up_value).astype(jnp.bfloat16)
    result = middle + reduce_rows(activated.reshape(span_rows, pair_count, -1), w_down, sp_rows)
    stored = (
        stream,
        normed_full,
        query_rows,
        key_own,
        value_own,
        mixed_full,
        middle,
        normed_two_full,
        gate_value,
        up_value,
    )
    return (result, stored)


def silu_product(gate_in, up_in):
    return gate_in * jax.nn.sigmoid(gate_in) * up_in


def layer_backward(grad_out, stored, params, tables):
    attn_gain, w_query, key_weight, value_weight, w_out, mlp_gain, w_gate, w_up, w_down = params
    row_cos, row_sin, row_pos, key_pos = tables
    (
        stream,
        normed_full,
        query_rows,
        key_own,
        value_own,
        mixed_full,
        middle,
        normed_two_full,
        gate_value,
        up_value,
    ) = stored[:10]
    key_all, value_all = (
        lax.all_gather(key_own, "ctx", axis=1, tiled=True),
        lax.all_gather(value_own, "ctx", axis=1, tiled=True),
    )
    sp_rows, pair_count, model_width = grad_out.shape
    span_rows = normed_full.shape[0]
    row_total = span_rows * pair_count
    grad_full = gather_grads(grad_out.astype(jnp.bfloat16))
    flat_grad = grad_full.reshape(-1, model_width)
    activated = silu_product(gate_value, up_value).astype(jnp.bfloat16)
    grad_w_down = outer_sum(activated, flat_grad)
    grad_act = matmul_back(flat_grad, w_down)
    unused, act_pull = jax.vjp(silu_product, gate_value, up_value)
    grad_gate, grad_up = act_pull(grad_act)
    grad_gate = grad_gate.astype(jnp.bfloat16)
    grad_up = grad_up.astype(jnp.bfloat16)
    flat_two = normed_two_full.reshape(-1, model_width)
    grad_w_gate = outer_sum(flat_two, grad_gate)
    grad_w_up = outer_sum(flat_two, grad_up)
    grad_normed_two = reduce_grads(
        (
            (grad_gate.reshape(span_rows, pair_count, -1), w_gate),
            (grad_up.reshape(span_rows, pair_count, -1), w_up),
        ),
        sp_rows,
    )
    unused_two, norm_pull = jax.vjp(rms_norm, middle, mlp_gain)
    grad_middle_part, grad_mlp_gain = norm_pull(grad_normed_two)
    grad_middle = grad_out + grad_middle_part
    grad_mid_full = gather_grads(grad_middle.astype(jnp.bfloat16))
    flat_mid = grad_mid_full.reshape(-1, model_width)
    flat_mixed = mixed_full.reshape(row_total, -1)
    grad_w_out = outer_sum(flat_mixed, flat_mid)
    grad_mixed = matmul_back(flat_mid, w_out).astype(jnp.bfloat16)
    attn_probs, grouped, key_heads = attention_probs(query_rows, key_all, row_pos, key_pos)
    kv_local = key_heads.shape[1]
    value_heads = value_all.reshape(-1, kv_local, HEAD_DIM)
    grad_heads = grad_mixed.reshape(row_total, kv_local, -1, HEAD_DIM)
    grad_probs = jnp.einsum(
        "rhgd,khd->hgrk", grad_heads, value_heads, preferred_element_type=jnp.float32
    )
    grad_values = jnp.einsum(
        "hgrk,rhgd->khd",
        attn_probs.astype(jnp.bfloat16),
        grad_heads,
        preferred_element_type=jnp.float32,
    )
    centre = jnp.sum(attn_probs * grad_probs, axis=-1, keepdims=True)
    grad_scores = (attn_probs * (grad_probs - centre) * HEAD_DIM ** (-0.5)).astype(jnp.bfloat16)
    grad_queries = jnp.einsum(
        "hgrk,khd->rhgd", grad_scores, key_heads, preferred_element_type=jnp.float32
    )
    grad_keys = jnp.einsum(
        "hgrk,rhgd->khd", grad_scores, grouped, preferred_element_type=jnp.float32
    )
    key_grad_all = grad_keys.reshape(span_rows, -1, kv_local * HEAD_DIM)
    value_grad_all = grad_values.reshape(span_rows, -1, kv_local * HEAD_DIM)
    grad_key_own, grad_value_own = (
        lax.psum_scatter(
            key_grad_all.astype(jnp.bfloat16), "ctx", scatter_dimension=1, tiled=True
        ).astype(jnp.float32),
        lax.psum_scatter(
            value_grad_all.astype(jnp.bfloat16), "ctx", scatter_dimension=1, tiled=True
        ).astype(jnp.float32),
    )
    grad_key_raw = (
        rotate_back(grad_key_own.reshape(row_total, kv_local, HEAD_DIM), row_cos, row_sin)
        .astype(jnp.bfloat16)
        .reshape(row_total, -1)
    )
    grad_value_raw = grad_value_own.reshape(row_total, -1).astype(jnp.bfloat16)
    grad_query_raw = (
        rotate_back(grad_queries.reshape(row_total, -1, HEAD_DIM), row_cos, row_sin)
        .astype(jnp.bfloat16)
        .reshape(row_total, -1)
    )
    flat_in = normed_full.reshape(-1, model_width)
    grad_w_query = outer_sum(flat_in, grad_query_raw)
    grad_w_key = outer_sum(flat_in, grad_key_raw)
    grad_w_value = outer_sum(flat_in, grad_value_raw)
    grad_normed = reduce_grads(
        (
            (grad_query_raw.reshape(span_rows, pair_count, -1), w_query),
            (grad_key_raw.reshape(span_rows, pair_count, -1), key_weight),
            (grad_value_raw.reshape(span_rows, pair_count, -1), value_weight),
        ),
        sp_rows,
    )
    unused_three, norm_pull_one = jax.vjp(rms_norm, stream, attn_gain)
    grad_stream_part, grad_attn_gain = norm_pull_one(grad_normed)
    grad_stream = grad_middle + grad_stream_part
    return (
        grad_stream,
        (
            grad_attn_gain,
            grad_w_query,
            grad_w_key,
            grad_w_value,
            grad_w_out,
            grad_mlp_gain,
            grad_w_gate,
            grad_w_up,
            grad_w_down,
        ),
    )


def to_layout(array_four):
    return jnp.transpose(array_four, (0, 2, 1, 3))[:, None]


def on_device(
    inputs,
    cotangent,
    block_order,
    attn_gain,
    w_query,
    key_weight,
    value_weight,
    w_out,
    mlp_gain,
    w_gate,
    w_up,
    w_down,
):
    section_rank = lax.axis_index("section")
    first_section = section_rank == 0
    ctx_rank = lax.axis_index("ctx")
    n_tensor = lax.axis_size("tensor")
    seq_count, unit_dim, pair_count, sp_rows, half_width = inputs.shape
    span_rows = sp_rows * n_tensor
    own_ids = lax.dynamic_slice_in_dim(block_order, 2 * ctx_rank, 2, 0)
    offsets = jnp.arange(span_rows, dtype=jnp.int32)
    row_pos = (offsets[:, None] + own_ids[None, :] * span_rows).reshape(-1)
    key_pos = (offsets[:, None] + block_order[None, :] * span_rows).reshape(-1)
    row_cos, row_sin = rope_tables(row_pos)
    tables = (row_cos, row_sin, row_pos, key_pos)
    params = tuple(
        (
            stacked[0]
            for stacked in (
                attn_gain,
                w_query,
                key_weight,
                value_weight,
                w_out,
                mlp_gain,
                w_gate,
                w_up,
                w_down,
            )
        )
    )
    full_in, full_grad = (
        lax.all_gather(inputs, "section", axis=4, tiled=True),
        lax.all_gather(cotangent, "section", axis=4, tiled=True),
    )
    feed_in = jnp.transpose(full_in[:, 0].astype(jnp.float32), (0, 2, 1, 3))
    feed_grad = jnp.transpose(full_grad[:, 0].astype(jnp.float32), (0, 2, 1, 3))
    padding = jnp.zeros((1,) + feed_in.shape[1:], jnp.float32)
    feed_in = jnp.concatenate([feed_in, padding], 0)
    feed_grad = jnp.concatenate([feed_grad, padding], 0)
    empty_rows = jnp.zeros(feed_in.shape[1:], jnp.float32)

    def forward_step(received, incoming):
        stream = jnp.where(first_section, incoming, received)
        result, stored = layer_forward(stream, params, tables)
        passed = hand_over(result.astype(jnp.bfloat16))
        return (passed.astype(jnp.float32), (result, stored))

    unused, (results_all, stored_all) = lax.scan(forward_step, empty_rows, feed_in)

    def backward_step(carried, step_idx):
        received, totals = carried
        incoming = lax.dynamic_index_in_dim(feed_grad, step_idx, 0, keepdims=False)
        grad_out = jnp.where(first_section, received, incoming)
        source = jnp.clip(jnp.where(first_section, step_idx - 1, step_idx + 1), 0, seq_count)
        stored_now = jax.tree.map(
            lambda stacked: lax.dynamic_index_in_dim(stacked, source, 0, keepdims=False), stored_all
        )
        grad_stream, step_grads = layer_backward(grad_out, stored_now, params, tables)
        passed = hand_over(grad_stream.astype(jnp.bfloat16)).astype(jnp.float32)
        totals = jax.tree.map(jnp.add, totals, step_grads)
        return ((passed, totals), grad_stream)

    zero_grads = tuple((jnp.zeros(weight.shape, jnp.float32) for weight in params))
    (unused_two, totals), grad_streams = lax.scan(
        backward_step, (empty_rows, zero_grads), jnp.arange(seq_count + 1)
    )
    gain_one, gain_two = lax.psum((totals[0], totals[5]), ("ctx", "tensor"))
    summed = (
        lax.psum(totals[1].astype(jnp.bfloat16), "ctx").astype(jnp.float32),
        lax.psum(totals[2].astype(jnp.bfloat16), "ctx").astype(jnp.float32),
        lax.psum(totals[3].astype(jnp.bfloat16), "ctx").astype(jnp.float32),
        lax.psum(totals[4].astype(jnp.bfloat16), "ctx").astype(jnp.float32),
        lax.psum(totals[6].astype(jnp.bfloat16), "ctx").astype(jnp.float32),
        lax.psum(totals[7].astype(jnp.bfloat16), "ctx").astype(jnp.float32),
        lax.psum(totals[8].astype(jnp.bfloat16), "ctx").astype(jnp.float32),
    )
    outputs_mine = jnp.where(
        first_section, grad_streams[1:], results_all[1:].astype(jnp.bfloat16).astype(jnp.float32)
    )
    own_part = lax.dynamic_slice_in_dim(outputs_mine, section_rank * half_width, half_width, 3)
    other_part = lax.dynamic_slice_in_dim(
        outputs_mine, (1 - section_rank) * half_width, half_width, 3
    )
    arrived = partner(other_part.astype(jnp.bfloat16), "section", 0).astype(other_part.dtype)
    block_out = jnp.where(first_section, arrived, own_part)
    grad_block = jnp.where(first_section, own_part, arrived)
    return (
        to_layout(block_out).astype(jnp.bfloat16),
        to_layout(grad_block),
        gain_one[None],
        summed[0][None],
        summed[1][None],
        summed[2][None],
        summed[3][None],
        gain_two[None],
        summed[4][None],
        summed[5][None],
        summed[6][None],
    )


def solution(mesh):
    in_specs = (
        P(None, "ctx", None, "tensor", "section"),
        P(None, "ctx", None, "tensor", "section"),
        P(),
        P("section", None),
        P("section", None, "tensor"),
        P("section", None, "tensor"),
        P("section", None, "tensor"),
        P("section", "tensor", None),
        P("section", None),
        P("section", None, "tensor"),
        P("section", None, "tensor"),
        P("section", "tensor", None),
    )
    out_specs = (
        P(None, "ctx", None, "tensor", "section"),
        P(None, "ctx", None, "tensor", "section"),
        P("section", None),
        P("section", None, "tensor"),
        P("section", None, "tensor"),
        P("section", None, "tensor"),
        P("section", "tensor", None),
        P("section", None),
        P("section", None, "tensor"),
        P("section", None, "tensor"),
        P("section", "tensor", None),
    )
    return jax.shard_map(
        on_device, mesh=mesh, in_specs=in_specs, out_specs=out_specs, check_vma=False
    )
```

profile of v0, /device:TPU:0, one launch (start us, length us, event | category | flops | bytes accessed | tf_op | source)
XLA Modules:
  0.0 3537.0 jit_solution(16570081444201783496)
XLA Ops:
  27.0 8.5 all-gather.21.cloned.1.call-done
  45.2 1203.9 %while.66 = (s32[]{:T(128)}, f32[128,2,1536]{2,0,1:T(8,128)}, bf16[3,128,2,1536]{3,1,2,0:T(8,128)(2,1)}, f32[3,128,2,1536]{3,1,2,0:T(8,128)}, bf16[3,512,2,1536]...) while((s32[]{:T(128)}, f32[128,2,1536]{2,0,1:T(8,128)}, ...), condition=%wide.region_7.8_spmd.clone, body=%wide.region_0.7_spmd.clone.sunk | while | flops 19858368512 | bytes 469268544 | solution.py:366
  50.8 45.3 %all-gather.23.cloned.1.call-done = bf16[512,2,1536]{2,0,1:T(8,128)(2,1)} async-done(((bf16[128,2,1536]{2,0,1:T(8,128)(2,1)}), bf16[512,2,1536]{2,0,1:T(8,128)(2,1)}) %all-gather.23.cloned.1.call-update) | async-done | bytes 3145744 | tf_op jit(solution)/shard_map/while/body/eval_jaxpr/all_gather | solution.py:69
  137.8 14.7 all-gather.27.cloned.1.call-done
  161.2 28.8 all-gather.25.cloned.1.call-done
  198.7 31.2 fusion.274
  229.8 23.5 fusion.275
  261.6 42.2 %reduce-scatter.7.cloned.1.call-done = bf16[128,2,1536]{2,0,1:T(8,128)(2,1)} async-done(((bf16[512,2,1536]{2,0,1:T(8,128)(2,1)}), bf16[128,2,1536]{2,0,1:T(8,128)(2,1)}) %reduce-scatter.7.cloned.1.call-update) | async-done | bytes 786448 | tf_op jit(solution)/shard_map/while/body/eval_jaxpr/reduce_scatter | solution.py:81
  307.6 44.1 %all-gather.29.cloned.1.call-done = bf16[512,2,1536]{2,0,1:T(8,128)(2,1)} async-done(((bf16[128,2,1536]{2,0,1:T(8,128)(2,1)}), bf16[512,2,1536]{2,0,1:T(8,128)(2,1)}) %all-gather.29.cloned.1.call-update) | async-done | bytes 3145744 | tf_op jit(solution)/shard_map/while/body/eval_jaxpr/all_gather | solution.py:69
  358.5 7.7 reshape.483
  366.2 8.4 bitcast_dynamic-update-slice_fusion.19
  412.1 24.1 reduce-scatter.9.cloned.1.call-done
  452.4 44.2 %all-gather.23.cloned.1.call-done = bf16[512,2,1536]{2,0,1:T(8,128)(2,1)} async-done(((bf16[128,2,1536]{2,0,1:T(8,128)(2,1)}), bf16[512,2,1536]{2,0,1:T(8,128)(2,1)}) %all-gather.23.cloned.1.call-update) | async-done | bytes 3145744 | tf_op jit(solution)/shard_map/while/body/eval_jaxpr/all_gather | solution.py:69
  538.0 15.0 all-gather.27.cloned.1.call-done
  561.8 28.9 all-gather.25.cloned.1.call-done
  599.4 31.2 fusion.274
  630.5 23.5 fusion.275
  662.4 42.2 %reduce-scatter.7.cloned.1.call-done = bf16[128,2,1536]{2,0,1:T(8,128)(2,1)} async-done(((bf16[512,2,1536]{2,0,1:T(8,128)(2,1)}), bf16[128,2,1536]{2,0,1:T(8,128)(2,1)}) %reduce-scatter.7.cloned.1.call-update) | async-done | bytes 786448 | tf_op jit(solution)/shard_map/while/body/eval_jaxpr/reduce_scatter | solution.py:81
  708.4 44.1 %all-gather.29.cloned.1.call-done = bf16[512,2,1536]{2,0,1:T(8,128)(2,1)} async-done(((bf16[128,2,1536]{2,0,1:T(8,128)(2,1)}), bf16[512,2,1536]{2,0,1:T(8,128)(2,1)}) %all-gather.29.cloned.1.call-update) | async-done | bytes 3145744 | tf_op jit(solution)/shard_map/while/body/eval_jaxpr/all_gather | solution.py:69
  759.3 7.8 reshape.483
  767.1 8.5 bitcast_dynamic-update-slice_fusion.19
  785.3 7.6 convolution_convert_fusion.10
  813.1 24.0 reduce-scatter.9.cloned.1.call-done
  853.2 44.2 %all-gather.23.cloned.1.call-done = bf16[512,2,1536]{2,0,1:T(8,128)(2,1)} async-done(((bf16[128,2,1536]{2,0,1:T(8,128)(2,1)}), bf16[512,2,1536]{2,0,1:T(8,128)(2,1)}) %all-gather.23.cloned.1.call-update) | async-done | bytes 3145744 | tf_op jit(solution)/shard_map/while/body/eval_jaxpr/all_gather | solution.py:69
  938.8 15.0 all-gather.27.cloned.1.call-done
  962.5 28.8 all-gather.25.cloned.1.call-done
  999.9 31.2 fusion.274
  1031.1 23.5 fusion.275
  1063.1 42.2 %reduce-scatter.7.cloned.1.call-done = bf16[128,2,1536]{2,0,1:T(8,128)(2,1)} async-done(((bf16[512,2,1536]{2,0,1:T(8,128)(2,1)}), bf16[128,2,1536]{2,0,1:T(8,128)(2,1)}) %reduce-scatter.7.cloned.1.call-update) | async-done | bytes 786448 | tf_op jit(solution)/shard_map/while/body/eval_jaxpr/reduce_scatter | solution.py:81
  1109.1 44.1 %all-gather.29.cloned.1.call-done = bf16[512,2,1536]{2,0,1:T(8,128)(2,1)} async-done(((bf16[128,2,1536]{2,0,1:T(8,128)(2,1)}), bf16[512,2,1536]{2,0,1:T(8,128)(2,1)}) %all-gather.29.cloned.1.call-update) | async-done | bytes 3145744 | tf_op jit(solution)/shard_map/while/body/eval_jaxpr/all_gather | solution.py:69
  1160.0 7.7 reshape.483
  1167.7 8.5 bitcast_dynamic-update-slice_fusion.19
  1186.0 7.6 convolution_convert_fusion.10
  1213.6 24.2 reduce-scatter.9.cloned.1.call-done
  1252.0 1799.1 %while.67 = (s32[]{:T(128)}, f32[128,2,1536]{2,0,1:T(8,128)S(1)}, f32[1536]{0:T(1024)}, f32[1536,384]{1,0:T(8,128)}, f32[1536,192]{0,1:T(8,128)}, /*index=5*/f32...) while((s32[]{:T(128)}, f32[128,2,1536]{2,0,1:T(8,128)S(1)}, ...), condition=%wide.region_22.23_spmd.clone, body=%wide.region_8.22_spmd.clone.sunk | while | flops 43088084992 | bytes 1169429888 | solution.py:382
  1259.6 42.9 %all-gather.31.cloned.1.call-done = bf16[512,2,1536]{2,0,1:T(8,128)(2,1)} async-done(((bf16[128,2,1536]{2,0,1:T(8,128)(2,1)}), bf16[512,2,1536]{2,0,1:T(8,128)(2,1)}) %all-gather.31.cloned.1.call-update) | async-done | bytes 3145744 | tf_op jit(solution)/shard_map/while/body/eval_jaxpr/all_gather | solution.py:73
  1310.5 11.2 fusion.314
  1346.1 37.9 %reduce-scatter.11.cloned.1.call-done = bf16[128,2,1536]{2,0,1:T(8,128)(2,1)} async-done(((bf16[512,2,1536]{2,0,1:T(8,128)(2,1)}), bf16[128,2,1536]{2,0,1:T(8,128)(2,1)}) %reduce-scatter.11.cloned.1.call-update) | async-done | bytes 786448 | tf_op jit(solution)/shard_map/while/body/eval_jaxpr/reduce_scatter | solution.py:100
  1422.6 33.3 fusion.321
  1478.6 24.3 fusion.320
  1502.9 82.9 %fusion.326 = bf16[4096,2,96]{0,2,1:T(8,128)(2,1)} fusion(bf16[1024,2,2,96]{0,3,2,1:T(8,128)(2,1)S(1)} %bitcast.467, f32[2,4096,1024,2]{2,1,3,0:T(8,128)} %fusion.320, f32[2,2,1024,4096]{2,3,1,0:T(8,128)} %get-tuple-element.1778, f32[2,2,1024]{2,1,0:T(2,128)S(1)} %get-tuple-element.1779), kind=kOutput, calls=%fused_computation.93.clone.1 | convolution fusion | flops 3339460608 | bytes 136593408 | tf_op jit(solution)/shard_map/while/body/eval_jaxpr/hgrk,rhgd->khd/dot_general | solution.py:248
  1598.2 24.9 fusion.329
  1635.6 81.2 %fusion.322 = f32[2,96,2,1024]{3,1,2,0:T(8,128)S(1)} fusion(bf16[4096,2,96,1]{0,2,3,1:T(8,128)(2,1)S(1)} %copy-done.40, f32[2,4096,1024,2]{2,1,3,0:T(8,128)} %fusion.320, f32[2,2,1024,4096]{2,3,1,0:T(8,128)} %get-tuple-element.1778, f32[2,2,1024]{2,1,0:T(2,128)S(1)} %get-tuple-element.1779), kind=kOutput, calls=%fused_computation.80.clone.1 | convolution fusion | flops 3338674176 | bytes 137379840 | tf_op jit(solution)/shard_map/while/body/eval_jaxpr/hgrk,khd->rhgd/dot_general | solution.py:245
  1799.5 8.9 select_add_fusion.13
  1852.0 43.0 %all-gather.31.cloned.1.call-done = bf16[512,2,1536]{2,0,1:T(8,128)(2,1)} async-done(((bf16[128,2,1536]{2,0,1:T(8,128)(2,1)}), bf16[512,2,1536]{2,0,1:T(8,128)(2,1)}) %all-gather.31.cloned.1.call-update) | async-done | bytes 3145744 | tf_op jit(solution)/shard_map/while/body/eval_jaxpr/all_gather | solution.py:73
  1903.0 11.2 fusion.314
  1938.5 37.9 %reduce-scatter.11.cloned.1.call-done = bf16[128,2,1536]{2,0,1:T(8,128)(2,1)} async-done(((bf16[512,2,1536]{2,0,1:T(8,128)(2,1)}), bf16[128,2,1536]{2,0,1:T(8,128)(2,1)}) %reduce-scatter.11.cloned.1.call-update) | async-done | bytes 786448 | tf_op jit(solution)/shard_map/while/body/eval_jaxpr/reduce_scatter | solution.py:100
  2015.5 33.3 fusion.321
  2071.3 24.3 fusion.320
  2095.6 82.9 %fusion.326 = bf16[4096,2,96]{0,2,1:T(8,128)(2,1)} fusion(bf16[1024,2,2,96]{0,3,2,1:T(8,128)(2,1)S(1)} %bitcast.467, f32[2,4096,1024,2]{2,1,3,0:T(8,128)} %fusion.320, f32[2,2,1024,4096]{2,3,1,0:T(8,128)} %get-tuple-element.1778, f32[2,2,1024]{2,1,0:T(2,128)S(1)} %get-tuple-element.1779), kind=kOutput, calls=%fused_computation.93.clone.1 | convolution fusion | flops 3339460608 | bytes 136593408 | tf_op jit(solution)/shard_map/while/body/eval_jaxpr/hgrk,rhgd->khd/dot_general | solution.py:248
  2191.0 24.9 fusion.329
  2228.3 81.2 %fusion.322 = f32[2,96,2,1024]{3,1,2,0:T(8,128)S(1)} fusion(bf16[4096,2,96,1]{0,2,3,1:T(8,128)(2,1)S(1)} %copy-done.40, f32[2,4096,1024,2]{2,1,3,0:T(8,128)} %fusion.320, f32[2,2,1024,4096]{2,3,1,0:T(8,128)} %get-tuple-element.1778, f32[2,2,1024]{2,1,0:T(2,128)S(1)} %get-tuple-element.1779), kind=kOutput, calls=%fused_computation.80.clone.1 | convolution fusion | flops 3338674176 | bytes 137379840 | tf_op jit(solution)/shard_map/while/body/eval_jaxpr/hgrk,khd->rhgd/dot_general | solution.py:245
  2392.2 10.8 select_add_fusion.13
  2452.8 43.0 %all-gather.31.cloned.1.call-done = bf16[512,2,1536]{2,0,1:T(8,128)(2,1)} async-done(((bf16[128,2,1536]{2,0,1:T(8,128)(2,1)}), bf16[512,2,1536]{2,0,1:T(8,128)(2,1)}) %all-gather.31.cloned.1.call-update) | async-done | bytes 3145744 | tf_op jit(solution)/shard_map/while/body/eval_jaxpr/all_gather | solution.py:73
  2503.8 11.3 fusion.314
  2539.5 37.9 %reduce-scatter.11.cloned.1.call-done = bf16[128,2,1536]{2,0,1:T(8,128)(2,1)} async-done(((bf16[512,2,1536]{2,0,1:T(8,128)(2,1)}), bf16[128,2,1536]{2,0,1:T(8,128)(2,1)}) %reduce-scatter.11.cloned.1.call-update) | async-done | bytes 786448 | tf_op jit(solution)/shard_map/while/body/eval_jaxpr/reduce_scatter | solution.py:100
  2616.4 33.4 fusion.321
  2672.0 24.3 fusion.320
  2696.3 82.9 %fusion.326 = bf16[4096,2,96]{0,2,1:T(8,128)(2,1)} fusion(bf16[1024,2,2,96]{0,3,2,1:T(8,128)(2,1)S(1)} %bitcast.467, f32[2,4096,1024,2]{2,1,3,0:T(8,128)} %fusion.320, f32[2,2,1024,4096]{2,3,1,0:T(8,128)} %get-tuple-element.1778, f32[2,2,1024]{2,1,0:T(2,128)S(1)} %get-tuple-element.1779), kind=kOutput, calls=%fused_computation.93.clone.1 | convolution fusion | flops 3339460608 | bytes 136593408 | tf_op jit(solution)/shard_map/while/body/eval_jaxpr/hgrk,rhgd->khd/dot_general | solution.py:248
  2791.7 24.9 fusion.329
  2829.1 81.2 %fusion.322 = f32[2,96,2,1024]{3,1,2,0:T(8,128)S(1)} fusion(bf16[4096,2,96,1]{0,2,3,1:T(8,128)(2,1)S(1)} %copy-done.40, f32[2,4096,1024,2]{2,1,3,0:T(8,128)} %fusion.320, f32[2,2,1024,4096]{2,3,1,0:T(8,128)} %get-tuple-element.1778, f32[2,2,1024]{2,1,0:T(2,128)S(1)} %get-tuple-element.1779), kind=kOutput, calls=%fused_computation.80.clone.1 | convolution fusion | flops 3338674176 | bytes 137379840 | tf_op jit(solution)/shard_map/while/body/eval_jaxpr/hgrk,khd->rhgd/dot_general | solution.py:245
  2993.0 10.8 select_add_fusion.13
  3071.8 79.6 %all-reduce.2 = (f32[1,1536]{1,0:T(1,128)}, f32[1,1536]{1,0:T(1,128)}) all-reduce(f32[1,1536]{1,0:T(1,128)S(1)} %broadcast_in_dim.187, f32[1,1536]{1,0:T(1,128)S(1)} %broadcast_in_dim.196), channel_id=1, replica_groups=mesh['section'=2,'ctx'=4,'tensor'=4] {'ctx','tensor'}, use_global_device_ids=true, to_apply=%region_23.24 | all-reduce | flops 3072 | bytes 24576 | tf_op jit(solution)/shard_map/psum | solution.py:385
  3156.1 355.7 %all-reduce.6.cloned.1.call-done = (bf16[1,1536,384]{2,1,0:T(8,128)(2,1)}, bf16[1,1536,192]{1,2,0:T(8,128)(2,1)}, bf16[1,1536,192]{1,2,0:T(8,128)(2,1)}, bf16[1,...) async-done(((bf16[1,1536,384]{2,1,0:T(8,128)(2,1)}, bf16[1,1536,192]{1,2,0:T(8,128)(2,1)}, ...) | async-done | bytes 12976144 | tf_op jit(solution)/shard_map/psum | solution.py:387
  (1029 shorter events, 1184.2 us)
Async XLA Ops:
  8.0 14.9 all-gather.19.cloned.1.call-start
  8.7 26.7 all-gather.21.cloned.1.call-start
  45.5 90.9 %copy-start.33 = (f32[1024,96]{0,1:T(8,128)}, f32[1024,96]{0,1:T(8,128)S(1)}, u32[]{:S(2)}) copy-start(f32[1024,96]{0,1:T(8,128)S(1)} %get-tuple-element.1874) | copy-start | bytes 1179652 | tf_op jit(solution)/shard_map/while
  45.5 90.9 %copy-start.35 = (f32[1024,96]{0,1:T(8,128)}, f32[1024,96]{0,1:T(8,128)S(1)}, u32[]{:S(2)}) copy-start(f32[1024,96]{0,1:T(8,128)S(1)} %get-tuple-element.1873) | copy-start | bytes 1179652 | tf_op jit(solution)/shard_map/while
  45.5 50.5 %all-gather.23.cloned.1.call-start = ((), (), s32[]{:S(2)}) async-start(), calls=%async_computation.9 | async-start | bytes 3932160 | tf_op jit(solution)/shard_map/while/body/eval_jaxpr/all_gather | solution.py:69
  50.8 101.7 %all-gather.27.cloned.1.call-start = ((), (), s32[]{:S(2)}) async-start(), calls=%async_computation.11 | async-start | bytes 1966080 | tf_op jit(solution)/shard_map/while/body/eval_jaxpr/all_gather | solution.py:143
  115.2 74.7 %all-gather.25.cloned.1.call-start = ((), (), s32[]{:S(2)}) async-start(), calls=%async_computation.10 | async-start | bytes 1966080 | tf_op jit(solution)/shard_map/while/body/eval_jaxpr/all_gather | solution.py:142
  128.6 175.2 %reduce-scatter.7.cloned.1.call-start = ((), (), s32[]{:S(2)}) async-start(), calls=%async_computation.12 | async-start | bytes 3932160 | tf_op jit(solution)/shard_map/while/body/eval_jaxpr/reduce_scatter | solution.py:81
  260.9 90.8 %all-gather.29.cloned.1.call-start = ((), (), s32[]{:S(2)}) async-start(), calls=%async_computation.13 | async-start | bytes 3932160 | tf_op jit(solution)/shard_map/while/body/eval_jaxpr/all_gather | solution.py:69
  307.6 128.7 %reduce-scatter.9.cloned.1.call-start = ((), (), s32[]{:S(2)}) async-start(), calls=%async_computation.14 | async-start | bytes 3932160 | tf_op jit(solution)/shard_map/while/body/eval_jaxpr/reduce_scatter | solution.py:81
  437.7 6.6 collective-permute-start
  446.7 89.9 %copy-start.33 = (f32[1024,96]{0,1:T(8,128)}, f32[1024,96]{0,1:T(8,128)S(1)}, u32[]{:S(2)}) copy-start(f32[1024,96]{0,1:T(8,128)S(1)} %get-tuple-element.1874) | copy-start | bytes 1179652 | tf_op jit(solution)/shard_map/while
  446.7 89.9 %copy-start.35 = (f32[1024,96]{0,1:T(8,128)}, f32[1024,96]{0,1:T(8,128)S(1)}, u32[]{:S(2)}) copy-start(f32[1024,96]{0,1:T(8,128)S(1)} %get-tuple-element.1873) | copy-start | bytes 1179652 | tf_op jit(solution)/shard_map/while
  446.7 49.9 %all-gather.23.cloned.1.call-start = ((), (), s32[]{:S(2)}) async-start(), calls=%async_computation.9 | async-start | bytes 3932160 | tf_op jit(solution)/shard_map/while/body/eval_jaxpr/all_gather | solution.py:69
  452.4 100.6 %all-gather.27.cloned.1.call-start = ((), (), s32[]{:S(2)}) async-start(), calls=%async_computation.11 | async-start | bytes 1966080 | tf_op jit(solution)/shard_map/while/body/eval_jaxpr/all_gather | solution.py:143
  515.8 74.9 %all-gather.25.cloned.1.call-start = ((), (), s32[]{:S(2)}) async-start(), calls=%async_computation.10 | async-start | bytes 1966080 | tf_op jit(solution)/shard_map/while/body/eval_jaxpr/all_gather | solution.py:142
  529.1 175.5 %reduce-scatter.7.cloned.1.call-start = ((), (), s32[]{:S(2)}) async-start(), calls=%async_computation.12 | async-start | bytes 3932160 | tf_op jit(solution)/shard_map/while/body/eval_jaxpr/reduce_scatter | solution.py:81
  661.6 90.9 %all-gather.29.cloned.1.call-start = ((), (), s32[]{:S(2)}) async-start(), calls=%async_computation.13 | async-start | bytes 3932160 | tf_op jit(solution)/shard_map/while/body/eval_jaxpr/all_gather | solution.py:69
  708.4 128.7 %reduce-scatter.9.cloned.1.call-start = ((), (), s32[]{:S(2)}) async-start(), calls=%async_computation.14 | async-start | bytes 3932160 | tf_op jit(solution)/shard_map/while/body/eval_jaxpr/reduce_scatter | solution.py:81
  838.5 6.6 collective-permute-start
  847.3 90.1 %copy-start.33 = (f32[1024,96]{0,1:T(8,128)}, f32[1024,96]{0,1:T(8,128)S(1)}, u32[]{:S(2)}) copy-start(f32[1024,96]{0,1:T(8,128)S(1)} %get-tuple-element.1874) | copy-start | bytes 1179652 | tf_op jit(solution)/shard_map/while
  847.3 90.1 %copy-start.35 = (f32[1024,96]{0,1:T(8,128)}, f32[1024,96]{0,1:T(8,128)S(1)}, u32[]{:S(2)}) copy-start(f32[1024,96]{0,1:T(8,128)S(1)} %get-tuple-element.1873) | copy-start | bytes 1179652 | tf_op jit(solution)/shard_map/while
  847.3 50.0 %all-gather.23.cloned.1.call-start = ((), (), s32[]{:S(2)}) async-start(), calls=%async_computation.9 | async-start | bytes 3932160 | tf_op jit(solution)/shard_map/while/body/eval_jaxpr/all_gather | solution.py:69
  853.1 100.6 %all-gather.27.cloned.1.call-start = ((), (), s32[]{:S(2)}) async-start(), calls=%async_computation.11 | async-start | bytes 1966080 | tf_op jit(solution)/shard_map/while/body/eval_jaxpr/all_gather | solution.py:143
  916.5 74.7 %all-gather.25.cloned.1.call-start = ((), (), s32[]{:S(2)}) async-start(), calls=%async_computation.10 | async-start | bytes 1966080 | tf_op jit(solution)/shard_map/while/body/eval_jaxpr/all_gather | solution.py:142
  929.9 175.4 %reduce-scatter.7.cloned.1.call-start = ((), (), s32[]{:S(2)}) async-start(), calls=%async_computation.12 | async-start | bytes 3932160 | tf_op jit(solution)/shard_map/while/body/eval_jaxpr/reduce_scatter | solution.py:81
  1062.3 90.8 %all-gather.29.cloned.1.call-start = ((), (), s32[]{:S(2)}) async-start(), calls=%async_computation.13 | async-start | bytes 3932160 | tf_op jit(solution)/shard_map/while/body/eval_jaxpr/all_gather | solution.py:69
  1109.1 128.7 %reduce-scatter.9.cloned.1.call-start = ((), (), s32[]{:S(2)}) async-start(), calls=%async_computation.14 | async-start | bytes 3932160 | tf_op jit(solution)/shard_map/while/body/eval_jaxpr/reduce_scatter | solution.py:81
  1239.2 6.7 collective-permute-start
  1252.9 93.2 %copy-start.74 = (s32[8]{0:T(128)}, s32[8]{0:T(128)S(1)}, u32[]{:S(2)}) copy-start(s32[8]{0:T(128)S(1)} %get-tuple-element.2011) | copy-start | bytes 100 | tf_op jit(solution)/shard_map/while
  1252.9 138.6 %copy-start.70 = (s32[2]{0:T(128)}, s32[2]{0:T(128)S(1)}, u32[]{:S(2)}) copy-start(s32[2]{0:T(128)S(1)} %get-tuple-element.2010) | copy-start | bytes 28 | tf_op jit(solution)/shard_map/while
  1252.9 49.6 %all-gather.31.cloned.1.call-start = ((), (), s32[]{:S(2)}) async-start(), calls=%async_computation.15 | async-start | bytes 3932160 | tf_op jit(solution)/shard_map/while/body/eval_jaxpr/all_gather | solution.py:73
  1258.3 125.8 %reduce-scatter.11.cloned.1.call-start = ((), (), s32[]{:S(2)}) async-start(), calls=%async_computation.16 | async-start | bytes 3932160 | tf_op jit(solution)/shard_map/while/body/eval_jaxpr/reduce_scatter | solution.py:100
  1339.9 65.5 %all-gather.33.cloned.1.call-start = ((), (), s32[]{:S(2)}) async-start(), calls=%async_computation.17 | async-start | bytes 1966080 | tf_op jit(solution)/shard_map/while/body/eval_jaxpr/all_gather | solution.py:197
  1341.8 75.0 %all-gather.37.cloned.1.call-start = ((), (), s32[]{:S(2)}) async-start(), calls=%async_computation.19 | async-start | bytes 1966080 | tf_op jit(solution)/shard_map/while/body/eval_jaxpr/all_gather | solution.py:198
  1343.7 117.8 %all-gather.35.cloned.1.call-start = ((), (), s32[]{:S(2)}) async-start(), calls=%async_computation.18 | async-start | bytes 3932160 | tf_op jit(solution)/shard_map/while/body/eval_jaxpr/all_gather | solution.py:73
  1391.1 349.8 %reduce-scatter.13.cloned.1.call-start = ((), (), s32[]{:S(2)}) async-start(), calls=%async_computation.20 | async-start | bytes 1966080 | tf_op jit(solution)/shard_map/while/body/eval_jaxpr/reduce_scatter | solution.py:254
  1598.2 157.6 %reduce-scatter.15.cloned.1.call-start = ((), (), s32[]{:S(2)}) async-start(), calls=%async_computation.21 | async-start | bytes 1966080 | tf_op jit(solution)/shard_map/while/body/eval_jaxpr/reduce_scatter | solution.py:257
  1716.8 120.2 %reduce-scatter.17.cloned.1.call-start = ((), (), s32[]{:S(2)}) async-start(), calls=%async_computation.22 | async-start | bytes 3932160 | tf_op jit(solution)/shard_map/while/body/eval_jaxpr/reduce_scatter | solution.py:100
  1841.4 3.2 collective-permute-start.1
  1845.3 93.2 %copy-start.74 = (s32[8]{0:T(128)}, s32[8]{0:T(128)S(1)}, u32[]{:S(2)}) copy-start(s32[8]{0:T(128)S(1)} %get-tuple-element.2011) | copy-start | bytes 100 | tf_op jit(solution)/shard_map/while
  1845.3 139.1 %copy-start.70 = (s32[2]{0:T(128)}, s32[2]{0:T(128)S(1)}, u32[]{:S(2)}) copy-start(s32[2]{0:T(128)S(1)} %get-tuple-element.2010) | copy-start | bytes 28 | tf_op jit(solution)/shard_map/while
  1845.3 49.6 %all-gather.31.cloned.1.call-start = ((), (), s32[]{:S(2)}) async-start(), calls=%async_computation.15 | async-start | bytes 3932160 | tf_op jit(solution)/shard_map/while/body/eval_jaxpr/all_gather | solution.py:73
  1850.6 125.8 %reduce-scatter.11.cloned.1.call-start = ((), (), s32[]{:S(2)}) async-start(), calls=%async_computation.16 | async-start | bytes 3932160 | tf_op jit(solution)/shard_map/while/body/eval_jaxpr/reduce_scatter | solution.py:100
  1932.4 65.9 %all-gather.33.cloned.1.call-start = ((), (), s32[]{:S(2)}) async-start(), calls=%async_computation.17 | async-start | bytes 1966080 | tf_op jit(solution)/shard_map/while/body/eval_jaxpr/all_gather | solution.py:197
  1934.2 75.4 %all-gather.37.cloned.1.call-start = ((), (), s32[]{:S(2)}) async-start(), calls=%async_computation.19 | async-start | bytes 1966080 | tf_op jit(solution)/shard_map/while/body/eval_jaxpr/all_gather | solution.py:198
  1936.1 118.1 %all-gather.35.cloned.1.call-start = ((), (), s32[]{:S(2)}) async-start(), calls=%async_computation.18 | async-start | bytes 3932160 | tf_op jit(solution)/shard_map/while/body/eval_jaxpr/all_gather | solution.py:73
  1984.0 349.7 %reduce-scatter.13.cloned.1.call-start = ((), (), s32[]{:S(2)}) async-start(), calls=%async_computation.20 | async-start | bytes 1966080 | tf_op jit(solution)/shard_map/while/body/eval_jaxpr/reduce_scatter | solution.py:254
  2190.9 157.6 %reduce-scatter.15.cloned.1.call-start = ((), (), s32[]{:S(2)}) async-start(), calls=%async_computation.21 | async-start | bytes 1966080 | tf_op jit(solution)/shard_map/while/body/eval_jaxpr/reduce_scatter | solution.py:257
  2309.6 128.4 %reduce-scatter.17.cloned.1.call-start = ((), (), s32[]{:S(2)}) async-start(), calls=%async_computation.22 | async-start | bytes 3932160 | tf_op jit(solution)/shard_map/while/body/eval_jaxpr/reduce_scatter | solution.py:100
  2442.3 3.1 collective-permute-start.1
  2446.1 93.3 %copy-start.74 = (s32[8]{0:T(128)}, s32[8]{0:T(128)S(1)}, u32[]{:S(2)}) copy-start(s32[8]{0:T(128)S(1)} %get-tuple-element.2011) | copy-start | bytes 100 | tf_op jit(solution)/shard_map/while
  2446.1 139.2 %copy-start.70 = (s32[2]{0:T(128)}, s32[2]{0:T(128)S(1)}, u32[]{:S(2)}) copy-start(s32[2]{0:T(128)S(1)} %get-tuple-element.2010) | copy-start | bytes 28 | tf_op jit(solution)/shard_map/while
  2446.2 49.7 %all-gather.31.cloned.1.call-start = ((), (), s32[]{:S(2)}) async-start(), calls=%async_computation.15 | async-start | bytes 3932160 | tf_op jit(solution)/shard_map/while/body/eval_jaxpr/all_gather | solution.py:73
  2451.5 125.9 %reduce-scatter.11.cloned.1.call-start = ((), (), s32[]{:S(2)}) async-start(), calls=%async_computation.16 | async-start | bytes 3932160 | tf_op jit(solution)/shard_map/while/body/eval_jaxpr/reduce_scatter | solution.py:100
  2533.3 65.9 %all-gather.33.cloned.1.call-start = ((), (), s32[]{:S(2)}) async-start(), calls=%async_computation.17 | async-start | bytes 1966080 | tf_op jit(solution)/shard_map/while/body/eval_jaxpr/all_gather | solution.py:197
  2535.2 75.4 %all-gather.37.cloned.1.call-start = ((), (), s32[]{:S(2)}) async-start(), calls=%async_computation.19 | async-start | bytes 1966080 | tf_op jit(solution)/shard_map/while/body/eval_jaxpr/all_gather | solution.py:198
  2537.1 117.9 %all-gather.35.cloned.1.call-start = ((), (), s32[]{:S(2)}) async-start(), calls=%async_computation.18 | async-start | bytes 3932160 | tf_op jit(solution)/shard_map/while/body/eval_jaxpr/all_gather | solution.py:73
  2584.9 349.5 %reduce-scatter.13.cloned.1.call-start = ((), (), s32[]{:S(2)}) async-start(), calls=%async_computation.20 | async-start | bytes 1966080 | tf_op jit(solution)/shard_map/while/body/eval_jaxpr/reduce_scatter | solution.py:254
  2791.7 157.6 %reduce-scatter.15.cloned.1.call-start = ((), (), s32[]{:S(2)}) async-start(), calls=%async_computation.21 | async-start | bytes 1966080 | tf_op jit(solution)/shard_map/while/body/eval_jaxpr/reduce_scatter | solution.py:257
  2910.3 128.4 %reduce-scatter.17.cloned.1.call-start = ((), (), s32[]{:S(2)}) async-start(), calls=%async_computation.22 | async-start | bytes 3932160 | tf_op jit(solution)/shard_map/while/body/eval_jaxpr/reduce_scatter | solution.py:100
  3043.0 3.2 collective-permute-start.1
  3051.1 460.7 %all-reduce.6.cloned.1.call-start = ((), (), s32[]{:S(2)}) async-start(), calls=%async_computation.8 | async-start | bytes 25952256 | tf_op jit(solution)/shard_map/psum | solution.py:387
  3071.2 80.1 %collective-permute-start.2 = (bf16[2,128,2,768]{3,1,2,0:T(8,128)(2,1)}, bf16[2,128,2,768]{3,1,2,0:T(8,128)(2,1)}, u32[]{:S(2)}, u32[]{:S(2)}) collective-permute-start(bf16[2,128,2,768]{3,1,2,0:T(8,128)(2,1)} %dynamic-slice_convert_fusion), channel_id=1, source_target_pairs={{0,16},{16,0},{1,17},{17,1},{2,18},{18,2},{3,19},{19,3},{4,20},{20... | collective-permute-start | bytes 2359304 | tf_op jit(solution)/shard_map/ppermute | solution.py:16
  (203 other events, 1751.6 us)
Sparse Core Ops, SparseCore 0:
  10.4 12.4 all-gather.18
  24.5 10.9 all-gather.20
  50.9 45.1 all-gather.22
  115.4 37.0 all-gather.26
  154.0 35.9 all-gather.24
  261.0 42.7 reduce-scatter.6
  307.7 43.9 all-gather.28
  392.2 43.9 reduce-scatter.8
  452.5 44.0 all-gather.22
  515.9 37.0 all-gather.26
  554.7 35.9 all-gather.24
  661.7 42.8 reduce-scatter.6
  708.5 43.9 all-gather.28
  793.1 43.9 reduce-scatter.8
  853.2 44.0 all-gather.22
  916.6 37.0 all-gather.26
  955.2 35.9 all-gather.24
  1062.5 42.7 reduce-scatter.6
  1109.2 43.9 all-gather.28
  1193.8 43.9 reduce-scatter.8
  1258.4 44.1 all-gather.30
  1340.1 43.9 reduce-scatter.10
  1763.3 43.9 reduce-scatter.16
  1850.7 44.1 all-gather.30
  1932.5 43.9 reduce-scatter.10
  2356.0 43.9 reduce-scatter.16
  2451.6 44.1 all-gather.30
  2533.4 43.9 reduce-scatter.10
  2956.8 43.9 reduce-scatter.16
  3067.5 444.2 all-reduce.5
Sparse Core Ops, SparseCore 1:
  1342.1 36.9 all-gather.32
  1380.5 35.8 all-gather.36
  1418.8 42.6 all-gather.34
  1598.3 35.3 reduce-scatter.12
  1716.9 35.3 reduce-scatter.14
  1934.8 36.9 all-gather.32
  1973.3 35.8 all-gather.36
  2011.5 42.6 all-gather.34
  2191.0 35.3 reduce-scatter.12
  2309.6 35.3 reduce-scatter.14
  2535.4 36.9 all-gather.32
  2574.0 35.8 all-gather.36
  2612.3 42.6 all-gather.34
  2791.7 35.3 reduce-scatter.12
  2910.4 35.3 reduce-scatter.14
where the time goes:
time: 3550 us; the launch traced here: 3540 us
  matrix products  1240 us (35%)
  waiting for transfers between devices  1220 us (34%)
  local copies, waits for them, and re-layouts  719 us (20%)
  other arithmetic  227 us (6%)
  blocking collectives  79.6 us (2%)
    psum x1, waiting for transfers between devices, on_device(): lax.psum(totals[1].astype(jnp.bfloat16), 'ctx').astype(jnp.float32)  356 us
    all_gather x6, waiting for transfers between devices, gather_rows(): return lax.all_gather(normalized_input, 'tensor', axis=0, tiled=True)  266 us
    dot_general x3, matrix products, layer_backward(): jnp.einsum('hgrk,rhgd->khd', grad_scores, grouped, preferred_element_type...  249 us
    dot_general x3, matrix products, layer_backward(): jnp.einsum('hgrk,khd->rhgd', grad_scores, key_heads, preferred_element_ty...  244 us
    reduce_scatter x6, waiting for transfers between devices, reduce_rows(): lax.psum_scatter(term_rows(jnp.int32(0), sp_rows * lax.axis_size('tensor'...  199 us
    sub x6, matrix products, attention_probs(): powers = jnp.exp(masked - largest)  193 us
    all_gather x6, waiting for transfers between devices, gather_grads(): return lax.all_gather(grad_rows, 'tensor', axis=0, tiled=True)  145 us
    reduce_scatter x6, waiting for transfers between devices, reduce_grads(): lax.psum_scatter(term_rows(jnp.int32(0), sp_rows * lax.axis_size('tensor'...  114 us
  transfers between devices with their start and end apart: 52, of which 30 were waited for; matrix products, arithmetic and copies ran while one was open for 32% of the time, Pallas kernels for 0%

commit v1 on v0

v1 whole, which is shorter than its diff:
```python
import jax
import jax.numpy as jnp
import numpy as np
from jax import lax
from jax.experimental import pallas as pl
from jax.experimental.pallas import tpu as pltpu
from jax.sharding import PartitionSpec as P

HEAD_DIM = 96
EPSILON = 1e-05
ROPE_BASE = 100000.0
LOG2E = 1.4426950408889634
BF = jnp.bfloat16
F32 = jnp.float32


def nn(a, b):
    return lax.dot_general(a, b, (((1,), (0,)), ((), ())), preferred_element_type=F32)


def nt(a, b):
    return lax.dot_general(a, b, (((1,), (1,)), ((), ())), preferred_element_type=F32)


def tn(a, b):
    return lax.dot_general(a, b, (((0,), (0,)), ((), ())), preferred_element_type=F32)


def head_of(x, h):
    return x[:, h * HEAD_DIM : (h + 1) * HEAD_DIM]


def transposed(x):
    return x.astype(F32).T.astype(BF)


def causal(length):
    keys = lax.broadcasted_iota(jnp.int32, (length, length), 0)
    queries = lax.broadcasted_iota(jnp.int32, (length, length), 1)
    return keys <= queries


def fwd_kernel(order_ref, own_ref, q_ref, kv_ref, mix_ref, mixt_ref, lse_ref, qt, m_s, l_s, acc):
    n_ctx, n_t, _, sp, width = kv_ref.shape
    length = n_t * sp
    kv_heads = width // (2 * HEAD_DIM)
    q_heads = q_ref.shape[-1] // HEAD_DIM
    group = q_heads // kv_heads
    scale = HEAD_DIM**-0.5 * LOG2E
    for j in range(2):
        x = q_ref[:, j].reshape(length, -1)
        for h in range(q_heads):
            qt[j, h] = transposed(head_of(x, h))
    m_s[...] = jnp.full_like(m_s, -1e30)
    l_s[...] = jnp.zeros_like(l_s)
    acc[...] = jnp.zeros_like(acc)

    def body(k, _):
        c_at = k // 2
        j_at = lax.rem(k, 2)
        key_block = order_ref[k]
        x = kv_ref[c_at, :, pl.ds(j_at, 1)].reshape(length, width)
        keys = [head_of(x, h) for h in range(kv_heads)]
        values = [transposed(head_of(x, kv_heads + h)) for h in range(kv_heads)]

        def step(j, masked):
            for h in range(q_heads):
                s = nn(keys[h // group], qt[j, h]) * scale
                if masked:
                    s = jnp.where(causal(length), s, -1e30)
                m_old = m_s[j, h]
                m_new = jnp.maximum(m_old, jnp.max(s, axis=0, keepdims=True))
                alpha = jnp.exp2(m_old - m_new)
                p = jnp.exp2(s - m_new)
                l_s[j, h] = l_s[j, h] * alpha + jnp.sum(p, axis=0, keepdims=True)
                m_s[j, h] = m_new
                acc[j, h] = acc[j, h] * alpha + nn(values[h // group], p.astype(BF))

        for j in range(2):
            own_block = own_ref[j]

            @pl.when(key_block < own_block)
            def _():
                step(j, False)

            @pl.when(key_block == own_block)
            def _():
                step(j, True)

        return 0

    lax.fori_loop(0, 2 * n_ctx, body, 0)
    for j in range(2):
        outs = []
        for h in range(q_heads):
            out = acc[j, h] / l_s[j, h]
            mixt_ref[j, h] = out.astype(BF)
            lse_ref[j, h] = m_s[j, h] + jnp.log2(l_s[j, h])
            outs.append(out.T)
        mix_ref[:, j] = jnp.concatenate(outs, axis=-1).astype(BF).reshape(n_t, sp, -1)


def flash_forward(order, own, q, kv):
    n_ctx, n_t, _, sp, width = kv.shape
    q_heads = q.shape[-1] // HEAD_DIM
    length = n_t * sp
    vm = pl.BlockSpec(memory_space=pltpu.VMEM)
    sm = pl.BlockSpec(memory_space=pltpu.SMEM)
    rows = (2, q_heads, 1, length)
    cols = (2, q_heads, HEAD_DIM, length)
    return pl.pallas_call(
        fwd_kernel,
        out_shape=(
            jax.ShapeDtypeStruct(q.shape, BF),
            jax.ShapeDtypeStruct(cols, BF),
            jax.ShapeDtypeStruct(rows, F32),
        ),
        in_specs=[sm, sm, vm, vm],
        out_specs=(vm, vm, vm),
        scratch_shapes=[
            pltpu.VMEM(cols, BF),
            pltpu.VMEM(rows, F32),
            pltpu.VMEM(rows, F32),
            pltpu.VMEM(cols, F32),
        ],
        compiler_params=pltpu.CompilerParams(vmem_limit_bytes=48 * 2**20),
    )(order, own, q, kv)


def bwd_kernel(
    order_ref, own_ref, q_ref, kv_ref, do_ref, mixt_ref, lse_ref, cos_ref, sin_ref,
    dq_ref, dkv_ref, qt, dot, qn, don, dl_s, dqt,
):
    n_ctx, n_t, _, sp, width = kv_ref.shape
    length = n_t * sp
    kv_heads = width // (2 * HEAD_DIM)
    q_heads = q_ref.shape[-1] // HEAD_DIM
    group = q_heads // kv_heads
    scale = HEAD_DIM**-0.5
    for j in range(2):
        x = q_ref[:, j].reshape(length, -1)
        y = do_ref[:, j].reshape(length, -1)
        for h in range(q_heads):
            a = head_of(x, h)
            qn[j, h] = a
            qt[j, h] = transposed(a)
            b = head_of(y, h)
            don[j, h] = b
            bt = b.astype(F32).T
            dot[j, h] = bt.astype(BF)
            dl_s[j, h] = jnp.sum(bt * mixt_ref[j, h].astype(F32), axis=0, keepdims=True)
    dqt[...] = jnp.zeros_like(dqt)

    def body(k, _):
        c_at = k // 2
        j_at = lax.rem(k, 2)
        key_block = order_ref[k]
        x = kv_ref[c_at, :, pl.ds(j_at, 1)].reshape(length, width)
        for kh in range(kv_heads):
            key = head_of(x, kh)
            value = head_of(x, kv_heads + kh)
            key_t = transposed(key)

            def step(j, masked, dk, dv):
                for g in range(group):
                    h = kh * group + g
                    s = nn(key, qt[j, h]) * (scale * LOG2E)
                    p = jnp.exp2(s - lse_ref[j, h])
                    if masked:
                        p = jnp.where(causal(length), p, 0.0)
                    dp = nn(value, dot[j, h])
                    ds = (p * (dp - dl_s[j, h])).astype(BF)
                    dv = dv + nn(p.astype(BF), don[j, h])
                    dk = dk + nn(ds, qn[j, h])
                    dqt[j, h] += nn(key_t, ds)
                return dk, dv

            dk = jnp.zeros((length, HEAD_DIM), F32)
            dv = dk
            for j in range(2):
                own_block = own_ref[j]
                dk, dv = lax.cond(
                    key_block < own_block,
                    lambda a, b: step(j, False, a, b),
                    lambda a, b: lax.cond(
                        key_block == own_block,
                        lambda a, b: step(j, True, a, b),
                        lambda a, b: (a, b),
                        a,
                        b,
                    ),
                    dk,
                    dv,
                )
            at = pl.ds(j_at, 1)
            shape = (n_t, 1, sp, HEAD_DIM)
            lo, hi = kh * HEAD_DIM, (kv_heads + kh) * HEAD_DIM
            dkv_ref[c_at, :, at, :, lo : lo + HEAD_DIM] = (dk * scale).astype(BF).reshape(shape)
            dkv_ref[c_at, :, at, :, hi : hi + HEAD_DIM] = dv.astype(BF).reshape(shape)
        return 0

    lax.fori_loop(0, 2 * n_ctx, body, 0)
    half = HEAD_DIM // 2
    for j in range(2):
        outs = []
        for h in range(q_heads):
            d = dqt[j, h] * scale
            sc = d * sin_ref[j]
            back = d * cos_ref[j] + jnp.concatenate([sc[half:], -sc[:half]], axis=0)
            outs.append(back.T)
        dq_ref[:, j] = jnp.concatenate(outs, axis=-1).astype(BF).reshape(n_t, sp, -1)


def flash_backward(order, own, q, kv, do, mixt, lse, cos_t, sin_t):
    n_ctx, n_t, _, sp, width = kv.shape
    q_heads = q.shape[-1] // HEAD_DIM
    length = n_t * sp
    vm = pl.BlockSpec(memory_space=pltpu.VMEM)
    sm = pl.BlockSpec(memory_space=pltpu.SMEM)
    cols = pltpu.VMEM((2, q_heads, HEAD_DIM, length), BF)
    natural = pltpu.VMEM((2, q_heads, length, HEAD_DIM), BF)
    return pl.pallas_call(
        bwd_kernel,
        out_shape=(jax.ShapeDtypeStruct(q.shape, BF), jax.ShapeDtypeStruct(kv.shape, BF)),
        in_specs=[sm, sm] + [vm] * 7,
        out_specs=(vm, vm),
        scratch_shapes=[
            cols,
            cols,
            natural,
            natural,
            pltpu.VMEM((2, q_heads, 1, length), F32),
            pltpu.VMEM((2, q_heads, HEAD_DIM, length), F32),
        ],
        compiler_params=pltpu.CompilerParams(vmem_limit_bytes=48 * 2**20),
    )(order, own, q, kv, do, mixt, lse, cos_t, sin_t)


def rms_norm(v, gain):
    return v * lax.rsqrt(jnp.mean(v * v, axis=-1, keepdims=True) + EPSILON) * gain


def silu_product(gate, up):
    return gate * jax.nn.sigmoid(gate) * up


def turn_matrix(heads, total):
    half = HEAD_DIM // 2
    m = np.zeros((total, total), np.float32)
    for h in range(heads):
        at = h * HEAD_DIM
        for i in range(half):
            m[at + half + i, at + i] = -1.0
            m[at + i, at + half + i] = 1.0
    return m


def swap(value):
    return lax.ppermute(value, "section", [(0, 1), (1, 0)])


def gather_rows(x):
    return lax.all_gather(x, "tensor", axis=0)


def scatter_rows(x):
    return lax.psum_scatter(x.astype(BF), "tensor", scatter_dimension=0).astype(F32)


def on_device(
    inputs, cotangent, block_order, attn_gain, w_query, key_weight, value_weight, w_out,
    mlp_gain, w_gate, w_up, w_down,
):
    sec = lax.axis_index("section")
    first = sec == 0
    ctx = lax.axis_index("ctx")
    n_t = lax.axis_size("tensor")
    n_ctx = lax.axis_size("ctx")
    _, _, _, sp, half_width = inputs.shape
    length = sp * n_t
    d = 2 * half_width
    rows = n_t * 2 * sp
    wq, wk, wv = w_query[0], key_weight[0], value_weight[0]
    q_w, kv_w = wq.shape[1], 2 * wk.shape[1]
    qkv_w = q_w + kv_w
    q_heads, kv_heads = q_w // HEAD_DIM, kv_w // (2 * HEAD_DIM)

    def to_own(x):
        keep = lax.dynamic_index_in_dim(x[:, 0], sec, 0, keepdims=False)
        give = lax.dynamic_index_in_dim(x[:, 0], 1 - sec, 0, keepdims=False)
        got = swap(give)
        return jnp.where(
            first, jnp.concatenate([keep, got], -1), jnp.concatenate([got, keep], -1)
        )

    def from_own(y, out_dtype):
        lo, hi = y[..., :half_width], y[..., half_width:]
        keep = jnp.where(first, lo, hi)
        got = swap(jnp.where(first, hi, lo).astype(BF)).astype(y.dtype)
        return jnp.where(first, jnp.stack([keep, got]), jnp.stack([got, keep]))[
            :, None
        ].astype(out_dtype)

    x_own = to_own(inputs)
    g_own = to_own(cotangent)

    turn_q = jnp.asarray(turn_matrix(q_heads, q_w), BF)
    turn_kv = turn_matrix(kv_heads, kv_w)
    wkv = jnp.concatenate([wk, wv], 1)
    wcat = jnp.concatenate(
        [wq, wkv, nn(wq, turn_q).astype(BF), nn(wkv, jnp.asarray(turn_kv, BF)).astype(BF)], 1
    )

    def both(w):
        return lax.all_gather(w, "section", axis=0)

    wcat2, wo2, wg2, wu2, wd2, gains2 = (
        both(wcat), both(w_out[0]), both(w_gate[0]), both(w_up[0]), both(w_down[0]),
        both(jnp.concatenate([attn_gain, mlp_gain], 0)),
    )

    own = lax.dynamic_slice_in_dim(block_order, 2 * ctx, 2, 0)
    offs = jnp.arange(length, dtype=jnp.int32)
    pos = own[:, None] * length + offs[None, :]
    freq = ROPE_BASE ** (-(jnp.arange(0, HEAD_DIM, 2).astype(F32) / HEAD_DIM))
    phase_t = freq[None, :, None] * pos.astype(F32)[:, None, :]
    phase_t = jnp.concatenate([phase_t, phase_t], 1)
    cos_t, sin_t = jnp.cos(phase_t), jnp.sin(phase_t)

    def rows_of(t):
        t = jnp.swapaxes(t, 1, 2).reshape(2, n_t, sp, HEAD_DIM)
        return jnp.swapaxes(t, 0, 1).reshape(rows, HEAD_DIM)

    cos_r, sin_r = rows_of(cos_t), rows_of(sin_t)
    ones = jnp.ones((rows, kv_w // 2), F32)
    cos_kv = jnp.concatenate([jnp.tile(cos_r, (1, kv_heads)), ones], 1)
    sin_kv = jnp.concatenate([jnp.tile(sin_r, (1, kv_heads)), 0 * ones], 1)
    cos_all = jnp.concatenate([jnp.tile(cos_r, (1, q_heads)), cos_kv], 1)
    sin_all = jnp.concatenate([jnp.tile(sin_r, (1, q_heads)), sin_kv], 1)

    def forward(h, layer):
        a_gain, m_gain = gains2[layer, 0], gains2[layer, 1]
        n1 = gather_rows(rms_norm(h, a_gain).astype(BF)).reshape(rows, d)
        raw = nn(n1, wcat2[layer])
        qkv = (raw[:, :qkv_w] * cos_all + raw[:, qkv_w:] * sin_all).astype(BF)
        q = qkv[:, :q_w].reshape(n_t, 2, sp, q_w)
        kv = lax.all_gather(qkv[:, q_w:].reshape(n_t, 2, sp, kv_w), "ctx", axis=0)
        mix, mixt, lse = flash_forward(block_order, own, q, kv)
        part = nn(mix.reshape(rows, q_w), wo2[layer])
        h2 = h + scatter_rows(part.reshape(n_t, 2, sp, d))
        n2 = gather_rows(rms_norm(h2, m_gain).astype(BF)).reshape(rows, d)
        gate, up = nn(n2, wg2[layer]), nn(n2, wu2[layer])
        act = silu_product(gate, up).astype(BF)
        out = h2 + scatter_rows(nn(act, wd2[layer]).reshape(n_t, 2, sp, d))
        return out, (h, n1, q, kv, mix, mixt, lse, h2, n2, gate, up, act)

    def reduce_grad(g):
        g = lax.psum_scatter(g.astype(BF), "section", scatter_dimension=0, tiled=True)
        return lax.psum(g, "ctx")

    def backward(g, gm, layer, kept):
        h, n1, q, kv, mix, mixt, lse, h2, n2, gate, up, act = kept
        a_gain, m_gain = gains2[layer, 0], gains2[layer, 1]
        gm = gather_rows(gm).reshape(rows, d)
        dact = nt(gm, wd2[layer])
        _, pull = jax.vjp(silu_product, gate, up)
        dgate, dup = pull(dact)
        dgate, dup = dgate.astype(BF), dup.astype(BF)
        dn2 = scatter_rows((nt(dgate, wg2[layer]) + nt(dup, wu2[layer])).reshape(n_t, 2, sp, d))
        _, pull = jax.vjp(rms_norm, h2, m_gain)
        dh2, d_mg = pull(dn2)
        dh2 = g + dh2
        ga = gather_rows(dh2.astype(BF)).reshape(rows, d)
        dmix = nt(ga, wo2[layer]).astype(BF)
        dq, dkv = flash_backward(
            block_order, own, q, kv, dmix.reshape(n_t, 2, sp, q_w), mixt, lse, cos_t, sin_t
        )
        dkv = lax.psum_scatter(dkv, "ctx", scatter_dimension=0).astype(F32).reshape(rows, kv_w)
        turned = lax.dot_general(
            dkv * sin_kv,
            jnp.asarray(-turn_kv),
            (((1,), (0,)), ((), ())),
            precision=lax.Precision.HIGHEST,
            preferred_element_type=F32,
        )
        dkv = (dkv * cos_kv + turned).astype(BF)
        dqkv = jnp.concatenate([dq.reshape(rows, q_w), dkv], 1)
        dn1 = scatter_rows(nt(dqkv, wcat2[layer][:, :qkv_w]).reshape(n_t, 2, sp, d))
        _, pull = jax.vjp(rms_norm, h, a_gain)
        dh, d_ag = pull(dn1)
        dh = dh2 + dh
        grads = (
            reduce_grad(tn(act, gm)),
            reduce_grad(tn(n2, dgate)),
            reduce_grad(tn(n2, dup)),
            reduce_grad(tn(mix.reshape(rows, q_w), ga)),
            reduce_grad(tn(n1, dqkv)),
        )
        return dh, (d_ag, d_mg), grads

    out0, kept0 = forward(x_own.astype(F32), 0)
    y, kept1 = forward(out0.astype(BF).astype(F32), 1)
    dh1, gains1, grads1 = backward(g_own.astype(F32), g_own, 1, kept1)
    g0 = dh1.astype(BF)
    dh0, gains0, grads0 = backward(g0.astype(F32), g0, 0, kept0)

    gain_sum = lax.psum(jnp.stack([jnp.stack(gains0), jnp.stack(gains1)]), ("section", "ctx", "tensor"))
    gain_own = lax.dynamic_index_in_dim(gain_sum, sec, 0, keepdims=False)

    def to_owner(r0, r1):
        got = swap(jnp.where(first, r1, r0))
        keep = jnp.where(first, r0, r1)
        return jnp.where(
            first, jnp.concatenate([keep, got], 0), jnp.concatenate([got, keep], 0)
        ).astype(F32)

    gd, gg, gu, go, gqkv = (to_owner(a, b) for a, b in zip(grads0, grads1))
    half_kv = kv_w // 2
    return (
        from_own(y, BF),
        from_own(dh0, F32),
        gain_own[0:1],
        gqkv[None, :, :q_w],
        gqkv[None, :, q_w : q_w + half_kv],
        gqkv[None, :, q_w + half_kv :],
        go[None],
        gain_own[1:2],
        gg[None],
        gu[None],
        gd[None],
    )


def solution(mesh):
    rows = P(None, "ctx", None, "tensor", "section")
    gain = P("section", None)
    col = P("section", None, "tensor")
    row = P("section", "tensor", None)
    return jax.shard_map(
        on_device,
        mesh=mesh,
        in_specs=(rows, rows, P(), gain, col, col, col, row, gain, col, col, row),
        out_specs=(rows, rows, gain, col, col, col, row, gain, col, col, row),
        check_vma=False,
    )
```

time: 3550 us -> 1980 us (0.56)
  matrix products: 1240 us -> 218 us
  local copies, waits for them, and re-layouts: 719 us -> 73.8 us
  waiting for transfers between devices: 1220 us -> 1400 us
  other arithmetic: 227 us -> 77 us
  Pallas kernels: 0 us -> 134 us
    dot_general x78 -> x35, matrix products: 1050 us -> 218 us  [the longest x13 78 us: nn(): lax.dot_general(a, b, (((1,), (0,)), ((), ())), preferred_element_type=F32)]
    unnamed x3 -> x44, waiting for transfers between devices: 1.39 us -> 352 us
    reshape x69 -> x6, local copies, waits for them, and re-layouts: 266 us -> 3.25 us  [the longest x2 2.37 us: backward(): dqkv = jnp.concatenate([dq.reshape(rows, q_w), dkv], 1)]
    sub x6 -> x0, matrix products: 193 us -> none  [attention_probs(): powers = jnp.exp(masked - largest)]
    reduce_scatter x18 -> x12, waiting for transfers between devices: 313 us -> 159 us  [the longest x10 102 us: reduce_grad(): lax.psum_scatter(g.astype(BF), 'section', scatter_dimension=0, tiled=True)]
    pallas_call x0 -> x4, Pallas kernels: none -> 134 us  [the longest x2 86 us: flash_backward(): pl.pallas_call(bwd_kernel, out_shape=(jax.ShapeDtypeStruct(q.shape, BF),...]
    all_gather x24 -> x0, local copies, waits for them, and re-layouts: 122 us -> none  [the longest x6 40.8 us: gather_rows(): return lax.all_gather(normalized_input, 'tensor', axis=0, tiled=True)]
    convert_element_type x35 -> x2, local copies, waits for them, and re-layouts: 91.9 us -> 5.15 us  [backward(): lax.psum_scatter(dkv, 'ctx', scatter_dimension=0).astype(F32)]
  transfers between devices with their start and end apart: 52 -> 45, of which waited for: 30 -> 34; matrix products, arithmetic and copies ran while one was open for 32% -> 10% of each run, Pallas kernels for 0% -> 1%
where the time goes in v1:
time: 1980 us; the launch traced here: 1970 us
  waiting for transfers between devices  1400 us (71%)
  matrix products  218 us (11%)
  Pallas kernels  134 us (7%)
  other arithmetic  77 us (4%)
  local copies, waits for them, and re-layouts  73.8 us (4%)
  blocking collectives  45.6 us (2%)
    psum x1, waiting for transfers between devices, reduce_grad(): return lax.psum(g, 'ctx')  395 us
    unnamed x44, waiting for transfers between devices  352 us
    all_gather x8, waiting for transfers between devices, gather_rows(): return lax.all_gather(x, 'tensor', axis=0)  312 us
    all_gather x2, waiting for transfers between devices, forward(): kv = lax.all_gather(qkv[:, q_w:].reshape(n_t, 2, sp, kv_w), 'ctx', axis=0)  127 us
    reduce_scatter x10, waiting for transfers between devices, reduce_grad(): lax.psum_scatter(g.astype(BF), 'section', scatter_dimension=0, tiled=True)  102 us
    pallas_call x2, Pallas kernels, flash_backward(): pl.pallas_call(bwd_kernel, out_shape=(jax.ShapeDtypeStruct(q.shape, BF),...  86 us
    dot_general x13, matrix products, nn(): lax.dot_general(a, b, (((1,), (0,)), ((), ())), preferred_element_type=F32)  78 us
    dot_general x10, matrix products, nt(): lax.dot_general(a, b, (((1,), (1,)), ((), ())), preferred_element_type=F32)  68.8 us
  transfers between devices with their start and end apart: 45, of which 34 were waited for; matrix products, arithmetic and copies ran while one was open for 10% of the time, Pallas kernels for 1%

profile of v1, /device:TPU:0, one launch (start us, length us, event | category | flops | bytes accessed | tf_op | source)
XLA Modules:
  0.0 1971.2 jit_solution(2328310915405543816)
XLA Ops:
  40.7 18.9 all-gather.19.cloned.1.call-done
  59.7 24.0 %all-gather.47.cloned.1.call-done = bf16[3072,1536]{0,1:T(8,128)(2,1)} async-done(((bf16[1536,1536]{0,1:T(8,128)(2,1)}), bf16[3072,1536]{0,1:T(8,128)(2,1)}) %all-gather.47.cloned.1.call-update) | async-done | bytes 9437200 | tf_op jit(solution)/shard_map/all_gather | solution.py:315
  83.7 8.0 fusion.2
  94.8 64.0 %all-gather.21.cloned.1.call-done.kv_ref = bf16[4,4,2,128,384]{4,3,2,1,0:T(8,128)(2,1)} async-done(((bf16[1,4,2,128,384]{4,3,2,1,0:T(8,128)(2,1)}), bf16[4,4,2,128,384]{4,3,2,1,0:T(8,128)(2,1)}) %all-gather.21.cloned.1.call-update) | async-done | bytes 3145744 | tf_op jit(solution)/shard_map/all_gather | solution.py:347
  160.7 23.9 %shard_map.239 = (bf16[4,2,128,384]{3,2,1,0:T(8,128)(2,1)S(1)}, bf16[2,4,96,512]{3,2,1,0:T(8,128)(2,1)S(1)}, f32[2,4,1,512]{3,2,1,0:T(1,128)S(1)}) custom-call(s32[8]{0:T(128)S(1)} %copy-done.10, s32[2]{0:T(128)S(1)} %get-tuple-element.91.own_ref, bf16[4,2,128,384]{3,2,1,0:T(8,128)(2,1)S(1)} %bitcast.345, bf16[4,4,2,128,384]{4,3,2,1,0:T(8,128)(2,1)S(1)} %copy-done), custom_call_target="tpu_custom_call" | custom-call | tf_op jit(solution)/shard_map/pallas_call | solution.py:111
  185.4 5.0 convolution_convert_fusion.3
  191.1 42.1 %reduce-scatter.61.cloned.1.call-done = bf16[1,2,128,1536]{3,2,1,0:T(8,128)(2,1)} async-done(((bf16[4,2,128,1536]{3,2,1,0:T(8,128)(2,1)}), bf16[1,2,128,1536]{3,2,1,0:T(8,128)(2,1)}) %reduce-scatter.61.cloned.1.call-update) | async-done | bytes 786448
  239.2 12.2 all-gather.27.cloned.1.call-done
  251.4 47.6 %all-gather.25.cloned.1.call-done = bf16[4,2,128,1536]{3,2,1,0:T(8,128)(2,1)} async-done(((bf16[1,2,128,1536]{3,2,1,0:T(8,128)(2,1)}), bf16[4,2,128,1536]{3,2,1,0:T(8,128)(2,1)}) %all-gather.25.cloned.1.call-update) | async-done | bytes 3145744 | tf_op jit(solution)/shard_map/all_gather | solution.py:263
  299.0 8.3 fusion.29
  307.3 10.0 all-gather.29.cloned.1.call-done
  317.3 10.7 multiply_convert_fusion.3
  328.0 8.8 all-gather.31.cloned.1.call-done
  336.8 7.6 convolution_convert_fusion.11
  344.5 45.2 %reduce-scatter.63.cloned.1.call-done = bf16[1,2,128,1536]{3,2,1,0:T(8,128)(2,1)} async-done(((bf16[4,2,128,1536]{3,2,1,0:T(8,128)(2,1)}), bf16[1,2,128,1536]{3,2,1,0:T(8,128)(2,1)}) %reduce-scatter.63.cloned.1.call-update) | async-done | bytes 786448
  394.2 44.1 %all-gather.33.cloned.1.call-done = bf16[4,2,128,1536]{3,2,1,0:T(8,128)(2,1)} async-done(((bf16[1,2,128,1536]{3,2,1,0:T(8,128)(2,1)}), bf16[4,2,128,1536]{3,2,1,0:T(8,128)(2,1)}) %all-gather.33.cloned.1.call-update) | async-done | bytes 3145744 | tf_op jit(solution)/shard_map/all_gather | solution.py:263
  438.3 8.1 fusion
  448.8 63.4 %all-gather.35.cloned.1.call-done.kv_ref = bf16[4,4,2,128,384]{4,3,2,1,0:T(8,128)(2,1)} async-done(((bf16[1,4,2,128,384]{4,3,2,1,0:T(8,128)(2,1)}), bf16[4,4,2,128,384]{4,3,2,1,0:T(8,128)(2,1)}) %all-gather.35.cloned.1.call-update) | async-done | bytes 3145744 | tf_op jit(solution)/shard_map/all_gather | solution.py:347
  514.1 23.9 %shard_map.240 = (bf16[4,2,128,384]{3,2,1,0:T(8,128)(2,1)S(1)}, bf16[2,4,96,512]{3,2,1,0:T(8,128)(2,1)S(1)}, f32[2,4,1,512]{3,2,1,0:T(1,128)S(1)}) custom-call(s32[8]{0:T(128)S(1)} %copy-done.10, s32[2]{0:T(128)S(1)} %get-tuple-element.91.own_ref, bf16[4,2,128,384]{3,2,1,0:T(8,128)(2,1)S(1)} %bitcast.347, bf16[4,4,2,128,384]{4,3,2,1,0:T(8,128)(2,1)S(1)} %copy-done.1), custom_call_target="tpu_custom_call" | custom-call | tf_op jit(solution)/shard_map/pallas_call | solution.py:111
  542.4 42.7 %reduce-scatter.65.cloned.1.call-done = bf16[1,2,128,1536]{3,2,1,0:T(8,128)(2,1)} async-done(((bf16[4,2,128,1536]{3,2,1,0:T(8,128)(2,1)}), bf16[1,2,128,1536]{3,2,1,0:T(8,128)(2,1)}) %reduce-scatter.65.cloned.1.call-update) | async-done | bytes 786448
  594.2 38.1 %all-gather.37.cloned.1.call-done = bf16[4,2,128,1536]{3,2,1,0:T(8,128)(2,1)} async-done(((bf16[1,2,128,1536]{3,2,1,0:T(8,128)(2,1)}), bf16[4,2,128,1536]{3,2,1,0:T(8,128)(2,1)}) %all-gather.37.cloned.1.call-update) | async-done | bytes 3145744 | tf_op jit(solution)/shard_map/all_gather | solution.py:263
  632.3 8.3 fusion.33
  640.6 7.3 fusion.32
  647.8 30.7 %all-gather.39.cloned.1.call-done = bf16[4,2,128,1536]{3,2,1,0:T(8,128)(2,1)} async-done(((bf16[1,2,128,1536]{3,2,1,0:T(8,128)(2,1)}), bf16[4,2,128,1536]{3,2,1,0:T(8,128)(2,1)}) %all-gather.39.cloned.1.call-update) | async-done | bytes 3145744 | tf_op jit(solution)/shard_map/all_gather | solution.py:263
  678.5 11.5 multiply_convert_fusion.1
  690.1 6.9 fusion.31
  697.0 6.9 add_convert_fusion.1
  704.0 44.1 %reduce-scatter.69.cloned.1.call-done = bf16[1,2,128,1536]{3,2,1,0:T(8,128)(2,1)} async-done(((bf16[4,2,128,1536]{3,2,1,0:T(8,128)(2,1)}), bf16[1,2,128,1536]{3,2,1,0:T(8,128)(2,1)}) %reduce-scatter.69.cloned.1.call-update) | async-done | bytes 786448
  753.8 44.1 %all-gather.41.cloned.1.call-done = bf16[4,2,128,1536]{3,2,1,0:T(8,128)(2,1)} async-done(((bf16[1,2,128,1536]{3,2,1,0:T(8,128)(2,1)}), bf16[4,2,128,1536]{3,2,1,0:T(8,128)(2,1)}) %all-gather.41.cloned.1.call-update) | async-done | bytes 3145744 | tf_op jit(solution)/shard_map/all_gather | solution.py:263
  802.0 43.0 %shard_map.241 = (bf16[4,2,128,384]{3,2,1,0:T(8,128)(2,1)S(1)}, bf16[4,4,2,128,384]{4,3,2,1,0:T(8,128)(2,1)}) custom-call(s32[8]{0:T(128)S(1)} %copy-done.10, s32[2]{0:T(128)S(1)} %get-tuple-element.91.own_ref, bf16[4,2,128,384]{3,2,1,0:T(8,128)(2,1)S(1)} %bitcast.348, bf16[4,4,2,128,384]{4,3,2,1,0:T(8,128)(2,1)} %all-gather.35.cloned.1.call-done.kv_ref, ...), custom_call_target="tpu_custom_call" | custom-call | tf_op jit(solution)/shard_map/pallas_call | solution.py:222
  848.2 57.1 %reduce-scatter.37.cloned.1.call-done = bf16[1,4,2,128,384]{4,3,2,1,0:T(8,128)(2,1)} async-done(((bf16[4,4,2,128,384]{4,3,2,1,0:T(8,128)(2,1)}), bf16[1,4,2,128,384]{4,3,2,1,0:T(8,128)(2,1)}) %reduce-scatter.37.cloned.1.call-update) | async-done | bytes 786448 | tf_op jit(solution)/shard_map/reduce_scatter | solution.py:378
  910.9 5.2 fusion.58
  916.1 6.0 convolution_convert_fusion.1
  922.1 44.1 %reduce-scatter.71.cloned.1.call-done = bf16[1,2,128,1536]{3,2,1,0:T(8,128)(2,1)} async-done(((bf16[4,2,128,1536]{3,2,1,0:T(8,128)(2,1)}), bf16[1,2,128,1536]{3,2,1,0:T(8,128)(2,1)}) %reduce-scatter.71.cloned.1.call-update) | async-done | bytes 786448
  972.5 44.1 %all-gather.43.cloned.1.call-done = bf16[4,2,128,1536]{3,2,1,0:T(8,128)(2,1)} async-done(((bf16[1,2,128,1536]{3,2,1,0:T(8,128)(2,1)}), bf16[4,2,128,1536]{3,2,1,0:T(8,128)(2,1)}) %all-gather.43.cloned.1.call-update) | async-done | bytes 3145744 | tf_op jit(solution)/shard_map/all_gather | solution.py:263
  1016.6 9.9 multiply_convert_fusion
  1026.5 6.9 fusion.28
  1033.4 6.9 add_convert_fusion
  1040.4 44.0 %reduce-scatter.73.cloned.1.call-done = bf16[1,2,128,1536]{3,2,1,0:T(8,128)(2,1)} async-done(((bf16[4,2,128,1536]{3,2,1,0:T(8,128)(2,1)}), bf16[1,2,128,1536]{3,2,1,0:T(8,128)(2,1)}) %reduce-scatter.73.cloned.1.call-update) | async-done | bytes 786448
  1090.2 44.1 %all-gather.45.cloned.1.call-done = bf16[4,2,128,1536]{3,2,1,0:T(8,128)(2,1)} async-done(((bf16[1,2,128,1536]{3,2,1,0:T(8,128)(2,1)}), bf16[4,2,128,1536]{3,2,1,0:T(8,128)(2,1)}) %all-gather.45.cloned.1.call-update) | async-done | bytes 3145744 | tf_op jit(solution)/shard_map/all_gather | solution.py:263
  1138.4 43.0 %shard_map.242 = (bf16[4,2,128,384]{3,2,1,0:T(8,128)(2,1)S(1)}, bf16[4,4,2,128,384]{4,3,2,1,0:T(8,128)(2,1)}) custom-call(s32[8]{0:T(128)S(1)} %copy-done.10, s32[2]{0:T(128)S(1)} %get-tuple-element.91.own_ref, bf16[4,2,128,384]{3,2,1,0:T(8,128)(2,1)S(1)} %bitcast.346, bf16[4,4,2,128,384]{4,3,2,1,0:T(8,128)(2,1)} %all-gather.21.cloned.1.call-done.kv_ref, ...), custom_call_target="tpu_custom_call" | custom-call | tf_op jit(solution)/shard_map/pallas_call | solution.py:222
  1181.7 7.7 convolution_convert_fusion.4
  1189.5 7.7 convolution_convert_fusion.8
  1197.2 7.7 convolution_convert_fusion.6
  1209.9 6.0 convolution_convert_fusion.12
  1217.5 6.7 convolution_convert_fusion.5
  1225.8 6.8 convolution_convert_fusion.9
  1234.2 6.7 convolution_convert_fusion.7
  1262.9 7.5 convolution_convert_fusion.10
  1271.7 5.7 convolution_convert_fusion
  1277.5 5.6 reduce-scatter.55.cloned.1.call-done
  1283.1 12.6 reduce-scatter.47.cloned.1.call-done
  1295.7 14.0 reduce-scatter.43.cloned.1.call-done
  1309.7 14.4 reduce-scatter.57.cloned.1.call-done
  1324.1 14.2 reduce-scatter.49.cloned.1.call-done
  1338.3 14.4 reduce-scatter.53.cloned.1.call-done
  1352.7 12.7 reduce-scatter.45.cloned.1.call-done
  1365.4 13.9 reduce-scatter.41.cloned.1.call-done
  1379.3 48.7 %reduce-scatter.67.cloned.1.call-done = bf16[1,2,128,1536]{3,2,1,0:T(8,128)(2,1)} async-done(((bf16[4,2,128,1536]{3,2,1,0:T(8,128)(2,1)}), bf16[1,2,128,1536]{3,2,1,0:T(8,128)(2,1)}) %reduce-scatter.67.cloned.1.call-update) | async-done | bytes 786448
  1437.4 38.1 %reduce-scatter.75.cloned.1.call-done = bf16[1,2,128,1536]{3,2,1,0:T(8,128)(2,1)} async-done(((bf16[4,2,128,1536]{3,2,1,0:T(8,128)(2,1)}), bf16[1,2,128,1536]{3,2,1,0:T(8,128)(2,1)}) %reduce-scatter.75.cloned.1.call-update) | async-done | bytes 786448
  1483.2 43.8 %psum.77 = f32[2,2,1536]{2,1,0:T(2,128)S(1)} all-reduce(f32[2,2,1536]{2,1,0:T(2,128)S(1)} %pad_maximum_fusion.7), channel_id=1, replica_groups=mesh['section'=2,'ctx'=4,'tensor'=4] {'section','ctx','tensor'}, use_global_device_ids=true, to_apply=%region_22.23 | all-reduce | flops 6144 | bytes 49152 | tf_op jit(solution)/shard_map/psum | solution.py:407
  1530.3 395.1 %all-reduce.13.cloned.1.call-done = (bf16[768,768]{1,0:T(8,128)(2,1)}, bf16[768,768]{1,0:T(8,128)(2,1)}, bf16[192,1536]{1,0:T(8,128)(2,1)}, bf16[192,1536]{1,0:T...) async-done(((bf16[768,768]{1,0:T(8,128)(2,1)}, ...) | async-done | bytes 12976144 | tf_op jit(solution)/shard_map/psum | solution.py:359
  1950.5 4.8 fusion.16
  1955.3 4.8 fusion.17
  (401 shorter events, 185.6 us)
Async XLA Ops:
  7.2 52.5 %all-gather.19.cloned.1.call-start = ((), (), s32[]{:S(2)}) async-start(), calls=%async_computation.20 | async-start | bytes 3932160 | tf_op jit(solution)/shard_map/all_gather | solution.py:263
  8.4 381.3 %copy-start.23 = (bf16[2,128,768]{2,1,0:T(8,128)(2,1)}, bf16[2,128,768]{2,1,0:T(8,128)(2,1)S(1)}, u32[]{:S(2)}) copy-start(bf16[2,128,768]{2,1,0:T(8,128)(2,1)S(1)} %get-tuple-element.120) | copy-start | bytes 1179652
  8.5 3.2 collective-permute-start
  11.6 1075.8 %copy-start.76 = (f32[1536]{0:T(1024)}, f32[1536]{0:T(1024)S(1)}, u32[]{:S(2)}) copy-start(f32[1536]{0:T(1024)S(1)} %get-tuple-element.74) | copy-start | bytes 18436
  11.6 380.8 %copy-start.11 = (bf16[2,128,768]{2,1,0:T(8,128)(2,1)}, bf16[2,128,768]{2,1,0:T(8,128)(2,1)S(1)}, u32[]{:S(2)}) copy-start(bf16[2,128,768]{2,1,0:T(8,128)(2,1)S(1)} %collective-permute-done) | copy-start | bytes 1179652
  13.1 70.6 %all-gather.47.cloned.1.call-start = ((), (), s32[]{:S(2)}) async-start(), calls=%async_computation.46 | async-start | bytes 14155776 | tf_op jit(solution)/shard_map/all_gather | solution.py:315
  22.5 136.2 %all-gather.21.cloned.1.call-start = ((), (), s32[]{:S(2)}) async-start(), calls=%async_computation.21 | async-start | bytes 3932160 | tf_op jit(solution)/shard_map/all_gather | solution.py:347
  93.9 91.5 %all-gather.23.cloned.1.call-start = ((), (), s32[]{:S(2)}) async-start(), calls=%async_computation.22 | async-start | bytes 3538944 | tf_op jit(solution)/shard_map/all_gather | solution.py:315
  94.5 138.7 %reduce-scatter.61.cloned.1.call-start = ((), (), s32[]{:S(2)}) async-start(), calls=%async_computation.47 | async-start | bytes 3932160
  190.5 60.9 %all-gather.27.cloned.1.call-start = ((), (), s32[]{:S(2)}) async-start(), calls=%async_computation.24 | async-start | bytes 9437184 | tf_op jit(solution)/shard_map/all_gather | solution.py:315
  191.0 107.9 %all-gather.25.cloned.1.call-start = ((), (), s32[]{:S(2)}) async-start(), calls=%async_computation.23 | async-start | bytes 3932160 | tf_op jit(solution)/shard_map/all_gather | solution.py:263
  234.8 852.5 %copy-start.80 = (f32[2,128]{1,0:T(2,128)}, f32[2,128]{1,0:T(2,128)S(1)}, u32[]{:S(2)}) copy-start(f32[2,128]{1,0:T(2,128)S(1)} %fusion.114) | copy-start | bytes 3076
  237.3 80.1 %all-gather.29.cloned.1.call-start = ((), (), s32[]{:S(2)}) async-start(), calls=%async_computation.25 | async-start | bytes 9437184 | tf_op jit(solution)/shard_map/all_gather | solution.py:315
  238.0 98.8 %all-gather.31.cloned.1.call-start = ((), (), s32[]{:S(2)}) async-start(), calls=%async_computation.26 | async-start | bytes 9437184 | tf_op jit(solution)/shard_map/all_gather | solution.py:315
  238.7 151.0 %reduce-scatter.63.cloned.1.call-start = ((), (), s32[]{:S(2)}) async-start(), calls=%async_computation.48 | async-start | bytes 3932160
  344.4 93.8 %all-gather.33.cloned.1.call-start = ((), (), s32[]{:S(2)}) async-start(), calls=%async_computation.27 | async-start | bytes 3932160 | tf_op jit(solution)/shard_map/all_gather | solution.py:263
  392.4 576.6 %copy-start.81 = (f32[2,128]{1,0:T(2,128)}, f32[2,128]{1,0:T(2,128)S(1)}, u32[]{:S(2)}) copy-start(f32[2,128]{1,0:T(2,128)S(1)} %fusion.115) | copy-start | bytes 3076
  394.2 118.1 %all-gather.35.cloned.1.call-start = ((), (), s32[]{:S(2)}) async-start(), calls=%async_computation.28 | async-start | bytes 3932160 | tf_op jit(solution)/shard_map/all_gather | solution.py:347
  438.3 8.1 copy-start.48
  448.6 136.5 %reduce-scatter.65.cloned.1.call-start = ((), (), s32[]{:S(2)}) async-start(), calls=%async_computation.49 | async-start | bytes 3932160
  514.1 24.7 %copy-start.92 = (bf16[2,384,1536]{2,1,0:T(8,128)(2,1)S(1)}, bf16[2,384,1536]{2,1,0:T(8,128)(2,1)}, u32[]{:S(2)}) copy-start(bf16[2,384,1536]{2,1,0:T(8,128)(2,1)} %all-gather.23.cloned.1.call-done) | copy-start | bytes 7077892
  542.3 89.9 %all-gather.37.cloned.1.call-start = ((), (), s32[]{:S(2)}) async-start(), calls=%async_computation.29 | async-start | bytes 3932160 | tf_op jit(solution)/shard_map/all_gather | solution.py:263
  586.9 382.2 %copy-start.79 = (f32[2,128]{1,0:T(2,128)}, f32[2,128]{1,0:T(2,128)S(1)}, u32[]{:S(2)}) copy-start(f32[2,128]{1,0:T(2,128)S(1)} %fusion.116) | copy-start | bytes 3076
  588.1 90.4 %all-gather.39.cloned.1.call-start = ((), (), s32[]{:S(2)}) async-start(), calls=%async_computation.30 | async-start | bytes 3932160 | tf_op jit(solution)/shard_map/all_gather | solution.py:263
  590.1 1.7 collective-permute-start.2
  593.7 154.3 %reduce-scatter.69.cloned.1.call-start = ((), (), s32[]{:S(2)}) async-start(), calls=%async_computation.51 | async-start | bytes 3932160
  632.3 8.3 copy-start.91
  703.9 94.0 %all-gather.41.cloned.1.call-start = ((), (), s32[]{:S(2)}) async-start(), calls=%async_computation.31 | async-start | bytes 3932160 | tf_op jit(solution)/shard_map/all_gather | solution.py:263
  751.1 218.0 %copy-start.86 = (f32[2,128]{1,0:T(2,128)}, f32[2,128]{1,0:T(2,128)S(1)}, u32[]{:S(2)}) copy-start(f32[2,128]{1,0:T(2,128)S(1)} %multiply_multiply_fusion.3) | copy-start | bytes 3076
  753.8 151.6 %reduce-scatter.37.cloned.1.call-start = ((), (), s32[]{:S(2)}) async-start(), calls=%async_computation.32 | async-start | bytes 3932160 | tf_op jit(solution)/shard_map/reduce_scatter | solution.py:378
  845.9 120.3 %reduce-scatter.71.cloned.1.call-start = ((), (), s32[]{:S(2)}) async-start(), calls=%async_computation.52 | async-start | bytes 3932160
  922.1 47.0 %copy-start.19 = (bf16[1,2,128,1536]{3,2,1,0:T(8,128)(2,1)S(1)}, bf16[1,2,128,1536]{3,2,1,0:T(8,128)(2,1)}, u32[]{:S(2)}) copy-start(bf16[1,2,128,1536]{3,2,1,0:T(8,128)(2,1)} %reduce-scatter.65.cloned.1.call-done) | copy-start | bytes 2359300
  922.1 94.5 %all-gather.43.cloned.1.call-start = ((), (), s32[]{:S(2)}) async-start(), calls=%async_computation.33 | async-start | bytes 3932160 | tf_op jit(solution)/shard_map/all_gather | solution.py:263
  972.5 112.0 %reduce-scatter.73.cloned.1.call-start = ((), (), s32[]{:S(2)}) async-start(), calls=%async_computation.53 | async-start | bytes 3932160
  1040.3 44.1 %copy-start.12 = (bf16[2,128,768]{2,1,0:T(8,128)(2,1)S(1)}, bf16[2,128,768]{2,1,0:T(8,128)(2,1)}, u32[]{:S(2)}) copy-start(bf16[2,128,768]{2,1,0:T(8,128)(2,1)} %copy-done.11) | copy-start | bytes 1179652
  1040.3 44.1 %copy-start.24 = (bf16[2,128,768]{2,1,0:T(8,128)(2,1)S(1)}, bf16[2,128,768]{2,1,0:T(8,128)(2,1)}, u32[]{:S(2)}) copy-start(bf16[2,128,768]{2,1,0:T(8,128)(2,1)} %copy-done.23) | copy-start | bytes 1179652
  1040.3 93.9 %all-gather.45.cloned.1.call-start = ((), (), s32[]{:S(2)}) async-start(), calls=%async_computation.34 | async-start | bytes 3932160 | tf_op jit(solution)/shard_map/all_gather | solution.py:263
  1090.2 157.7 %reduce-scatter.39.cloned.1.call-start = ((), (), s32[]{:S(2)}) async-start(), calls=%async_computation.35 | async-start | bytes 3932160 | tf_op jit(solution)/shard_map/reduce_scatter | solution.py:378
  1181.4 96.1 %reduce-scatter.59.cloned.1.call-start = ((), (), s32[]{:S(2)}) async-start(), calls=%async_computation.45 | async-start | bytes 4718592 | tf_op jit(solution)/shard_map/reduce_scatter | solution.py:358
  1189.4 88.1 %reduce-scatter.51.cloned.1.call-start = ((), (), s32[]{:S(2)}) async-start(), calls=%async_computation.41 | async-start | bytes 4718592 | tf_op jit(solution)/shard_map/reduce_scatter | solution.py:358
  1197.1 85.9 %reduce-scatter.55.cloned.1.call-start = ((), (), s32[]{:S(2)}) async-start(), calls=%async_computation.43 | async-start | bytes 4718592 | tf_op jit(solution)/shard_map/reduce_scatter | solution.py:358
  1204.9 90.8 %reduce-scatter.47.cloned.1.call-start = ((), (), s32[]{:S(2)}) async-start(), calls=%async_computation.39 | async-start | bytes 1769472 | tf_op jit(solution)/shard_map/reduce_scatter | solution.py:358
  1209.4 100.2 %reduce-scatter.43.cloned.1.call-start = ((), (), s32[]{:S(2)}) async-start(), calls=%async_computation.37 | async-start | bytes 3538944 | tf_op jit(solution)/shard_map/reduce_scatter | solution.py:358
  1215.9 108.2 %reduce-scatter.57.cloned.1.call-start = ((), (), s32[]{:S(2)}) async-start(), calls=%async_computation.44 | async-start | bytes 4718592 | tf_op jit(solution)/shard_map/reduce_scatter | solution.py:358
  1224.3 114.0 %reduce-scatter.49.cloned.1.call-start = ((), (), s32[]{:S(2)}) async-start(), calls=%async_computation.40 | async-start | bytes 4718592 | tf_op jit(solution)/shard_map/reduce_scatter | solution.py:358
  1232.7 120.0 %reduce-scatter.53.cloned.1.call-start = ((), (), s32[]{:S(2)}) async-start(), calls=%async_computation.42 | async-start | bytes 4718592 | tf_op jit(solution)/shard_map/reduce_scatter | solution.py:358
  1241.0 124.4 %reduce-scatter.45.cloned.1.call-start = ((), (), s32[]{:S(2)}) async-start(), calls=%async_computation.38 | async-start | bytes 1769472 | tf_op jit(solution)/shard_map/reduce_scatter | solution.py:358
  1246.4 132.8 %reduce-scatter.41.cloned.1.call-start = ((), (), s32[]{:S(2)}) async-start(), calls=%async_computation.36 | async-start | bytes 3538944 | tf_op jit(solution)/shard_map/reduce_scatter | solution.py:358
  1261.3 166.7 %reduce-scatter.67.cloned.1.call-start = ((), (), s32[]{:S(2)}) async-start(), calls=%async_computation.50 | async-start | bytes 3932160
  1270.4 205.1 %reduce-scatter.75.cloned.1.call-start = ((), (), s32[]{:S(2)}) async-start(), calls=%async_computation.54 | async-start | bytes 3932160
  1277.4 648.0 %all-reduce.13.cloned.1.call-start = ((), (), s32[]{:S(2)}) async-start(), calls=%async_computation.55 | async-start | bytes 25952256 | tf_op jit(solution)/shard_map/psum | solution.py:359
  1379.2 48.7 %copy-start.20 = (bf16[1,2,128,1536]{3,2,1,0:T(8,128)(2,1)S(1)}, bf16[1,2,128,1536]{3,2,1,0:T(8,128)(2,1)}, u32[]{:S(2)}) copy-start(bf16[1,2,128,1536]{3,2,1,0:T(8,128)(2,1)} %reduce-scatter.65.cloned.1.call-done) | copy-start | bytes 2359300
  1379.2 48.7 %copy-start.21 = (bf16[2,128,1536]{2,1,0:T(8,128)(2,1)S(1)}, bf16[2,128,1536]{2,1,0:T(8,128)(2,1)}, u32[]{:S(2)}) copy-start(bf16[2,128,1536]{2,1,0:T(8,128)(2,1)} %get-tuple-element.89) | copy-start | bytes 2359300
  1429.4 46.1 %copy-start.13 = (bf16[2,128,768]{2,1,0:T(8,128)(2,1)S(1)}, bf16[2,128,768]{2,1,0:T(8,128)(2,1)}, u32[]{:S(2)}) copy-start(bf16[2,128,768]{2,1,0:T(8,128)(2,1)} %copy-done.11) | copy-start | bytes 1179652
  1429.4 46.1 %copy-start.25 = (bf16[2,128,768]{2,1,0:T(8,128)(2,1)S(1)}, bf16[2,128,768]{2,1,0:T(8,128)(2,1)}, u32[]{:S(2)}) copy-start(bf16[2,128,768]{2,1,0:T(8,128)(2,1)} %copy-done.23) | copy-start | bytes 1179652
  1429.4 48.7 %copy-start.16 = (bf16[1,2,128,1536]{3,2,1,0:T(8,128)(2,1)S(1)}, bf16[1,2,128,1536]{3,2,1,0:T(8,128)(2,1)}, u32[]{:S(2)}) copy-start(bf16[1,2,128,1536]{3,2,1,0:T(8,128)(2,1)} %reduce-scatter.61.cloned.1.call-done) | copy-start | bytes 2359300
  1429.4 48.7 %copy-start.57 = (bf16[2,128,768]{2,1,0:T(8,128)(2,1)S(1)}, bf16[2,128,768]{2,1,0:T(8,128)(2,1)}, u32[]{:S(2)}) copy-start(bf16[2,128,768]{2,1,0:T(8,128)(2,1)} %get-tuple-element.113) | copy-start | bytes 1179652
  1430.4 2.1 collective-permute-start.1
  1483.0 46.0 %collective-permute-start.3 = (bf16[2,128,768]{2,1,0:T(8,128)(2,1)S(1)}, bf16[2,128,768]{2,1,0:T(8,128)(2,1)S(1)}, u32[]{:S(2)}, u32[]{:S(2)}) collective-permute-start(bf16[2,128,768]{2,1,0:T(8,128)(2,1)S(1)} %select_convert_fusion), channel_id=1, source_target_pairs={{0,16},{16,0},{1,17},{17,1},{2,18},{18,2},{3,19},{19,3},{4,20},{20... | collective-permute-start | bytes 1179656 | tf_op jit(solution)/shard_map/ppermute | solution.py:259
  1926.9 9.3 collective-permute-start.5
  1927.6 10.3 collective-permute-start.4
  1930.6 19.9 %collective-permute-start.6 = (bf16[768,1024]{1,0:T(8,128)(2,1)}, bf16[768,1024]{1,0:T(8,128)(2,1)}, u32[]{:S(2)}, u32[]{:S(2)}) collective-permute-start(bf16[768,1024]{1,0:T(8,128)(2,1)} %get-tuple-element.104), channel_id=1, source_target_pairs={{0,16},{16,0},{1,17},{17,1},{2,18},{18,2},{3,19},{19,3},{4,20},{20... | collective-permute-start | bytes 4718600 | tf_op jit(solution)/shard_map/ppermute | solution.py:259
  1933.1 22.2 %collective-permute-start.7 = (bf16[768,1024]{1,0:T(8,128)(2,1)}, bf16[768,1024]{1,0:T(8,128)(2,1)}, u32[]{:S(2)}, u32[]{:S(2)}) collective-permute-start(bf16[768,1024]{1,0:T(8,128)(2,1)} %get-tuple-element.102), channel_id=1, source_target_pairs={{0,16},{16,0},{1,17},{17,1},{2,18},{18,2},{3,19},{19,3},{4,20},{20... | collective-permute-start | bytes 4718600 | tf_op jit(solution)/shard_map/ppermute | solution.py:259
  1936.1 24.0 %collective-permute-start.8 = (bf16[512,1536]{1,0:T(8,128)(2,1)}, bf16[512,1536]{1,0:T(8,128)(2,1)}, u32[]{:S(2)}, u32[]{:S(2)}) collective-permute-start(bf16[512,1536]{1,0:T(8,128)(2,1)} %get-tuple-element.100), channel_id=1, source_target_pairs={{0,16},{16,0},{1,17},{17,1},{2,18},{18,2},{3,19},{19,3},{4,20},{20... | collective-permute-start | bytes 4718600 | tf_op jit(solution)/shard_map/ppermute | solution.py:259
  (83 other events, 287.4 us)
Sparse Core Ops, SparseCore 0:
  13.2 46.4 all-gather.18
  61.8 21.8 all-gather.46
  94.1 64.6 all-gather.20
  160.2 9.6 all-gather.22
  190.6 42.5 reduce-scatter.60
  234.6 16.7 all-gather.26
  253.8 45.1 all-gather.24
  300.5 16.7 all-gather.28
  318.9 17.9 all-gather.30
  344.6 45.1 reduce-scatter.62
  394.3 43.9 all-gather.32
  448.7 63.4 all-gather.34
  542.5 42.5 reduce-scatter.64
  588.3 43.9 all-gather.36
  634.5 43.9 all-gather.38
  704.0 43.9 reduce-scatter.68
  753.9 43.9 all-gather.40
  846.1 59.2 reduce-scatter.36
  922.2 44.0 reduce-scatter.70
  972.6 43.9 all-gather.42
  1040.4 43.9 reduce-scatter.72
  1090.3 43.9 all-gather.44
  1181.5 59.2 reduce-scatter.38
  1243.0 10.9 reduce-scatter.58
  1256.8 12.0 reduce-scatter.50
  1271.0 12.0 reduce-scatter.54
  1285.8 9.8 reduce-scatter.46
  1298.5 11.1 reduce-scatter.42
  1312.0 12.0 reduce-scatter.56
  1326.2 12.0 reduce-scatter.48
  1340.6 12.0 reduce-scatter.52
  1355.5 9.7 reduce-scatter.44
  1368.1 11.0 reduce-scatter.40
  1382.8 45.1 reduce-scatter.66
  1431.5 43.9 reduce-scatter.74
  1479.3 446.1 all-reduce.12

commit v2 on v1

--- a/solution.py
+++ b/solution.py
@@ -1,3 +1,5 @@
+import functools
+
 import jax
 import jax.numpy as jnp
 import numpy as np
@@ -236,12 +238,289 @@
     )(order, own, q, kv, do, mixt, lse, cos_t, sin_t)
 
 
-def rms_norm(v, gain):
-    return v * lax.rsqrt(jnp.mean(v * v, axis=-1, keepdims=True) + EPSILON) * gain
-
-
 def silu_product(gate, up):
     return gate * jax.nn.sigmoid(gate) * up
+
+
+MESH = pl.DeviceIdType.MESH
+
+
+def tensor_peers():
+    t = lax.axis_index("tensor")
+    return t, t + 1 - 2 * lax.rem(t, 2), lax.rem(t + 2, 4), 3 - t
+
+
+def greet(*peers):
+    barrier = pltpu.get_barrier_semaphore()
+    for peer in peers:
+        pl.semaphore_signal(barrier, inc=1, device_id={"tensor": peer}, device_id_type=MESH)
+    pl.semaphore_wait(barrier, len(peers))
+
+
+def send(src, dst, sems, at, peer):
+    return pltpu.make_async_remote_copy(
+        src_ref=src,
+        dst_ref=dst,
+        send_sem=sems[0].at[at],
+        recv_sem=sems[1].at[at],
+        device_id={"tensor": peer},
+        device_id_type=MESH,
+    )
+
+
+def gather_start(full, sems, chunks, q):
+    t, x, y, _ = tensor_peers()
+    j, at = chunks[q]
+    near, far = (x, y) if j == 0 else (y, x)
+    own = full.at[t, j, at]
+    send(own, own, sems, (q, 0), near).start()
+    send(own, own, sems, (q, 1), far).start()
+
+
+def gather_pass(full, sems, chunks, q):
+    _, x, y, _ = tensor_peers()
+    j, at = chunks[q]
+    near, far = (x, y) if j == 0 else (y, x)
+    got = full.at[near, j, at]
+    send(got, got, sems, (q, 0), near).wait_recv()
+    send(got, got, sems, (q, 2), far).start()
+
+
+def gather_end(full, sems, chunks, q):
+    t, x, y, diag = tensor_peers()
+    j, at = chunks[q]
+    near, far = (x, y) if j == 0 else (y, x)
+    for kind, owner in ((1, far), (2, diag)):
+        got = full.at[owner, j, at]
+        send(got, got, sems, (q, kind), far).wait_recv()
+
+
+def gather_drain(full, sems, chunks, q):
+    t, x, _, _ = tensor_peers()
+    j, at = chunks[q]
+    own = full.at[t, j, at]
+    for kind in range(3):
+        send(own, own, sems, (q, kind), x).wait_send()
+
+
+def scatter_start(part, got, sems, chunks, q):
+    _, x, y, diag = tensor_peers()
+    j, at = chunks[q]
+    far = y if j == 0 else x
+    send(part.at[diag, j, at], got.at[0, j, at], sems, (q, 0), far).start()
+    send(part.at[far, j, at], got.at[2, j, at], sems, (q, 2), far).start()
+
+
+def scatter_pass(part, got, held, sems, chunks, q):
+    _, x, y, _ = tensor_peers()
+    j, at = chunks[q]
+    near = x if j == 0 else y
+    send(held.at[j, at], got.at[0, j, at], sems, (q, 0), near).wait_recv()
+    held[j, at] = (part[near, j, at].astype(F32) + got[0, j, at].astype(F32)).astype(BF)
+    send(held.at[j, at], got.at[1, j, at], sems, (q, 1), near).start()
+
+
+def scatter_end(part, got, held, sems, chunks, q):
+    t, x, _, _ = tensor_peers()
+    j, at = chunks[q]
+    for kind in (2, 1):
+        send(held.at[j, at], got.at[kind, j, at], sems, (q, kind), x).wait_recv()
+    return (
+        part[t, j, at].astype(F32) + got[1, j, at].astype(F32) + got[2, j, at].astype(F32)
+    )
+
+
+def scatter_drain(part, got, sems, chunks, q):
+    t, x, _, _ = tensor_peers()
+    j, at = chunks[q]
+    for kind in range(3):
+        send(part.at[t, j, at], got.at[kind, j, at], sems, (q, kind), x).wait_send()
+
+
+def inverse_rms(v):
+    return lax.rsqrt(jnp.mean(v * v, axis=-1, keepdims=True) + EPSILON)
+
+
+def norm_back(v, gain, dn):
+    r = inverse_rms(v)
+    unit = v * r
+    scaled = dn * gain
+    dv = r * (scaled - unit * jnp.mean(scaled * unit, axis=-1, keepdims=True))
+    return dv, jnp.sum(dn * unit, axis=0, keepdims=True)
+
+
+def chunk_list(sp):
+    parts = 2
+    size = sp // parts
+    return [(j, pl.ds(s * size, size)) for s in range(parts) for j in range(2)]
+
+
+def run_exchange(sp, part, finish, full, got, held, sc_sems, ga_sems):
+    chunks = chunk_list(sp)
+    n = range(len(chunks))
+    _, x, y, _ = tensor_peers()
+    greet(x, y)
+    if part is not None:
+        for q in n:
+            scatter_start(part, got, sc_sems, chunks, q)
+        for q in n:
+            scatter_pass(part, got, held, sc_sems, chunks, q)
+    for q in n:
+        j, at = chunks[q]
+        total = None if part is None else scatter_end(part, got, held, sc_sems, chunks, q)
+        finish(j, at, total)
+        if full is not None:
+            gather_start(full, ga_sems, chunks, q)
+    if full is not None:
+        for q in n:
+            gather_pass(full, ga_sems, chunks, q)
+        for q in n:
+            gather_end(full, ga_sems, chunks, q)
+        for q in n:
+            gather_drain(full, ga_sems, chunks, q)
+    if part is not None:
+        for q in n:
+            scatter_drain(part, got, sc_sems, chunks, q)
+
+
+def scatter_scratch(sp, d):
+    n = len(chunk_list(sp))
+    return [
+        pltpu.VMEM((3, 2, sp, d), BF),
+        pltpu.VMEM((2, sp, d), BF),
+        pltpu.SemaphoreType.DMA((n, 3)),
+        pltpu.SemaphoreType.DMA((n, 3)),
+    ]
+
+
+def gather_scratch(sp):
+    n = len(chunk_list(sp))
+    return [pltpu.SemaphoreType.DMA((n, 3)), pltpu.SemaphoreType.DMA((n, 3))]
+
+
+def call(kernel, out_shape, scratch, ident, *operands):
+    vm = pl.BlockSpec(memory_space=pltpu.VMEM)
+    return pl.pallas_call(
+        kernel,
+        out_shape=out_shape,
+        in_specs=[vm] * len(operands),
+        out_specs=(vm,) * len(out_shape),
+        scratch_shapes=scratch,
+        compiler_params=pltpu.CompilerParams(
+            collective_id=ident, has_side_effects=True, vmem_limit_bytes=50 * 2**20
+        ),
+    )(*operands)
+
+
+def shapes_of(h):
+    _, sp, d = h.shape
+    return (
+        jax.ShapeDtypeStruct((2, sp, d), F32),
+        jax.ShapeDtypeStruct((4, 2, sp, d), BF),
+        jax.ShapeDtypeStruct((1, d), F32),
+        jax.ShapeDtypeStruct((2, sp, d), BF),
+    )
+
+
+def norm_gather_kernel(h, gain, full, *sems):
+    t = lax.axis_index("tensor")
+
+    def finish(j, at, _):
+        v = h[j, at].astype(F32)
+        full[t, j, at] = (v * inverse_rms(v) * gain[...]).astype(BF)
+
+    run_exchange(h.shape[1], None, finish, full, None, None, None, sems)
+
+
+def norm_gather(h, gain):
+    _, full, _, _ = shapes_of(h)
+    return call(norm_gather_kernel, (full,), gather_scratch(h.shape[1]), 0, h, gain)[0]
+
+
+def plain_gather_kernel(h, full, *sems):
+    t = lax.axis_index("tensor")
+
+    def finish(j, at, _):
+        full[t, j, at] = h[j, at]
+
+    run_exchange(h.shape[1], None, finish, full, None, None, None, sems)
+
+
+def plain_gather(h):
+    _, full, _, _ = shapes_of(h)
+    return call(plain_gather_kernel, (full,), gather_scratch(h.shape[1]), 1, h)[0]
+
+
+def sum_norm_gather_kernel(rounded, part, h, gain, total, full, got, held, s0, s1, g0, g1):
+    t = lax.axis_index("tensor")
+
+    def finish(j, at, term):
+        v = h[j, at] + term
+        if rounded:
+            v = v.astype(BF).astype(F32)
+        total[j, at] = v
+        full[t, j, at] = (v * inverse_rms(v) * gain[...]).astype(BF)
+
+    run_exchange(h.shape[1], part, finish, full, got, held, (s0, s1), (g0, g1))
+
+
+def sum_norm_gather(part, h, gain, rounded):
+    wide, full, _, _ = shapes_of(h)
+    _, sp, d = h.shape
+    return call(
+        functools.partial(sum_norm_gather_kernel, rounded),
+        (wide, full),
+        scatter_scratch(sp, d) + gather_scratch(sp),
+        2 + rounded,
+        part, h, gain,
+    )
+
+
+def sum_only_kernel(part, h, total, got, held, s0, s1):
+    def finish(j, at, term):
+        total[j, at] = (h[j, at] + term).astype(BF)
+
+    run_exchange(h.shape[1], part, finish, None, got, held, (s0, s1), None)
+
+
+def sum_only(part, h):
+    _, _, _, narrow = shapes_of(h)
+    _, sp, d = h.shape
+    return call(sum_only_kernel, (narrow,), scatter_scratch(sp, d), 4, part, h)[0]
+
+
+def back_kernel(kind, part, h, gain, g, *refs):
+    t = lax.axis_index("tensor")
+    if kind == 2:
+        dv_out, dgain, got, held, s0, s1 = refs
+        full = ga = None
+    else:
+        dv_out, dgain, full, got, held, s0, s1, g0, g1 = refs
+        ga = (g0, g1)
+    dgain[...] = jnp.zeros_like(dgain)
+
+    def finish(j, at, term):
+        dv, dg = norm_back(h[j, at], gain[...], term)
+        dgain[...] += dg
+        dv = dv + g[j, at].astype(F32)
+        dv_out[j, at] = dv.astype(dv_out.dtype)
+        if full is not None:
+            full[t, j, at] = dv.astype(BF)
+
+    run_exchange(h.shape[1], part, finish, full, got, held, (s0, s1), ga)
+
+
+def back(part, h, gain, g, kind):
+    wide, full, row, narrow = shapes_of(h)
+    _, sp, d = h.shape
+    out = (narrow if kind == 1 else wide, row)
+    scratch = scatter_scratch(sp, d)
+    if kind != 2:
+        out += (full,)
+        scratch += gather_scratch(sp)
+    return call(
+        functools.partial(back_kernel, kind), out, scratch, 5 + kind, part, h, gain, g
+    )
 
 
 def turn_matrix(heads, total):
@@ -257,14 +536,6 @@
 
 def swap(value):
     return lax.ppermute(value, "section", [(0, 1), (1, 0)])
-
-
-def gather_rows(x):
-    return lax.all_gather(x, "tensor", axis=0)
-
-
-def scatter_rows(x):
-    return lax.psum_scatter(x.astype(BF), "tensor", scatter_dimension=0).astype(F32)
 
 
 def on_device(
@@ -338,39 +609,35 @@
     cos_all = jnp.concatenate([jnp.tile(cos_r, (1, q_heads)), cos_kv], 1)
     sin_all = jnp.concatenate([jnp.tile(sin_r, (1, q_heads)), sin_kv], 1)
 
-    def forward(h, layer):
-        a_gain, m_gain = gains2[layer, 0], gains2[layer, 1]
-        n1 = gather_rows(rms_norm(h, a_gain).astype(BF)).reshape(rows, d)
+    def gain_of(layer, kind):
+        return gains2[layer, kind : kind + 1]
+
+    def attend(n1, layer):
         raw = nn(n1, wcat2[layer])
         qkv = (raw[:, :qkv_w] * cos_all + raw[:, qkv_w:] * sin_all).astype(BF)
         q = qkv[:, :q_w].reshape(n_t, 2, sp, q_w)
         kv = lax.all_gather(qkv[:, q_w:].reshape(n_t, 2, sp, kv_w), "ctx", axis=0)
         mix, mixt, lse = flash_forward(block_order, own, q, kv)
-        part = nn(mix.reshape(rows, q_w), wo2[layer])
-        h2 = h + scatter_rows(part.reshape(n_t, 2, sp, d))
-        n2 = gather_rows(rms_norm(h2, m_gain).astype(BF)).reshape(rows, d)
+        part = nn(mix.reshape(rows, q_w), wo2[layer]).astype(BF)
+        return part.reshape(n_t, 2, sp, d), (q, kv, mix.reshape(rows, q_w), mixt, lse)
+
+    def feed(n2, layer):
         gate, up = nn(n2, wg2[layer]), nn(n2, wu2[layer])
         act = silu_product(gate, up).astype(BF)
-        out = h2 + scatter_rows(nn(act, wd2[layer]).reshape(n_t, 2, sp, d))
-        return out, (h, n1, q, kv, mix, mixt, lse, h2, n2, gate, up, act)
-
-    def reduce_grad(g):
-        g = lax.psum_scatter(g.astype(BF), "section", scatter_dimension=0, tiled=True)
-        return lax.psum(g, "ctx")
-
-    def backward(g, gm, layer, kept):
-        h, n1, q, kv, mix, mixt, lse, h2, n2, gate, up, act = kept
-        a_gain, m_gain = gains2[layer, 0], gains2[layer, 1]
-        gm = gather_rows(gm).reshape(rows, d)
+        part = nn(act, wd2[layer]).astype(BF)
+        return part.reshape(n_t, 2, sp, d), (gate, up, act)
+
+    def feed_back(gm, layer, kept):
+        gate, up, _ = kept
         dact = nt(gm, wd2[layer])
         _, pull = jax.vjp(silu_product, gate, up)
         dgate, dup = pull(dact)
         dgate, dup = dgate.astype(BF), dup.astype(BF)
-        dn2 = scatter_rows((nt(dgate, wg2[layer]) + nt(dup, wu2[layer])).reshape(n_t, 2, sp, d))
-        _, pull = jax.vjp(rms_norm, h2, m_gain)
-        dh2, d_mg = pull(dn2)
-        dh2 = g + dh2
-        ga = gather_rows(dh2.astype(BF)).reshape(rows, d)
+        part = (nt(dgate, wg2[layer]) + nt(dup, wu2[layer])).astype(BF)
+        return part.reshape(n_t, 2, sp, d), dgate, dup
+
+    def attend_back(ga, layer, kept):
+        q, kv, _, mixt, lse = kept
         dmix = nt(ga, wo2[layer]).astype(BF)
         dq, dkv = flash_backward(
             block_order, own, q, kv, dmix.reshape(n_t, 2, sp, q_w), mixt, lse, cos_t, sin_t
@@ -385,26 +652,58 @@
         )
         dkv = (dkv * cos_kv + turned).astype(BF)
         dqkv = jnp.concatenate([dq.reshape(rows, q_w), dkv], 1)
-        dn1 = scatter_rows(nt(dqkv, wcat2[layer][:, :qkv_w]).reshape(n_t, 2, sp, d))
-        _, pull = jax.vjp(rms_norm, h, a_gain)
-        dh, d_ag = pull(dn1)
-        dh = dh2 + dh
-        grads = (
-            reduce_grad(tn(act, gm)),
-            reduce_grad(tn(n2, dgate)),
-            reduce_grad(tn(n2, dup)),
-            reduce_grad(tn(mix.reshape(rows, q_w), ga)),
-            reduce_grad(tn(n1, dqkv)),
-        )
-        return dh, (d_ag, d_mg), grads
-
-    out0, kept0 = forward(x_own.astype(F32), 0)
-    y, kept1 = forward(out0.astype(BF).astype(F32), 1)
-    dh1, gains1, grads1 = backward(g_own.astype(F32), g_own, 1, kept1)
-    g0 = dh1.astype(BF)
-    dh0, gains0, grads0 = backward(g0.astype(F32), g0, 0, kept0)
-
-    gain_sum = lax.psum(jnp.stack([jnp.stack(gains0), jnp.stack(gains1)]), ("section", "ctx", "tensor"))
+        part = nt(dqkv, wcat2[layer][:, :qkv_w]).astype(BF)
+        return part.reshape(n_t, 2, sp, d), dqkv
+
+    def halve(g):
+        size = g.shape[0] // 2
+        give = lax.dynamic_slice_in_dim(g, (1 - sec) * size, size, 0).astype(BF)
+        keep = lax.dynamic_slice_in_dim(g, sec * size, size, 0)
+        return (keep + swap(give).astype(F32)).astype(BF)
+
+    def over_ctx(*grads, after=None):
+        halves = tuple(halve(g) for g in grads)
+        if after is not None:
+            halves, _ = lax.optimization_barrier((halves, after))
+        return lax.psum(halves, "ctx")
+
+    flat = lambda v: v.reshape(rows, d)
+    a0, a1, m0, m1 = gain_of(0, 0), gain_of(1, 0), gain_of(0, 1), gain_of(1, 1)
+
+    h0 = x_own.astype(F32)
+    n1_0 = flat(norm_gather(x_own, a0))
+    part, att0 = attend(n1_0, 0)
+    h2_0, full = sum_norm_gather(part, h0, m0, False)
+    n2_0 = flat(full)
+    part, mlp0 = feed(n2_0, 0)
+    h1, full = sum_norm_gather(part, h2_0, a1, True)
+    n1_1 = flat(full)
+    part, att1 = attend(n1_1, 1)
+    h2_1, full = sum_norm_gather(part, h1, m1, False)
+    n2_1 = flat(full)
+    part, mlp1 = feed(n2_1, 1)
+    y = sum_only(part, h2_1)
+
+    gm1 = flat(plain_gather(g_own))
+    part, dgate1, dup1 = feed_back(gm1, 1, mlp1)
+    dh2_1, dm1, full = back(part, h2_1, m1, g_own.astype(F32), 0)
+    ga1 = flat(full)
+    part, dqkv1 = attend_back(ga1, 1, att1)
+    g0, da1, full = back(part, h1, a1, dh2_1, 1)
+    gm0 = flat(full)
+    grads1 = over_ctx(
+        tn(mlp1[2], gm1), tn(n2_1, dgate1), tn(n2_1, dup1), tn(att1[2], ga1), tn(n1_1, dqkv1)
+    )
+    part, dgate0, dup0 = feed_back(gm0, 0, mlp0)
+    dh2_0, dm0, full = back(part, h2_0, m0, g0.astype(F32), 0)
+    ga0 = flat(full)
+    grads0 = over_ctx(tn(mlp0[2], gm0), tn(n2_0, dgate0), tn(n2_0, dup0), after=grads1)
+    part, dqkv0 = attend_back(ga0, 0, att0)
+    dh0, da0 = back(part, h0, a0, dh2_0, 2)
+    grads0 += over_ctx(tn(att0[2], ga0), tn(n1_0, dqkv0), after=grads0)
+    gains0, gains1 = (da0, dm0), (da1, dm1)
+
+    gain_sum = lax.psum(jnp.stack([jnp.concatenate(gains0), jnp.concatenate(gains1)]), ("section", "ctx", "tensor"))
     gain_own = lax.dynamic_index_in_dim(gain_sum, sec, 0, keepdims=False)
 
     def to_owner(r0, r1):

time: 1980 us -> 1300 us (0.66)
  waiting for transfers between devices: 1400 us -> 293 us
  Pallas kernels: 134 us -> 598 us
  matrix products: 218 us -> 191 us
    pallas_call x0 -> x10, Pallas kernels: none -> 467 us  [call(): pl.pallas_call(kernel, out_shape=out_shape, in_specs=[vm] * len(operands)...]
    all_gather x10 -> x2, waiting for transfers between devices: 439 us -> 88.8 us  [attend(): kv = lax.all_gather(qkv[:, q_w:].reshape(n_t, 2, sp, kv_w), 'ctx', axis=0)]
    unnamed x44 -> x12, waiting for transfers between devices: 352 us -> 2.39 us
    psum x1 -> x3, waiting for transfers between devices: 395 us -> 161 us  [over_ctx(): return lax.psum(halves, 'ctx')]
    reduce_scatter x12 -> x2, waiting for transfers between devices: 159 us -> 39.4 us  [attend_back(): lax.psum_scatter(dkv, 'ctx', scatter_dimension=0).astype(F32)]
    all_gather x5, waiting for transfers between devices: 55 us -> 0.01 us  [both(): return lax.all_gather(w, 'section', axis=0)]
    dot_general x10, matrix products: 62 us -> 39.1 us  [tn(): lax.dot_general(a, b, (((0,), (0,)), ((), ())), preferred_element_type=F32)]
    unnamed x210 -> x238, local copies, waits for them, and re-layouts: 35 us -> 41.4 us
  transfers between devices with their start and end apart: 45 -> 31, of which waited for: 34 -> 8; matrix products, arithmetic and copies ran while one was open for 10% -> 17% of each run, Pallas kernels for 1% -> 28%
where the time goes in v2:
time: 1300 us; the launch traced here: 1290 us
  Pallas kernels  598 us (46%)
  waiting for transfers between devices  293 us (23%)
  matrix products  191 us (15%)
  local copies, waits for them, and re-layouts  80.1 us (6%)
  other arithmetic  66.5 us (5%)
  blocking collectives  44.7 us (3%)
  between operations  16 us (1%)
    pallas_call x10, Pallas kernels, call(): pl.pallas_call(kernel, out_shape=out_shape, in_specs=[vm] * len(operands)...  467 us
    psum x3, waiting for transfers between devices, over_ctx(): return lax.psum(halves, 'ctx')  161 us
    all_gather x2, waiting for transfers between devices, attend(): kv = lax.all_gather(qkv[:, q_w:].reshape(n_t, 2, sp, kv_w), 'ctx', axis=0)  88.8 us
    pallas_call x2, Pallas kernels, flash_backward(): pl.pallas_call(bwd_kernel, out_shape=(jax.ShapeDtypeStruct(q.shape, BF),...  82.6 us
    dot_general x13, matrix products, nn(): lax.dot_general(a, b, (((1,), (0,)), ((), ())), preferred_element_type=F32)  78.9 us
    dot_general x10, matrix products, nt(): lax.dot_general(a, b, (((1,), (1,)), ((), ())), preferred_element_type=F32)  62.8 us
    pallas_call x2, Pallas kernels, flash_forward(): pl.pallas_call(fwd_kernel, out_shape=(jax.ShapeDtypeStruct(q.shape, BF),...  48.2 us
    psum x1, blocking collectives, on_device(): lax.psum(jnp.stack([jnp.concatenate(gains0), jnp.concatenate(gains1)]), (...  42.9 us
  transfers between devices with their start and end apart: 31, of which 8 were waited for; matrix products, arithmetic and copies ran while one was open for 17% of the time, Pallas kernels for 28%

profile of v2, /device:TPU:0, one launch (start us, length us, event | category | flops | bytes accessed | tf_op | source)
XLA Modules:
  0.0 1293.7 jit_solution(18385704405638745851)
XLA Ops:
  31.9 3.0 copy.53
  39.0 31.1 %shard_map.239 = bf16[4,2,128,1536]{3,2,1,0:T(8,128)(2,1)S(1)} custom-call(bf16[2,128,1536]{2,1,0:T(8,128)(2,1)S(1)} %get-tuple-element.121.h, f32[1,1536]{1,0:T(1,128)S(1)} %get-tuple-element.160.gain), custom_call_target="tpu_custom_call" | custom-call | tf_op jit(solution)/shard_map/pallas_call | solution.py:403
  71.8 8.0 fusion.2
  85.1 60.9 %all-gather.11.cloned.1.call-done.kv_ref = bf16[4,4,2,128,384]{4,3,2,1,0:T(8,128)(2,1)} async-done(((bf16[1,4,2,128,384]{4,3,2,1,0:T(8,128)(2,1)}), bf16[4,4,2,128,384]{4,3,2,1,0:T(8,128)(2,1)}) %all-gather.11.cloned.1.call-update) | async-done | bytes 3145744 | tf_op jit(solution)/shard_map/all_gather | solution.py:619
  149.3 24.0 %shard_map.240 = (bf16[4,2,128,384]{3,2,1,0:T(8,128)(2,1)S(1)}, bf16[2,4,96,512]{3,2,1,0:T(8,128)(2,1)S(1)}, f32[2,4,1,512]{3,2,1,0:T(1,128)S(1)}) custom-call(s32[8]{0:T(128)S(1)} %copy-done.34, s32[2]{0:T(128)S(1)} %copy-done.38, bf16[4,2,128,384]{3,2,1,0:T(8,128)(2,1)S(1)} %bitcast.213, bf16[4,4,2,128,384]{4,3,2,1,0:T(8,128)(2,1)S(1)} %copy-done), custom_call_target="tpu_custom_call" | custom-call | tf_op jit(solution)/shard_map/pallas_call | solution.py:113
  174.8 5.0 convolution_convert_fusion.3
  179.8 57.9 %shard_map.241 = (f32[2,128,1536]{2,1,0:T(8,128)S(1)}, bf16[4,2,128,1536]{3,2,1,0:T(8,128)(2,1)}) custom-call(bf16[4,2,128,1536]{3,2,1,0:T(8,128)(2,1)} %bitcast.248, f32[2,128,1536]{2,1,0:T(8,128)S(1)} %get-tuple-element.120.h, f32[1,1536]{1,0:T(1,128)S(1)} %get-tuple-element.159.gain), custom_call_target="tpu_custom_call" | custom-call | tf_op jit(solution)/shard_map/pallas_call | solution.py:403
  238.9 8.2 fusion.21
  247.1 10.4 multiply_convert_fusion.3
  257.5 7.7 convolution_convert_fusion.5
  265.2 56.1 %shard_map.242 = (f32[2,128,1536]{2,1,0:T(8,128)S(1)}, bf16[4,2,128,1536]{3,2,1,0:T(8,128)(2,1)}) custom-call(bf16[4,2,128,1536]{3,2,1,0:T(8,128)(2,1)} %bitcast.249, f32[2,128,1536]{2,1,0:T(8,128)S(1)} %copy-done.3, f32[1,1536]{1,0:T(1,128)S(1)} %get-tuple-element.158.gain), custom_call_target="tpu_custom_call" | custom-call | tf_op jit(solution)/shard_map/pallas_call | solution.py:403
  321.3 8.5 fusion
  336.6 28.3 %shard_map.246 = bf16[4,2,128,1536]{3,2,1,0:T(8,128)(2,1)S(1)} custom-call(bf16[2,128,1536]{2,1,0:T(8,128)(2,1)S(1)} %get-tuple-element.119.h), custom_call_target="tpu_custom_call" | custom-call | tf_op jit(solution)/shard_map/pallas_call | solution.py:403
  366.5 27.8 %all-gather.21.cloned.1.call-done.kv_ref = bf16[4,4,2,128,384]{4,3,2,1,0:T(8,128)(2,1)} async-done(((bf16[1,4,2,128,384]{4,3,2,1,0:T(8,128)(2,1)}), bf16[4,4,2,128,384]{4,3,2,1,0:T(8,128)(2,1)}) %all-gather.21.cloned.1.call-update) | async-done | bytes 3145744 | tf_op jit(solution)/shard_map/all_gather | solution.py:619
  397.6 24.2 %shard_map.243 = (bf16[4,2,128,384]{3,2,1,0:T(8,128)(2,1)S(1)}, bf16[2,4,96,512]{3,2,1,0:T(8,128)(2,1)S(1)}, f32[2,4,1,512]{3,2,1,0:T(1,128)S(1)}) custom-call(s32[8]{0:T(128)S(1)} %copy-done.35, s32[2]{0:T(128)S(1)} %copy-done.39, bf16[4,2,128,384]{3,2,1,0:T(8,128)(2,1)S(1)} %bitcast.215, bf16[4,4,2,128,384]{4,3,2,1,0:T(8,128)(2,1)S(1)} %copy-done.1), custom_call_target="tpu_custom_call" | custom-call | tf_op jit(solution)/shard_map/pallas_call | solution.py:113
  421.9 3.5 convolution_convert_fusion.2
  425.3 57.9 %shard_map.244 = (f32[2,128,1536]{2,1,0:T(8,128)S(1)}, bf16[4,2,128,1536]{3,2,1,0:T(8,128)(2,1)}) custom-call(bf16[4,2,128,1536]{3,2,1,0:T(8,128)(2,1)} %bitcast.247, f32[2,128,1536]{2,1,0:T(8,128)S(1)} %copy-done.6, f32[1,1536]{1,0:T(1,128)S(1)} %copy-done.30), custom_call_target="tpu_custom_call" | custom-call | tf_op jit(solution)/shard_map/pallas_call | solution.py:403
  483.2 8.9 fusion.26
  492.1 7.3 fusion.25
  499.4 8.6 multiply_convert_fusion.1
  508.0 6.9 fusion.24
  514.9 6.8 add_convert_fusion.1
  521.7 56.6 %shard_map.247 = (f32[2,128,1536]{2,1,0:T(8,128)S(1)}, f32[1,1536]{1,0:T(1,128)S(1)}, bf16[4,2,128,1536]{3,2,1,0:T(8,128)(2,1)}) custom-call(bf16[4,2,128,1536]{3,2,1,0:T(8,128)(2,1)} %bitcast.243, f32[2,128,1536]{2,1,0:T(8,128)S(1)} %get-tuple-element.50.h, f32[1,1536]{1,0:T(1,128)S(1)} %copy-done.30, f32[2,128,1536]{2,1,0:T(8,128)} %get-tuple-element.118.g), custom_call_target="tpu_custom_call" | custom-call | tf_op jit(solution)/shard_map/pallas_call | solution.py:403
  578.4 4.3 convolution_convert_fusion.8
  582.7 41.3 %shard_map.248 = (bf16[4,2,128,384]{3,2,1,0:T(8,128)(2,1)S(1)}, bf16[4,4,2,128,384]{4,3,2,1,0:T(8,128)(2,1)}) custom-call(s32[8]{0:T(128)S(1)} %copy-done.36, s32[2]{0:T(128)S(1)} %copy-done.40, bf16[4,2,128,384]{3,2,1,0:T(8,128)(2,1)S(1)} %bitcast.216, bf16[4,4,2,128,384]{4,3,2,1,0:T(8,128)(2,1)} %all-gather.21.cloned.1.call-done.kv_ref, ...), custom_call_target="tpu_custom_call" | custom-call | tf_op jit(solution)/shard_map/pallas_call | solution.py:224
  625.4 6.2 fusion.69
  633.0 2.8 copy-done.92
  635.9 3.5 fusion.71
  642.5 3.5 fusion.70
  651.5 3.4 convolution_bitcast_fusion
  657.6 26.9 %reduce-scatter.3.cloned.1.call-done = bf16[1,4,2,128,384]{4,3,2,1,0:T(8,128)(2,1)} async-done(((bf16[4,4,2,128,384]{4,3,2,1,0:T(8,128)(2,1)}), bf16[1,4,2,128,384]{4,3,2,1,0:T(8,128)(2,1)}) %reduce-scatter.3.cloned.1.call-update) | async-done | bytes 786448 | tf_op jit(solution)/shard_map/reduce_scatter | solution.py:645
  686.9 3.2 copy.58
  690.1 5.1 fusion.36
  695.2 5.1 fusion.44
  704.2 3.3 add_convert_fusion.2
  707.6 3.2 add_convert_fusion.3
  710.8 3.1 add_convert_fusion.4
  716.4 6.4 convolution_convert_fusion.1
  722.8 58.3 %shard_map.249 = (bf16[2,128,1536]{2,1,0:T(8,128)(2,1)S(1)}, f32[1,1536]{1,0:T(1,128)S(1)}, bf16[4,2,128,1536]{3,2,1,0:T(8,128)(2,1)}) custom-call(bf16[4,2,128,1536]{3,2,1,0:T(8,128)(2,1)} %bitcast.244, f32[2,128,1536]{2,1,0:T(8,128)S(1)} %copy-done.7, f32[1,1536]{1,0:T(1,128)S(1)} %get-tuple-element.158.gain, f32[2,128,1536]{2,1,0:T(8,128)S(1)} %copy-done.17), custom_call_target="tpu_custom_call" | custom-call | tf_op jit(solution)/shard_map/pallas_call | solution.py:403
  782.5 8.9 multiply_convert_fusion
  791.5 3.5 fusion.20
  795.0 7.3 add_convert_fusion
  802.4 57.1 %shard_map.250 = (f32[2,128,1536]{2,1,0:T(8,128)S(1)}, f32[1,1536]{1,0:T(1,128)S(1)}, bf16[4,2,128,1536]{3,2,1,0:T(8,128)(2,1)}) custom-call(bf16[4,2,128,1536]{3,2,1,0:T(8,128)(2,1)} %bitcast.245, f32[2,128,1536]{2,1,0:T(8,128)S(1)} %copy-done.4, f32[1,1536]{1,0:T(1,128)S(1)} %get-tuple-element.159.gain, f32[2,128,1536]{2,1,0:T(8,128)} %convert_element_type.265.g), custom_call_target="tpu_custom_call" | custom-call | tf_op jit(solution)/shard_map/pallas_call | solution.py:403
  859.5 4.3 convolution_convert_fusion.7
  863.9 41.3 %shard_map.251 = (bf16[4,2,128,384]{3,2,1,0:T(8,128)(2,1)S(1)}, bf16[4,4,2,128,384]{4,3,2,1,0:T(8,128)(2,1)}) custom-call(s32[8]{0:T(128)S(1)} %copy-done.37, s32[2]{0:T(128)S(1)} %copy-done.41, bf16[4,2,128,384]{3,2,1,0:T(8,128)(2,1)S(1)} %bitcast.214, bf16[4,4,2,128,384]{4,3,2,1,0:T(8,128)(2,1)} %all-gather.11.cloned.1.call-done.kv_ref, ...), custom_call_target="tpu_custom_call" | custom-call | tf_op jit(solution)/shard_map/pallas_call | solution.py:224
  906.4 6.3 fusion.68
  914.6 3.5 fusion.67
  920.0 3.5 fusion.66
  928.9 17.1 %all-reduce.13.cloned.1.call-done = (bf16[768,768]{1,0:T(8,128)(2,1)}, bf16[512,1536]{1,0:T(8,128)(2,1)}, bf16[768,1024]{1,0:T(8,128)(2,1)}, bf16[768,1024]{1,0:T(8,128)(2,1)}, bf16[192,1536]{1,0:T(8,128)(2,1)}) async-done(((bf16[768,768]{1,0:T(8,128)(2,1)}, bf16[512,1536]{1,0:T(8,128)(2,1)}, bf16[768,1024]{1,0:T(8,128)(2,1)}, bf16[768,1024]{1,0:T(8,128)(2,1)}, bf16[192,1536]{1,0:T(8,128)(2,1)}), ...) | async-done | bytes 6488080 | tf_op jit(solution)/shard_map/psum | solution.py:668
  946.5 7.6 convolution_convert_fusion.4
  954.2 31.3 %shard_map.245 = bf16[2,128,1536]{2,1,0:T(8,128)(2,1)S(1)} custom-call(bf16[4,2,128,1536]{3,2,1,0:T(8,128)(2,1)} %bitcast.252, f32[2,128,1536]{2,1,0:T(8,128)S(1)} %copy-done.9), custom_call_target="tpu_custom_call" | custom-call | tf_op jit(solution)/shard_map/pallas_call | solution.py:403
  995.5 12.5 reduce-scatter.5.cloned.1.call-done
  1010.4 3.0 copy.61
  1013.4 4.9 fusion.38
  1024.4 5.9 convolution_convert_fusion
  1030.3 32.5 %shard_map.252 = (f32[2,128,1536]{2,1,0:T(8,128)S(1)}, f32[1,1536]{1,0:T(1,128)S(1)}) custom-call(bf16[4,2,128,1536]{3,2,1,0:T(8,128)(2,1)} %bitcast.246, f32[2,128,1536]{2,1,0:T(8,128)S(1)} %get-tuple-element.120.h, f32[1,1536]{1,0:T(1,128)S(1)} %copy-done.29, f32[2,128,1536]{2,1,0:T(8,128)} %copy-done.18), custom_call_target="tpu_custom_call" | custom-call | tf_op jit(solution)/shard_map/pallas_call | solution.py:403
  1063.0 121.6 %all-reduce.11.cloned.1.call-done = (bf16[512,1536]{1,0:T(8,128)(2,1)}, bf16[768,1024]{1,0:T(8,128)(2,1)}, bf16[768,1024]{1,0:T(8,128)(2,1)}) async-done(((bf16[512,1536]{1,0:T(8,128)(2,1)}, bf16[768,1024]{1,0:T(8,128)(2,1)}, bf16[768,1024]{1,0:T(8,128)(2,1)}), (bf16[512,1536]{1,0:T(8,128)(2,1)}, bf16[768,1024]{1,0:T(8,128)(2,1)}, bf16[768,1024]{1,0:T(8,128)(2,1)})) %all-reduce.11.cloned.1.call-update) | async-done | bytes 4718608 | tf_op jit(solution)/shard_map/psum | solution.py:668
  1184.6 3.2 select_bitcast_fusion
  1187.8 3.3 add_convert_fusion.9
  1191.2 42.9 %psum.77 = f32[2,2,1536]{2,1,0:T(2,128)S(1)} all-reduce(f32[2,2,1536]{2,1,0:T(2,128)S(1)} %pad_maximum_fusion.7), channel_id=1, replica_groups=mesh['section'=2,'ctx'=4,'tensor'=4] {'section','ctx','tensor'}, use_global_device_ids=true, to_apply=%region_2.3 | all-reduce | flops 6144 | bytes 49152 | tf_op jit(solution)/shard_map/psum | solution.py:706
  1241.0 4.4 fusion.18
  1245.4 22.0 %all-reduce.9.cloned.1.call-done = (bf16[768,768]{1,0:T(8,128)(2,1)}, bf16[192,1536]{1,0:T(8,128)(2,1)}) async-done(((bf16[768,768]{1,0:T(8,128)(2,1)}, bf16[192,1536]{1,0:T(8,128)(2,1)}), (bf16[768,768]{1,0:T(8,128)(2,1)}, bf16[192,1536]{1,0:T(8,128)(2,1)})) %all-reduce.9.cloned.1.call-update) | async-done | bytes 1769488 | tf_op jit(solution)/shard_map/psum | solution.py:668
  1270.0 4.8 fusion.16
  1274.8 4.7 fusion.17
  (386 shorter events, 123.1 us)
Async XLA Ops:
  7.2 64.6 %all-gather.23.cloned.1.call-start = ((), (), s32[]{:S(2)}) async-start(), calls=%async_computation.10 | async-start | bytes 14155776 | tf_op jit(solution)/shard_map/all_gather | solution.py:586
  15.6 130.5 %all-gather.11.cloned.1.call-start = ((), (), s32[]{:S(2)}) async-start(), calls=%async_computation.2 | async-start | bytes 3932160 | tf_op jit(solution)/shard_map/all_gather | solution.py:619
  17.6 19.8 %collective-permute-start = (bf16[2,128,768]{2,1,0:T(8,128)(2,1)}, bf16[2,128,768]{2,1,0:T(8,128)(2,1)}, u32[]{:S(2)}, u32[]{:S(2)}) collective-permute-start(bf16[2,128,768]{2,1,0:T(8,128)(2,1)} %get-tuple-element.149), channel_id=1, source_target_pairs={{0,16},{16,0},{1,17},{17,1},{2,18},{18,2},{3,19},{19,3},{4,20},{20... | collective-permute-start | bytes 1179656 | tf_op jit(solution)/shard_map/ppermute | solution.py:538
  25.4 12.0 copy-start.53
  30.3 49.5 %copy-start.46 = (f32[1024,384]{1,0:T(8,128)}, f32[1024,384]{1,0:T(8,128)S(1)}, u32[]{:S(2)}) copy-start(f32[1024,384]{1,0:T(8,128)S(1)} %copy.56) | copy-start | bytes 4718596
  71.8 8.1 copy-start.55
  71.8 8.1 copy-start.57
  71.8 8.1 copy-start.84
  71.8 8.1 copy-start.86
  82.2 92.7 %all-gather.13.cloned.1.call-start = ((), (), s32[]{:S(2)}) async-start(), calls=%async_computation.3 | async-start | bytes 3538944 | tf_op jit(solution)/shard_map/all_gather | solution.py:586
  82.9 156.0 %all-gather.15.cloned.1.call-start = ((), (), s32[]{:S(2)}) async-start(), calls=%async_computation.4 | async-start | bytes 9437184 | tf_op jit(solution)/shard_map/all_gather | solution.py:586
  83.5 163.6 %all-gather.17.cloned.1.call-start = ((), (), s32[]{:S(2)}) async-start(), calls=%async_computation.5 | async-start | bytes 9437184 | tf_op jit(solution)/shard_map/all_gather | solution.py:586
  84.1 173.4 %all-gather.19.cloned.1.call-start = ((), (), s32[]{:S(2)}) async-start(), calls=%async_computation.6 | async-start | bytes 9437184 | tf_op jit(solution)/shard_map/all_gather | solution.py:586
  84.6 309.7 %all-gather.21.cloned.1.call-start = ((), (), s32[]{:S(2)}) async-start(), calls=%async_computation.7 | async-start | bytes 3932160 | tf_op jit(solution)/shard_map/all_gather | solution.py:619
  321.3 8.6 copy-start.5
  321.3 8.6 copy-start.47
  321.3 8.6 copy-start.49
  321.3 8.6 copy-start.56
  321.3 8.6 copy-start.58
  321.3 8.6 copy-start.85
  321.3 8.6 copy-start.87
  332.1 352.4 %reduce-scatter.3.cloned.1.call-start = ((), (), s32[]{:S(2)}) async-start(), calls=%async_computation.8 | async-start | bytes 3932160 | tf_op jit(solution)/shard_map/reduce_scatter | solution.py:645
  333.3 1.8 collective-permute-start.2
  397.6 24.2 %copy-start.94 = (bf16[2,384,1536]{2,1,0:T(8,128)(2,1)S(1)}, bf16[2,384,1536]{2,1,0:T(8,128)(2,1)}, u32[]{:S(2)}) copy-start(bf16[2,384,1536]{2,1,0:T(8,128)(2,1)} %all-gather.13.cloned.1.call-done) | copy-start | bytes 7077892
  483.2 38.5 %copy-start.8 = (f32[2,128,1536]{2,1,0:T(8,128)}, f32[2,128,1536]{2,1,0:T(8,128)S(1)}, u32[]{:S(2)}) copy-start(f32[2,128,1536]{2,1,0:T(8,128)S(1)} %get-tuple-element.50.h) | copy-start | bytes 4718596
  483.2 8.9 copy-start.91
  483.2 16.1 %slice-start.6 = ((s8[6291456]{0:T(1024)(128)(4,1)}), s8[4194304]{0:T(1024)(128)(4,1)S(1)}, s32[]{:S(2)}) async-start(s8[6291456]{0:T(1024)(128)(4,1)} %bitcast.256), calls=%async_computation.20 | async-start | bytes 8388608
  624.9 321.1 %all-reduce.13.cloned.1.call-start = ((), (), s32[]{:S(2)}) async-start(), calls=%async_computation.13 | async-start | bytes 12976128 | tf_op jit(solution)/shard_map/psum | solution.py:668
  633.0 77.8 %collective-permute-start.9 = (bf16[512,1536]{1,0:T(8,128)(2,1)}, bf16[512,1536]{1,0:T(8,128)(2,1)}, u32[]{:S(2)}, u32[]{:S(2)}) collective-permute-start(bf16[512,1536]{1,0:T(8,128)(2,1)} %dynamic-slice_convert_fusion.2), channel_id=1, source_target_pairs={{0,16},{16,0},{1,17},{17,1},{2,18},{18,2},{3,19},{19,3},{4,20},{20... | collective-permute-start | bytes 4718600 | tf_op jit(solution)/shard_map/ppermute | solution.py:538
  640.8 63.4 %collective-permute-start.11 = (bf16[768,1024]{1,0:T(8,128)(2,1)}, bf16[768,1024]{1,0:T(8,128)(2,1)}, u32[]{:S(2)}, u32[]{:S(2)}) collective-permute-start(bf16[768,1024]{1,0:T(8,128)(2,1)} %dynamic-slice_convert_fusion), channel_id=1, source_target_pairs={{0,16},{16,0},{1,17},{17,1},{2,18},{18,2},{3,19},{19,3},{4,20},{20... | collective-permute-start | bytes 4718600 | tf_op jit(solution)/shard_map/ppermute | solution.py:538
  649.2 58.4 %collective-permute-start.10 = (bf16[768,1024]{1,0:T(8,128)(2,1)}, bf16[768,1024]{1,0:T(8,128)(2,1)}, u32[]{:S(2)}, u32[]{:S(2)}) collective-permute-start(bf16[768,1024]{1,0:T(8,128)(2,1)} %dynamic-slice_convert_fusion.1), channel_id=1, source_target_pairs={{0,16},{16,0},{1,17},{17,1},{2,18},{18,2},{3,19},{19,3},{4,20},{20... | collective-permute-start | bytes 4718600 | tf_op jit(solution)/shard_map/ppermute | solution.py:538
  656.2 33.8 %copy-start.51 = (f32[1024,2,96]{0,2,1:T(8,128)S(1)}, f32[1024,2,96]{0,2,1:T(8,128)}, u32[]{:S(2)}) copy-start(f32[1024,2,96]{0,2,1:T(8,128)} %copy-done.50) | copy-start | bytes 2359300
  657.1 43.5 %collective-permute-start.12 = (bf16[192,1536]{1,0:T(8,128)(2,1)}, bf16[192,1536]{1,0:T(8,128)(2,1)}, u32[]{:S(2)}, u32[]{:S(2)}) collective-permute-start(bf16[192,1536]{1,0:T(8,128)(2,1)} %dynamic-slice_convert_fusion.8), channel_id=1, source_target_pairs={{0,16},{16,0},{1,17},{17,1},{2,18},{18,2},{3,19},{19,3},{4,20},{20... | collective-permute-start | bytes 1769480 | tf_op jit(solution)/shard_map/ppermute | solution.py:538
  690.1 14.2 %slice-start.2 = ((s8[6291456]{0:T(1024)(128)(4,1)}), s8[4194304]{0:T(1024)(128)(4,1)S(1)}, s32[]{:S(2)}) async-start(s8[6291456]{0:T(1024)(128)(4,1)} %bitcast.237), calls=%async_computation.16 | async-start | bytes 8388608
  690.1 17.5 %slice-start.4 = ((s8[6291456]{0:T(1024)(128)(4,1)}), s8[4194304]{0:T(1024)(128)(4,1)S(1)}, s32[]{:S(2)}) async-start(s8[6291456]{0:T(1024)(128)(4,1)} %bitcast.239), calls=%async_computation.18 | async-start | bytes 8388608
  695.2 9.0 slice-start.3
  695.2 12.4 slice-start.5
  700.5 13.4 %collective-permute-start.13 = (bf16[768,768]{1,0:T(8,128)(2,1)S(1)}, bf16[768,768]{1,0:T(8,128)(2,1)S(1)}, u32[]{:S(2)}, u32[]{:S(2)}) collective-permute-start(bf16[768,768]{1,0:T(8,128)(2,1)S(1)} %dynamic-slice_convert_fusion.6), channel_id=1, source_target_pairs={{0,16},{16,0},{1,17},{17,1},{2,18},{18,2},{3,19},{19,3},{4,20},{20... | collective-permute-start | bytes 3538952 | tf_op jit(solution)/shard_map/ppermute | solution.py:538
  702.0 8.8 slice-start
  715.3 292.7 %reduce-scatter.5.cloned.1.call-start = ((), (), s32[]{:S(2)}) async-start(), calls=%async_computation.9 | async-start | bytes 3932160 | tf_op jit(solution)/shard_map/reduce_scatter | solution.py:645
  722.8 59.7 %copy-start.98 = (f32[1024,1024]{1,0:T(8,128)S(1)}, f32[1024,1024]{1,0:T(8,128)}, u32[]{:S(2)}) copy-start(f32[1024,1024]{1,0:T(8,128)} %fusion.21) | copy-start | bytes 12582916
  722.8 68.7 %slice-start.8 = ((s8[6291456]{0:T(1024)(128)(4,1)}), s8[2097152]{0:T(1024)(128)(4,1)S(1)}, s32[]{:S(2)}) async-start(s8[6291456]{0:T(1024)(128)(4,1)} %bitcast.258), calls=%async_computation.22 | async-start | bytes 4194304
  781.1 10.3 copy-start.44
  782.5 9.0 slice-start.9
  802.4 57.1 %copy-start.95 = (bf16[2,384,1536]{2,1,0:T(8,128)(2,1)S(1)}, bf16[2,384,1536]{2,1,0:T(8,128)(2,1)}, u32[]{:S(2)}) copy-start(bf16[2,384,1536]{2,1,0:T(8,128)(2,1)} %all-gather.13.cloned.1.call-done) | copy-start | bytes 7077892
  906.1 278.5 %all-reduce.11.cloned.1.call-start = ((), (), s32[]{:S(2)}) async-start(), calls=%async_computation.12 | async-start | bytes 9437184 | tf_op jit(solution)/shard_map/psum | solution.py:668
  912.9 10.8 collective-permute-start.8
  918.3 7.2 collective-permute-start.7
  923.7 3.6 collective-permute-start.6
  946.1 321.3 %all-reduce.9.cloned.1.call-start = ((), (), s32[]{:S(2)}) async-start(), calls=%async_computation.11 | async-start | bytes 3538944 | tf_op jit(solution)/shard_map/psum | solution.py:668
  954.2 31.5 %copy-start.20 = (bf16[4,2,128,384]{3,2,1,0:T(8,128)(2,1)S(1)}, bf16[4,2,128,384]{3,2,1,0:T(8,128)(2,1)}, u32[]{:S(2)}) copy-start(bf16[4,2,128,384]{3,2,1,0:T(8,128)(2,1)} %copy-done.19) | copy-start | bytes 2359300
  954.2 31.5 %copy-start.68 = (bf16[4,2,128,1536]{3,2,1,0:T(8,128)(2,1)S(1)}, bf16[4,2,128,1536]{3,2,1,0:T(8,128)(2,1)}, u32[]{:S(2)}) copy-start(bf16[4,2,128,1536]{3,2,1,0:T(8,128)(2,1)} %get-tuple-element.59) | copy-start | bytes 9437188
  985.5 4.3 collective-permute-start.1
  989.3 3.8 collective-permute-start.4
  995.5 17.9 %copy-start.52 = (f32[1024,2,96]{0,2,1:T(8,128)S(1)}, f32[1024,2,96]{0,2,1:T(8,128)}, u32[]{:S(2)}) copy-start(f32[1024,2,96]{0,2,1:T(8,128)} %copy-done.50) | copy-start | bytes 2359300
  995.5 17.9 %copy-start.54 = (f32[1024,2,96]{0,2,1:T(8,128)S(1)}, f32[1024,2,96]{0,2,1:T(8,128)}, u32[]{:S(2)}) copy-start(f32[1024,2,96]{0,2,1:T(8,128)} %copy-done.53) | copy-start | bytes 2359300
  1024.4 163.4 %collective-permute-start.5 = (bf16[768,768]{1,0:T(8,128)(2,1)}, bf16[768,768]{1,0:T(8,128)(2,1)}, u32[]{:S(2)}, u32[]{:S(2)}) collective-permute-start(bf16[768,768]{1,0:T(8,128)(2,1)} %dynamic-slice_convert_fusion.7), channel_id=1, source_target_pairs={{0,16},{16,0},{1,17},{17,1},{2,18},{18,2},{3,19},{19,3},{4,20},{20... | collective-permute-start | bytes 3538952 | tf_op jit(solution)/shard_map/ppermute | solution.py:538
  1062.8 171.9 %collective-permute-start.3 = (bf16[2,128,768]{2,1,0:T(8,128)(2,1)S(1)}, bf16[2,128,768]{2,1,0:T(8,128)(2,1)S(1)}, u32[]{:S(2)}, u32[]{:S(2)}) collective-permute-start(bf16[2,128,768]{2,1,0:T(8,128)(2,1)S(1)} %select_convert_fusion), channel_id=1, source_target_pairs={{0,16},{16,0},{1,17},{17,1},{2,18},{18,2},{3,19},{19,3},{4,20},{20... | collective-permute-start | bytes 1179656 | tf_op jit(solution)/shard_map/ppermute | solution.py:538
  1187.8 53.2 %collective-permute-start.18 = (bf16[512,1536]{1,0:T(8,128)(2,1)}, bf16[512,1536]{1,0:T(8,128)(2,1)}, u32[]{:S(2)}, u32[]{:S(2)}) collective-permute-start(bf16[512,1536]{1,0:T(8,128)(2,1)} %get-tuple-element.132), channel_id=1, source_target_pairs={{0,16},{16,0},{1,17},{17,1},{2,18},{18,2},{3,19},{19,3},{4,20},{20... | collective-permute-start | bytes 4718600 | tf_op jit(solution)/shard_map/ppermute | solution.py:538
  1238.0 32.0 %collective-permute-start.16 = (bf16[768,1024]{1,0:T(8,128)(2,1)}, bf16[768,1024]{1,0:T(8,128)(2,1)}, u32[]{:S(2)}, u32[]{:S(2)}) collective-permute-start(bf16[768,1024]{1,0:T(8,128)(2,1)} %get-tuple-element.136), channel_id=1, source_target_pairs={{0,16},{16,0},{1,17},{17,1},{2,18},{18,2},{3,19},{19,3},{4,20},{20... | collective-permute-start | bytes 4718600 | tf_op jit(solution)/shard_map/ppermute | solution.py:538
  1241.0 33.8 %collective-permute-start.17 = (bf16[768,1024]{1,0:T(8,128)(2,1)}, bf16[768,1024]{1,0:T(8,128)(2,1)}, u32[]{:S(2)}, u32[]{:S(2)}) collective-permute-start(bf16[768,1024]{1,0:T(8,128)(2,1)} %get-tuple-element.134), channel_id=1, source_target_pairs={{0,16},{16,0},{1,17},{17,1},{2,18},{18,2},{3,19},{19,3},{4,20},{20... | collective-permute-start | bytes 4718600 | tf_op jit(solution)/shard_map/ppermute | solution.py:538
  1245.4 23.9 %copy-start.81 = (bf16[192,1536]{1,0:T(8,128)(2,1)S(1)}, bf16[192,1536]{1,0:T(8,128)(2,1)}, u32[]{:S(2)}) copy-start(bf16[192,1536]{1,0:T(8,128)(2,1)} %get-tuple-element.117) | copy-start | bytes 1769476
  1269.2 11.9 collective-permute-start.14
  1269.4 10.0 collective-permute-start.15
  (83 other events, 314.8 us)
Sparse Core Ops, SparseCore 0:
  15.7 24.5 all-gather.22
  82.3 63.7 all-gather.10
  147.6 9.6 all-gather.12
  158.7 17.9 all-gather.14
  178.1 17.9 all-gather.16
  197.4 17.9 all-gather.18
  332.2 62.0 all-gather.20
  625.0 59.4 reduce-scatter.2
  715.4 230.5 all-reduce.12
  948.9 59.0 reduce-scatter.4
  1011.9 172.6 all-reduce.10
  1191.3 76.0 all-reduce.8

commit v3 on v2

v3 whole, which is shorter than its diff:
```python
import functools

import jax
import jax.numpy as jnp
import numpy as np
from jax import lax
from jax.experimental import pallas as pl
from jax.experimental.pallas import tpu as pltpu
from jax.sharding import PartitionSpec as P

HEAD_DIM = 96
EPSILON = 1e-05
ROPE_BASE = 100000.0
LOG2E = 1.4426950408889634
BF = jnp.bfloat16
F32 = jnp.float32


def nn(a, b):
    return lax.dot_general(a, b, (((1,), (0,)), ((), ())), preferred_element_type=F32)


def nt(a, b):
    return lax.dot_general(a, b, (((1,), (1,)), ((), ())), preferred_element_type=F32)


def tn(a, b):
    return lax.dot_general(a, b, (((0,), (0,)), ((), ())), preferred_element_type=F32)


def head_of(x, h):
    return x[:, h * HEAD_DIM : (h + 1) * HEAD_DIM]


def transposed(x):
    return x.astype(F32).T.astype(BF)


def causal(length):
    keys = lax.broadcasted_iota(jnp.int32, (length, length), 0)
    queries = lax.broadcasted_iota(jnp.int32, (length, length), 1)
    return keys <= queries


def silu_product(gate, up):
    return gate * jax.nn.sigmoid(gate) * up


MESH = pl.DeviceIdType.MESH


def tensor_peers():
    t = lax.axis_index("tensor")
    return t, t + 1 - 2 * lax.rem(t, 2), lax.rem(t + 2, 4), 3 - t


def greet(tensor=True, line=False, after=False):
    barrier = pltpu.get_barrier_semaphore()
    count = 0
    if tensor:
        _, x, y, _ = tensor_peers()
        for peer in (x, y):
            pl.semaphore_signal(barrier, inc=1, device_id={"tensor": peer}, device_id_type=MESH)
        count += 2
    if line:
        c, _, has_left, has_right = ctx_ends()
        for there, peer in ((has_left, c - 1), (has_right, c + 1)):

            @pl.when(there)
            def _():
                pl.semaphore_signal(
                    barrier, inc=1, device_id={"ctx": peer}, device_id_type=MESH
                )

        count += has_left.astype(jnp.int32) + has_right.astype(jnp.int32)
    if after:
        count += lax.axis_index("section")
    pl.semaphore_wait(barrier, count)


def send(src, dst, sems, at, peer):
    return pltpu.make_async_remote_copy(
        src_ref=src,
        dst_ref=dst,
        send_sem=sems[0].at[at],
        recv_sem=sems[1].at[at],
        device_id={"tensor": peer},
        device_id_type=MESH,
    )


def gather_start(full, sems, chunks, q):
    t, x, y, _ = tensor_peers()
    j, at = chunks[q]
    near, far = (x, y) if j == 0 else (y, x)
    own = full.at[t, j, at]
    send(own, own, sems, (q, 0), near).start()
    send(own, own, sems, (q, 1), far).start()


def gather_pass(full, sems, chunks, q):
    _, x, y, _ = tensor_peers()
    j, at = chunks[q]
    near, far = (x, y) if j == 0 else (y, x)
    got = full.at[near, j, at]
    send(got, got, sems, (q, 0), near).wait_recv()
    send(got, got, sems, (q, 2), far).start()


def gather_end(full, sems, chunks, q):
    t, x, y, diag = tensor_peers()
    j, at = chunks[q]
    near, far = (x, y) if j == 0 else (y, x)
    for kind, owner in ((1, far), (2, diag)):
        got = full.at[owner, j, at]
        send(got, got, sems, (q, kind), far).wait_recv()


def gather_drain(full, sems, chunks, q):
    t, x, _, _ = tensor_peers()
    j, at = chunks[q]
    own = full.at[t, j, at]
    for kind in range(3):
        send(own, own, sems, (q, kind), x).wait_send()


def scatter_start(part, got, sems, chunks, q):
    _, x, y, diag = tensor_peers()
    j, at = chunks[q]
    far = y if j == 0 else x
    send(part.at[diag, j, at], got.at[0, j, at], sems, (q, 0), far).start()
    send(part.at[far, j, at], got.at[2, j, at], sems, (q, 2), far).start()


def scatter_pass(part, got, held, sems, chunks, q):
    _, x, y, _ = tensor_peers()
    j, at = chunks[q]
    near = x if j == 0 else y
    send(held.at[j, at], got.at[0, j, at], sems, (q, 0), near).wait_recv()
    held[j, at] = (part[near, j, at].astype(F32) + got[0, j, at].astype(F32)).astype(BF)
    send(held.at[j, at], got.at[1, j, at], sems, (q, 1), near).start()


def scatter_end(part, got, held, sems, chunks, q):
    t, x, _, _ = tensor_peers()
    j, at = chunks[q]
    for kind in (2, 1):
        send(held.at[j, at], got.at[kind, j, at], sems, (q, kind), x).wait_recv()
    return (
        part[t, j, at].astype(F32) + got[1, j, at].astype(F32) + got[2, j, at].astype(F32)
    )


def scatter_drain(part, got, sems, chunks, q):
    t, x, _, _ = tensor_peers()
    j, at = chunks[q]
    for kind in range(3):
        send(part.at[t, j, at], got.at[kind, j, at], sems, (q, kind), x).wait_send()


def inverse_rms(v):
    return lax.rsqrt(jnp.mean(v * v, axis=-1, keepdims=True) + EPSILON)


def norm_back(v, gain, dn):
    r = inverse_rms(v)
    unit = v * r
    scaled = dn * gain
    dv = r * (scaled - unit * jnp.mean(scaled * unit, axis=-1, keepdims=True))
    return dv, jnp.sum((dn * unit).reshape(-1, 8, v.shape[-1]), axis=0)


def chunk_list(sp):
    parts = 2
    size = sp // parts
    return [(j, pl.ds(s * size, size)) for s in range(parts) for j in range(2)]


def run_exchange(
    sp, part, finish, full, got, held, sc_sems, ga_sems,
    between=None, after=None, chain=None, turns=False,
):
    chunks = chunk_list(sp)
    n = range(len(chunks))
    greet(line=chain is not None, after=turns)
    steps = []
    if part is not None:
        for q in n:
            scatter_start(part, got, sc_sems, chunks, q)
        steps += [
            functools.partial(scatter_pass, part, got, held, sc_sems, chunks, q) for q in n
        ]

    def end(q):
        j, at = chunks[q]
        total = None if part is None else scatter_end(part, got, held, sc_sems, chunks, q)
        finish(j, at, total)
        if full is not None:
            gather_start(full, ga_sems, chunks, q)

    steps += [functools.partial(end, q) for q in n]
    if between is not None:
        steps.append(between)
    if full is not None:
        steps += [functools.partial(gather_pass, full, ga_sems, chunks, q) for q in n]
    if after is not None:
        steps.append(after)
    if full is not None:
        steps += [functools.partial(gather_end, full, ga_sems, chunks, q) for q in n]
    if chain is None:
        for step in steps:
            step()
    else:
        done = 0
        for time in range(chain.slots):
            chain.slot(time)
            goal = min(len(steps), int(len(steps) * (time + 1) / (0.8 * chain.slots)))
            for step in steps[done:goal]:
                step()
            done = goal
        for step in steps[done:]:
            step()
        chain.drain()
    if turns:

        @pl.when(lax.axis_index("section") == 0)
        def _():
            pl.semaphore_signal(
                pltpu.get_barrier_semaphore(),
                inc=1,
                device_id={"section": 1},
                device_id_type=MESH,
            )

    if full is not None:
        for q in n:
            gather_drain(full, ga_sems, chunks, q)
    if part is not None:
        for q in n:
            scatter_drain(part, got, sc_sems, chunks, q)


class Chain:
    def __init__(self, zs, gots, outs, sems):
        self.zs, self.gots, self.outs = zs, gots, outs
        self.sum_sems, self.back_sems = sems[:2], sems[2:]
        self.c, self.n, _, _ = ctx_ends()
        self.starts = [sum(z.shape[1] for z in zs[:k]) for k in range(len(zs))]
        self.hop = 2
        self.slots = sum(z.shape[1] for z in zs) + 2 * self.hop * (self.n - 1)

    def copy(self, src, dst, sems, d, k, i, peer):
        at = self.starts[k] + i
        return along(src[k].at[d, i], dst[k].at[d, i], sems[0].at[d, at], sems[1].at[d, at], peer)

    def sides(self, d):
        c, n = self.c, self.n
        return (c, c + 1, c - 1) if d == 0 else (n - 1 - c, c - 1, c + 1)

    def slot(self, time):
        n, zs, gots, outs = self.n, self.zs, self.gots, self.outs
        for d in range(2):
            place, ahead, behind = self.sides(d)
            due = time - self.hop * place
            due_back = time - self.hop * (2 * (n - 1) - place)
            for k in range(len(zs)):
                i = due - self.starts[k]
                going = (i >= 0) & (i < zs[k].shape[1])

                @pl.when(going & (place == 0))
                def _():
                    self.copy(zs, gots, self.sum_sems, d, k, i, ahead).start()

                @pl.when(going & (place > 0))
                def _():
                    self.copy(zs, gots, self.sum_sems, d, k, i, ahead).wait_recv()
                    total = (gots[k][d, i].astype(F32) + zs[k][d, i].astype(F32)).astype(BF)

                    @pl.when(place < n - 1)
                    def _():
                        gots[k][d, i] = total
                        self.copy(gots, gots, self.sum_sems, d, k, i, ahead).start()

                    @pl.when(place == n - 1)
                    def _():
                        outs[k][d, i] = total
                        self.copy(outs, outs, self.back_sems, d, k, i, behind).start()

                i_back = due_back - self.starts[k]
                coming = (i_back >= 0) & (i_back < zs[k].shape[1]) & (place < n - 1)

                @pl.when(coming)
                def _():
                    self.copy(outs, outs, self.back_sems, d, k, i_back, behind).wait_recv()

                    @pl.when(place > 0)
                    def _():
                        self.copy(outs, outs, self.back_sems, d, k, i_back, behind).start()

    def drain(self):
        for d in range(2):
            place, ahead, behind = self.sides(d)
            for k in range(len(self.zs)):

                def one(i, _):
                    @pl.when(place < self.n - 1)
                    def _():
                        self.copy(self.zs, self.gots, self.sum_sems, d, k, i, ahead).wait_send()

                    @pl.when(place > 0)
                    def _():
                        self.copy(
                            self.outs, self.outs, self.back_sems, d, k, i, behind
                        ).wait_send()

                    return 0

                lax.fori_loop(0, self.zs[k].shape[1], one, 0)


def chain_scratch(zs):
    sems = pltpu.SemaphoreType.DMA((2, sum(z.shape[1] for z in zs)))
    return [pltpu.VMEM(z.shape, BF) for z in zs] + [sems] * 4


def scatter_scratch(sp, d):
    n = len(chunk_list(sp))
    return [
        pltpu.VMEM((3, 2, sp, d), BF),
        pltpu.VMEM((2, sp, d), BF),
        pltpu.SemaphoreType.DMA((n, 3)),
        pltpu.SemaphoreType.DMA((n, 3)),
    ]


def gather_scratch(sp):
    n = len(chunk_list(sp))
    return [pltpu.SemaphoreType.DMA((n, 3)), pltpu.SemaphoreType.DMA((n, 3))]


def call(kernel, out_shape, scratch, ident, *operands):
    vm = pl.BlockSpec(memory_space=pltpu.VMEM)
    return pl.pallas_call(
        kernel,
        out_shape=out_shape,
        in_specs=[vm] * len(operands),
        out_specs=(vm,) * len(out_shape),
        scratch_shapes=scratch,
        compiler_params=pltpu.CompilerParams(
            collective_id=ident, has_side_effects=True, vmem_limit_bytes=50 * 2**20
        ),
    )(*operands)


def shapes_of(h):
    _, sp, d = h.shape
    return (
        jax.ShapeDtypeStruct((2, sp, d), F32),
        jax.ShapeDtypeStruct((4, 2, sp, d), BF),
        jax.ShapeDtypeStruct((1, d), F32),
        jax.ShapeDtypeStruct((2, sp, d), BF),
    )


def norm_gather_kernel(h, gain, full, *sems):
    t = lax.axis_index("tensor")

    def finish(j, at, _):
        v = h[j, at].astype(F32)
        full[t, j, at] = (v * inverse_rms(v) * gain[...]).astype(BF)

    run_exchange(h.shape[1], None, finish, full, None, None, None, sems)


def norm_gather(h, gain):
    _, full, _, _ = shapes_of(h)
    return call(norm_gather_kernel, (full,), gather_scratch(h.shape[1]), 0, h, gain)[0]


def sum_norm_gather_kernel(kind, part, h, gain, total, full, got, held, s0, s1, g0, g1):
    t = lax.axis_index("tensor")

    def finish(j, at, term):
        v = h[j, at] + term
        if kind == 1:
            v = v.astype(BF).astype(F32)
        total[j, at] = v
        full[t, j, at] = (v * inverse_rms(v) * gain[...]).astype(BF)

    run_exchange(
        h.shape[1], part, finish, full, got, held, (s0, s1), (g0, g1), turns=kind == 0
    )


def sum_norm_gather(part, h, gain, kind):
    wide, full, _, _ = shapes_of(h)
    _, sp, d = h.shape
    return call(
        functools.partial(sum_norm_gather_kernel, kind),
        (wide, full),
        scatter_scratch(sp, d) + gather_scratch(sp),
        2 + kind,
        part, h, gain,
    )


def line_sum(own, rows, sems):
    c, _, has_left, has_right = ctx_ends()
    sides = ((has_left, has_right, c + 1, 0), (has_right, has_left, c - 1, 1))
    for come, go, ahead, d in sides:
        copy = along(rows.at[2 * d + 1], rows.at[2 * d], sems[0].at[d], sems[1].at[d], ahead)
        rows[2 * d + 1] = own

        @pl.when(come)
        def _():
            copy.wait_recv()
            rows[2 * d + 1] = own + rows[2 * d]

        @pl.when(go)
        def _():
            copy.start()

    total = own
    for come, go, ahead, d in sides:
        copy = along(rows.at[2 * d + 1], rows.at[2 * d], sems[0].at[d], sems[1].at[d], ahead)
        total = total + jnp.where(come, rows[2 * d], 0.0)

        @pl.when(go)
        def _():
            copy.wait_send()

    return total


def back_kernel(kind, count, *refs):
    refs = list(refs)

    def take(size):
        out = refs[:size]
        del refs[:size]
        return out

    t, x, y, _ = tensor_peers()
    part, h, gain, g = take(4)
    others = take(1)[0] if kind == 2 else None
    zs = take(count)
    dv_out, dgain = take(2)
    z_out = take(count)
    full = take(1)[0] if kind != 2 else None
    got, held, s0, s1, rows, gs, gr = take(7)
    z_got = take(count)
    z_sems = take(4)
    ga = take(2) if kind != 2 else None
    line = take(3) if kind == 2 else None
    chain = Chain(zs, z_got, z_out, z_sems)
    rows[0] = jnp.zeros_like(rows[0])

    def finish(j, at, term):
        dv, dg = norm_back(h[j, at], gain[...], term)
        rows[0] = rows[0] + dg
        dv = dv + g[j, at].astype(F32)
        dv_out[j, at] = dv.astype(dv_out.dtype)
        if full is not None:
            full[t, j, at] = dv.astype(BF)

    def add_gains(step, peer):
        send(rows.at[2 * step], rows.at[2 * step + 1], (gs, gr), step, peer).start()

    def end_gains(step, peer):
        send(rows.at[2 * step], rows.at[2 * step + 1], (gs, gr), step, peer).wait()

    def between():
        add_gains(0, x)

    def after():
        end_gains(0, x)
        rows[2] = rows[0] + rows[1]
        add_gains(1, y)

    run_exchange(
        h.shape[1], part, finish, full, got, held, (s0, s1), ga, between, after, chain
    )
    end_gains(1, y)
    total = jnp.sum(rows[2] + rows[3], axis=0, keepdims=True)
    if kind == 2:
        blank = jnp.zeros((4, total.shape[1]), F32)
        total = jnp.concatenate([total, others[...], blank], axis=0)
        dgain[...] = line_sum(total, line[0], line[1:])
    else:
        dgain[...] = total


def back(part, h, gain, g, kind, zs, others=None):
    wide, full, row, narrow = shapes_of(h)
    _, sp, d = h.shape
    row = jax.ShapeDtypeStruct((8, d), F32) if kind == 2 else row
    out = (narrow if kind == 1 else wide, row)
    out += tuple(jax.ShapeDtypeStruct(z.shape, BF) for z in zs)
    scratch = scatter_scratch(sp, d) + [
        pltpu.VMEM((4, 8, d), F32),
        pltpu.SemaphoreType.DMA((2,)),
        pltpu.SemaphoreType.DMA((2,)),
    ] + chain_scratch(zs)
    if kind != 2:
        out += (full,)
        scratch += gather_scratch(sp)
    else:
        scratch += [
            pltpu.VMEM((4, 8, d), F32),
            pltpu.SemaphoreType.DMA((2,)),
            pltpu.SemaphoreType.DMA((2,)),
        ]
    operands = (part, h, gain, g) + (() if others is None else (others,)) + tuple(zs)
    res = call(
        functools.partial(back_kernel, kind, len(zs)), out, scratch, 5 + kind, *operands
    )
    return res[0], res[1], res[2 : 2 + len(zs)], res[2 + len(zs) :]


def ctx_ends():
    c = lax.axis_index("ctx")
    n = lax.axis_size("ctx")
    return c, n, c > 0, c < n - 1


def along(src, dst, send_sem, recv_sem, peer):
    return pltpu.make_async_remote_copy(
        src_ref=src,
        dst_ref=dst,
        send_sem=send_sem,
        recv_sem=recv_sem,
        device_id={"ctx": peer},
        device_id_type=MESH,
    )


def fwd_kernel(extra, *refs):
    if extra:
        (
            qkv_ref, h_ref, mix_ref, mixt_ref, lse_ref, kv_all, full,
            qt, m_s, l_s, acc, to_left, to_right, arrive, *ga,
        ) = refs
    else:
        (
            qkv_ref, mix_ref, mixt_ref, lse_ref, kv_all,
            qt, m_s, l_s, acc, to_left, to_right, arrive,
        ) = refs
    c, n, has_left, has_right = ctx_ends()
    n_t, _, sp, _ = qkv_ref.shape
    length, width = kv_all.shape[2:]
    kv_heads = width // (2 * HEAD_DIM)
    q_heads = qt.shape[1]
    q_w = q_heads * HEAD_DIM
    group = q_heads // kv_heads
    scale = HEAD_DIM**-0.5 * LOG2E

    def leftward(r, j):
        at = kv_all.at[r, j]
        return along(at, at, to_left.at[r, j], arrive.at[r, j], c - 1)

    def rightward(r):
        at = kv_all.at[r, 0]
        return along(at, at, to_right.at[r], arrive.at[r, 0], c + 1)

    def pass_left(r):
        @pl.when(has_left)
        def _():
            leftward(r, 0).start()
            leftward(r, 1).start()

    def pass_right(r):
        @pl.when(has_right)
        def _():
            rightward(r).start()

    for j in range(2):
        kv_all[c, j] = qkv_ref[:, j, :, q_w:].reshape(length, width)
    if extra:
        chunks = chunk_list(sp)
        t, _, _, _ = tensor_peers()

    greet(tensor=extra, line=True)
    pass_left(c)
    pass_right(c)
    if extra:
        for q in range(len(chunks)):
            j, at = chunks[q]
            full[t, j, at] = h_ref[j, at]
            gather_start(full, ga, chunks, q)

    for j in range(2):
        x = qkv_ref[:, j, :, :q_w].reshape(length, q_w)
        for h in range(q_heads):
            qt[j, h] = transposed(head_of(x, h))
    m_s[...] = jnp.full_like(m_s, -1e30)
    l_s[...] = jnp.zeros_like(l_s)
    acc[...] = jnp.zeros_like(acc)

    def pair(r, kj, j, masked):
        x = kv_all[r, kj]
        for h in range(q_heads):
            s = nn(head_of(x, h // group), qt[j, h]) * scale
            if masked:
                s = jnp.where(causal(length), s, -1e30)
            m_old = m_s[j, h]
            m_new = jnp.maximum(m_old, jnp.max(s, axis=0, keepdims=True))
            alpha = jnp.exp2(m_old - m_new)
            p = jnp.exp2(s - m_new)
            l_s[j, h] = l_s[j, h] * alpha + jnp.sum(p, axis=0, keepdims=True)
            m_s[j, h] = m_new
            value = transposed(head_of(x, kv_heads + h // group))
            acc[j, h] = acc[j, h] * alpha + nn(value, p.astype(BF))

    def diagonal(j, _):
        pair(c, j, j, True)
        return 0

    lax.fori_loop(0, 2, diagonal, 0)
    if extra:
        for q in range(len(chunks)):
            gather_pass(full, ga, chunks, q)

    def step(s, _):
        from_right = (s > 0) & (c + s < n)
        from_left = (s > 0) & (c - s >= 0)

        @pl.when(from_right)
        def _():
            leftward(c + s, 0).wait_recv()
            leftward(c + s, 1).wait_recv()
            pass_left(c + s)

        @pl.when(from_left)
        def _():
            rightward(c - s).wait_recv()
            pass_right(c - s)

        def item(i, _):
            side = i // 2
            k = lax.rem(i, 2)
            r = jnp.where(side == 0, c + s, c - s)
            ready = jnp.where(side == 0, from_right, from_left) | ((s == 0) & (i == 0))

            @pl.when(ready)
            def _():
                pair(r, jnp.where(side == 0, k, 0), jnp.where(side == 0, 1, k), False)

            return 0

        lax.fori_loop(0, 4, item, 0)
        return 0

    lax.fori_loop(0, n, step, 0)
    for j in range(2):
        outs = []
        for h in range(q_heads):
            out = acc[j, h] / l_s[j, h]
            mixt_ref[j, h] = out.astype(BF)
            lse_ref[j, h] = m_s[j, h] + jnp.log2(l_s[j, h])
            outs.append(out.T)
        mix_ref[:, j] = jnp.concatenate(outs, axis=-1).astype(BF).reshape(n_t, sp, -1)

    def drain(r, _):
        @pl.when((r >= c) & has_left)
        def _():
            leftward(r, 0).wait_send()
            leftward(r, 1).wait_send()

        @pl.when((r <= c) & has_right)
        def _():
            rightward(r).wait_send()

        return 0

    lax.fori_loop(0, n, drain, 0)
    if extra:
        for q in range(len(chunks)):
            gather_end(full, ga, chunks, q)
        for q in range(len(chunks)):
            gather_drain(full, ga, chunks, q)


def flash_forward(qkv, q_heads, h=None):
    n_t, _, sp, width = qkv.shape
    n = lax.axis_size("ctx")
    q_w = q_heads * HEAD_DIM
    length = n_t * sp
    rows = (2, q_heads, 1, length)
    cols = (2, q_heads, HEAD_DIM, length)
    extra = h is not None
    return call(
        functools.partial(fwd_kernel, extra),
        (
            jax.ShapeDtypeStruct((n_t, 2, sp, q_w), BF),
            jax.ShapeDtypeStruct(cols, BF),
            jax.ShapeDtypeStruct(rows, F32),
            jax.ShapeDtypeStruct((n, 2, length, width - q_w), BF),
        )
        + ((shapes_of(h)[1],) if extra else ()),
        [
            pltpu.VMEM(cols, BF),
            pltpu.VMEM(rows, F32),
            pltpu.VMEM(rows, F32),
            pltpu.VMEM(cols, F32),
            pltpu.SemaphoreType.DMA((n, 2)),
            pltpu.SemaphoreType.DMA((n,)),
            pltpu.SemaphoreType.DMA((n, 2)),
        ]
        + (gather_scratch(sp) if extra else []),
        9 if extra else 10,
        qkv,
        *((h,) if extra else ()),
    )


def bwd_kernel(extra, *refs):
    if extra:
        (
            qkv_ref, kv_all, do_ref, mixt_ref, lse_ref, cos_ref, sin_ref, cos_n, sin_n,
            part_ref, h_ref, out_ref, y_ref,
            qt, dot, qn, don, dl_s, dqt, acc, got_r, got_l, put_r, put_l, sr, ar, sl, al,
            sc_got, sc_held, *sc,
        ) = refs
    else:
        (
            qkv_ref, kv_all, do_ref, mixt_ref, lse_ref, cos_ref, sin_ref, cos_n, sin_n, out_ref,
            qt, dot, qn, don, dl_s, dqt, acc, got_r, got_l, put_r, put_l, sr, ar, sl, al,
        ) = refs
    c, n, has_left, has_right = ctx_ends()
    n_t, _, sp, _ = qkv_ref.shape
    length, width = kv_all.shape[2:]
    kv_heads = width // (2 * HEAD_DIM)
    q_heads = qt.shape[1]
    q_w = q_heads * HEAD_DIM
    group = q_heads // kv_heads
    scale = HEAD_DIM**-0.5
    half = HEAD_DIM // 2

    def rightward(r):
        return along(put_r.at[r], got_r.at[r], sr.at[r], ar.at[r], c + 1)

    def leftward(r):
        return along(put_l.at[r], got_l.at[r], sl.at[r], al.at[r], c - 1)

    greet(tensor=extra, line=True)
    if extra:
        chunks = chunk_list(sp)
        for q in range(len(chunks)):
            scatter_start(part_ref, sc_got, sc, chunks, q)
    for j in range(2):
        x = qkv_ref[:, j, :, :q_w].reshape(length, q_w)
        y = do_ref[:, j].reshape(length, q_w)
        for h in range(q_heads):
            a = head_of(x, h)
            qn[j, h] = a
            qt[j, h] = transposed(a)
            b = head_of(y, h)
            don[j, h] = b
            bt = b.astype(F32).T
            dot[j, h] = bt.astype(BF)
            dl_s[j, h] = jnp.sum(bt * mixt_ref[j, h].astype(F32), axis=0, keepdims=True)
    dqt[...] = jnp.zeros_like(dqt)

    def pair(r, kj, j, masked):
        x = kv_all[r, kj]
        for kh in range(kv_heads):
            key = head_of(x, kh)
            value = head_of(x, kv_heads + kh)
            key_t = transposed(key)
            dk = acc[kj, kh]
            dv = acc[kj, kv_heads + kh]
            for g in range(group):
                h = kh * group + g
                s = nn(key, qt[j, h]) * (scale * LOG2E)
                p = jnp.exp2(s - lse_ref[j, h])
                if masked:
                    p = jnp.where(causal(length), p, 0.0)
                dp = nn(value, dot[j, h])
                ds = (p * (dp - dl_s[j, h])).astype(BF)
                dv = dv + nn(p.astype(BF), don[j, h])
                dk = dk + nn(ds, qn[j, h])
                dqt[j, h] += nn(key_t, ds)
            acc[kj, kh] = dk
            acc[kj, kv_heads + kh] = dv

    def joined(kj):
        parts = [acc[kj, i] * (scale if i < kv_heads else 1.0) for i in range(2 * kv_heads)]
        return jnp.concatenate(parts, axis=-1)

    def finish_right(r, has_more):
        @pl.when(has_more)
        def _():
            rightward(r).wait_recv()
            for kj in range(2):
                put_r[r, kj] = (put_r[r, kj].astype(F32) + got_r[r, kj].astype(F32)).astype(BF)

        rightward(r).start()

    def finish_left(r, has_more):
        @pl.when(has_more)
        def _():
            leftward(r).wait_recv()
            put_l[r] = (put_l[r].astype(F32) + got_l[r].astype(F32)).astype(BF)

        leftward(r).start()

    def step(i, _):
        s = n - 1 - i

        def one_side(side, _):
            r = jnp.where(side == 0, c + s, c - s)
            ready = jnp.where(side == 0, c + s < n, (c - s >= 0) & (s > 0))

            @pl.when(ready)
            def _():
                acc[...] = jnp.zeros_like(acc)

                @pl.when(s == 0)
                def _():
                    def diagonal(j, _):
                        pair(c, j, j, True)
                        return 0

                    lax.fori_loop(0, 2, diagonal, 0)

                def item(k, _):
                    @pl.when((s > 0) | (k == 0))
                    def _():
                        pair(r, jnp.where(side == 0, k, 0), jnp.where(side == 0, 1, k), False)

                    return 0

                lax.fori_loop(0, 2, item, 0)

                @pl.when((side == 0) & (s > 0))
                def _():
                    for kj in range(2):
                        put_r[r, kj] = joined(kj).astype(BF)

                    @pl.when(jnp.logical_not(has_left))
                    def _():
                        rightward(r).start()

                @pl.when(side == 1)
                def _():
                    put_l[r] = joined(0).astype(BF)

                    @pl.when(jnp.logical_not(has_right))
                    def _():
                        leftward(r).start()

            return 0

        lax.fori_loop(0, 2, one_side, 0)
        late = s + 1

        @pl.when((c + late < n) & has_left)
        def _():
            finish_right(c + late, has_left)

        @pl.when((c - late >= 0) & has_right)
        def _():
            finish_left(c - late, has_right)

        return 0

    lax.fori_loop(0, 2, step, 0)
    if extra:
        for q in range(len(chunks)):
            scatter_pass(part_ref, sc_got, sc_held, sc, chunks, q)
    lax.fori_loop(2, n, step, 0)
    if extra:
        for q in range(len(chunks)):
            j, at = chunks[q]
            term = scatter_end(part_ref, sc_got, sc_held, sc, chunks, q)
            y_ref[j, at] = (h_ref[j, at] + term).astype(BF)
        for q in range(len(chunks)):
            scatter_drain(part_ref, sc_got, sc, chunks, q)
    for j in range(2):
        outs = []
        for h in range(q_heads):
            d = dqt[j, h] * scale
            sc = d * sin_ref[j]
            back = d * cos_ref[j] + jnp.concatenate([sc[half:], -sc[:half]], axis=0)
            outs.append(back.T)
        out_ref[:, j, :, :q_w] = jnp.concatenate(outs, axis=-1).astype(BF).reshape(n_t, sp, q_w)

    @pl.when(has_right)
    def _():
        leftward(c).wait_recv()

    @pl.when(has_left)
    def _():
        rightward(c).wait_recv()

    for kj in range(2):
        total = joined(kj)
        total += jnp.where(has_left, got_r[c, kj].astype(F32), 0.0)
        if kj == 0:
            total += jnp.where(has_right, got_l[c].astype(F32), 0.0)
        parts = []
        for kh in range(2 * kv_heads):
            d = head_of(total, kh)
            if kh < kv_heads:
                sc = d * sin_n[kj]
                d = d * cos_n[kj] + jnp.concatenate([sc[:, half:], -sc[:, :half]], axis=1)
            parts.append(d)
        out_ref[:, kj, :, q_w:] = jnp.concatenate(parts, axis=-1).astype(BF).reshape(n_t, sp, width)

    def drain(r, _):
        @pl.when((r > c) & has_right)
        def _():
            rightward(r).wait_send()

        @pl.when((r < c) & has_left)
        def _():
            leftward(r).wait_send()

        return 0

    lax.fori_loop(0, n, drain, 0)


def flash_backward(qkv, kv_all, do, mixt, lse, tables, part=None, h=None):
    n, _, length, width = kv_all.shape
    q_heads = mixt.shape[1]
    cols = pltpu.VMEM((2, q_heads, HEAD_DIM, length), BF)
    natural = pltpu.VMEM((2, q_heads, length, HEAD_DIM), BF)
    both = pltpu.VMEM((n, 2, length, width), BF)
    early = pltpu.VMEM((n, length, width), BF)
    sems = pltpu.SemaphoreType.DMA((n,))
    extra = part is not None
    return call(
        functools.partial(bwd_kernel, extra),
        (jax.ShapeDtypeStruct(qkv.shape, BF),) + ((shapes_of(h)[3],) if extra else ()),
        [
            cols,
            cols,
            natural,
            natural,
            pltpu.VMEM((2, q_heads, 1, length), F32),
            pltpu.VMEM((2, q_heads, HEAD_DIM, length), F32),
            pltpu.VMEM((2, width // HEAD_DIM, length, HEAD_DIM), F32),
            both,
            early,
            both,
            early,
            sems,
            sems,
            sems,
            sems,
        ]
        + (scatter_scratch(h.shape[1], h.shape[2]) if extra else []),
        12 if extra else 11,
        qkv, kv_all, do, mixt, lse, *tables, *((part, h) if extra else ()),
    )


def turn_matrix(heads, total):
    half = HEAD_DIM // 2
    m = np.zeros((total, total), np.float32)
    for h in range(heads):
        at = h * HEAD_DIM
        for i in range(half):
            m[at + half + i, at + i] = -1.0
            m[at + i, at + half + i] = 1.0
    return m


def swap(value):
    return lax.ppermute(value, "section", [(0, 1), (1, 0)])


def on_device(
    inputs, cotangent, block_order, attn_gain, w_query, key_weight, value_weight, w_out,
    mlp_gain, w_gate, w_up, w_down,
):
    sec = lax.axis_index("section")
    first = sec == 0
    ctx = lax.axis_index("ctx")
    n_t = lax.axis_size("tensor")
    n_ctx = lax.axis_size("ctx")
    _, _, _, sp, half_width = inputs.shape
    length = sp * n_t
    d = 2 * half_width
    rows = n_t * 2 * sp
    wq, wk, wv = w_query[0], key_weight[0], value_weight[0]
    q_w, kv_w = wq.shape[1], 2 * wk.shape[1]
    qkv_w = q_w + kv_w
    q_heads, kv_heads = q_w // HEAD_DIM, kv_w // (2 * HEAD_DIM)

    def to_own(x):
        keep = lax.dynamic_index_in_dim(x[:, 0], sec, 0, keepdims=False)
        give = lax.dynamic_index_in_dim(x[:, 0], 1 - sec, 0, keepdims=False)
        got = swap(give)
        return jnp.where(
            first, jnp.concatenate([keep, got], -1), jnp.concatenate([got, keep], -1)
        )

    def from_own(y, out_dtype):
        y = in_order(y)
        lo, hi = y[..., :half_width], y[..., half_width:]
        keep = jnp.where(first, lo, hi)
        got = swap(jnp.where(first, hi, lo).astype(BF)).astype(y.dtype)
        return jnp.where(first, jnp.stack([keep, got]), jnp.stack([got, keep]))[
            :, None
        ].astype(out_dtype)

    turned = lax.dynamic_index_in_dim(block_order, 2 * ctx, 0, keepdims=False) != ctx

    def in_order(x):
        return jnp.where(turned, jnp.stack([x[1], x[0]]), x)

    x_own = in_order(to_own(inputs))
    g_own = in_order(to_own(cotangent))

    turn_q = jnp.asarray(turn_matrix(q_heads, q_w), BF)
    turn_kv = turn_matrix(kv_heads, kv_w)
    wkv = jnp.concatenate([wk, wv], 1)
    wcat = jnp.concatenate(
        [wq, wkv, nn(wq, turn_q).astype(BF), nn(wkv, jnp.asarray(turn_kv, BF)).astype(BF)], 1
    )

    def both(w):
        return lax.all_gather(w, "section", axis=0)

    wcat2, wo2, wg2, wu2, wd2, gains2 = (
        both(wcat), both(w_out[0]), both(w_gate[0]), both(w_up[0]), both(w_down[0]),
        both(jnp.concatenate([attn_gain, mlp_gain], 0)),
    )

    own = jnp.stack([ctx, 2 * n_ctx - 1 - ctx])
    offs = jnp.arange(length, dtype=jnp.int32)
    pos = own[:, None] * length + offs[None, :]
    freq = ROPE_BASE ** (-(jnp.arange(0, HEAD_DIM, 2).astype(F32) / HEAD_DIM))
    phase_t = freq[None, :, None] * pos.astype(F32)[:, None, :]
    phase_t = jnp.concatenate([phase_t, phase_t], 1)
    cos_t, sin_t = jnp.cos(phase_t), jnp.sin(phase_t)

    def rows_of(t):
        t = jnp.swapaxes(t, 1, 2).reshape(2, n_t, sp, HEAD_DIM)
        return jnp.swapaxes(t, 0, 1).reshape(rows, HEAD_DIM)

    cos_r, sin_r = rows_of(cos_t), rows_of(sin_t)
    cos_n, sin_n = jnp.swapaxes(cos_t, 1, 2), jnp.swapaxes(sin_t, 1, 2)
    spread = np.zeros((HEAD_DIM, qkv_w), np.float32)
    turned_w = q_w + kv_w // 2
    spread[np.arange(turned_w) % HEAD_DIM, np.arange(turned_w)] = 1.0
    plain = np.where(np.arange(qkv_w) < turned_w, 0.0, 1.0).astype(np.float32)

    def wide_table(t):
        return lax.dot_general(
            t,
            jnp.asarray(spread),
            (((1,), (0,)), ((), ())),
            precision=lax.Precision.HIGHEST,
            preferred_element_type=F32,
        )

    cos_all, sin_all = wide_table(cos_r) + jnp.asarray(plain), wide_table(sin_r)

    def gain_of(layer, kind):
        return gains2[layer, kind : kind + 1]

    def attend(n1, layer, h=None):
        raw = nn(n1, wcat2[layer])
        qkv = (raw[:, :qkv_w] * cos_all + raw[:, qkv_w:] * sin_all).astype(BF)
        qkv = qkv.reshape(n_t, 2, sp, qkv_w)
        mix, mixt, lse, kv_all, *full = flash_forward(qkv, q_heads, h)
        mix = mix.reshape(rows, q_w)
        part = nn(mix, wo2[layer]).astype(BF)
        return part.reshape(n_t, 2, sp, d), (qkv, kv_all, mix, mixt, lse, *full)

    def feed(n2, layer):
        gate, up = nn(n2, wg2[layer]), nn(n2, wu2[layer])
        act = silu_product(gate, up).astype(BF)
        part = nn(act, wd2[layer]).astype(BF)
        return part.reshape(n_t, 2, sp, d), (gate, up, act)

    def feed_back(gm, layer, kept):
        gate, up, _ = kept
        dact = nt(gm, wd2[layer])
        _, pull = jax.vjp(silu_product, gate, up)
        dgate, dup = pull(dact)
        dgate, dup = dgate.astype(BF), dup.astype(BF)
        part = (nt(dgate, wg2[layer]) + nt(dup, wu2[layer])).astype(BF)
        return part.reshape(n_t, 2, sp, d), dgate, dup

    def attend_back(ga, layer, kept, *more):
        qkv, kv_all, _, mixt, lse = kept[:5]
        dmix = nt(ga, wo2[layer]).astype(BF).reshape(n_t, 2, sp, q_w)
        tables = (cos_t, sin_t, cos_n, sin_n)
        dqkv, *more = flash_backward(qkv, kv_all, dmix, mixt, lse, tables, *more)
        dqkv = dqkv.reshape(rows, qkv_w)
        part = nt(dqkv, wcat2[layer][:, :qkv_w]).astype(BF)
        return part.reshape(n_t, 2, sp, d), dqkv, more

    def exchange(*grads):
        out = []
        for g in grads:
            size = g.shape[0] // 2
            give = lax.dynamic_slice_in_dim(g, (1 - sec) * size, size, 0).astype(BF)
            keep = lax.dynamic_slice_in_dim(g, sec * size, size, 0)
            out.append((keep, swap(give)))
        return out

    def terms(halves):
        return [(keep + got.astype(F32)).astype(BF) for keep, got in halves]

    def cut(size, term):
        return term.reshape(2, -1, size, term.shape[1])

    def tie(x, others):
        return lax.optimization_barrier((x, others))

    flat = lambda v: v.reshape(rows, d)
    a0, a1, m0, m1 = gain_of(0, 0), gain_of(1, 0), gain_of(0, 1), gain_of(1, 1)

    h0 = x_own.astype(F32)
    n1_0 = flat(norm_gather(x_own, a0))
    part, att0 = attend(n1_0, 0)
    h2_0, full = sum_norm_gather(part, h0, m0, 0)
    n2_0 = flat(full)
    part, mlp0 = feed(n2_0, 0)
    h1, full = sum_norm_gather(part, h2_0, a1, 1)
    n1_1 = flat(full)
    part, att1 = attend(n1_1, 1, g_own)
    h2_1, full = sum_norm_gather(part, h1, m1, 2)
    n2_1 = flat(full)
    y_part, mlp1 = feed(n2_1, 1)

    gm1 = flat(att1[5])
    def backward(layer, gm, g, h, h2, n1, n2, att, mlp, kind, a_gain, m_gain, others, *more):
        part, dgate, dup = feed_back(gm, layer, mlp)
        wide = exchange(tn(n2, dgate), tn(n2, dup))
        down = exchange(tn(mlp[2], gm))
        zs = [cut(48, v) for v in terms(wide)]
        dh2, dm, wide, (full,) = back(part, h2, m_gain, g, 0, zs)
        ga = flat(full)
        out = exchange(tn(att[2], ga))
        part, dqkv, more = attend_back(ga, layer, att, *more)
        rest = terms(down + out + exchange(tn(n1, dqkv)))
        zs = [cut(size, v) for size, v in zip((32, 32, 64), rest)]
        if others is not None:
            others = jnp.concatenate([dm, *others], 0)
        dh, da, rest, full = back(part, h, a_gain, dh2, kind, zs, others)
        grads = [z.reshape(-1, z.shape[-1]) for z in (rest[0], *wide, *rest[1:])]
        return dh, full, (da, dm), grads, more

    g0, full, gains1, grads1, (y,) = backward(
        1, gm1, g_own.astype(F32), h1, h2_1, n1_1, n2_1, att1, mlp1, 1, a1, m1,
        None, y_part, h2_1,
    )
    dh0, _, (gains, _), grads0, _ = backward(
        0, flat(full[0]), g0.astype(F32), h0, h2_0, n1_0, n2_0, att0, mlp0, 2, a0, m0, gains1
    )
    gains = gains + swap(gains)
    gain_own = lax.dynamic_slice_in_dim(gains, 2 * sec, 2, 0)

    def to_owner(r0, r1):
        got0 = lax.ppermute(r0, "section", [(1, 0)])
        got1 = lax.ppermute(r1, "section", [(0, 1)])
        return jnp.where(
            first, jnp.concatenate([r0, got0], 0), jnp.concatenate([got1, r1], 0)
        ).astype(F32)

    gd, gg, gu, go, gqkv = (to_owner(a, b) for a, b in zip(grads0, grads1))
    half_kv = kv_w // 2
    return (
        from_own(y, BF),
        from_own(dh0, F32),
        gain_own[0:1],
        gqkv[None, :, :q_w],
        gqkv[None, :, q_w : q_w + half_kv],
        gqkv[None, :, q_w + half_kv :],
        go[None],
        gain_own[1:2],
        gg[None],
        gu[None],
        gd[None],
    )


def solution(mesh):
    rows = P(None, "ctx", None, "tensor", "section")
    gain = P("section", None)
    col = P("section", None, "tensor")
    row = P("section", "tensor", None)
    return jax.shard_map(
        on_device,
        mesh=mesh,
        in_specs=(rows, rows, P(), gain, col, col, col, row, gain, col, col, row),
        out_specs=(rows, rows, gain, col, col, col, row, gain, col, col, row),
        check_vma=False,
    )
```

time: 1300 us -> 1120 us (0.86)
  waiting for transfers between devices: 293 us -> 2.01 us
  Pallas kernels: 598 us -> 777 us
  starting transfers between devices: 4.71 us -> 55.2 us
  local copies, waits for them, and re-layouts: 80.1 us -> 33.6 us
  blocking collectives: 44.7 us -> 2.12 us
  other arithmetic: 66.5 us -> 43.1 us
    pallas_call x10 -> x12, Pallas kernels: 467 us -> 777 us  [call(): pl.pallas_call(kernel, out_shape=out_shape, in_specs=[vm] * len(operands)...]
    psum x3 -> x0, waiting for transfers between devices: 161 us -> none  [over_ctx(): return lax.psum(halves, 'ctx')]
    pallas_call x4 -> x0, Pallas kernels: 131 us -> none  [the longest x2 82.6 us: flash_backward(): pl.pallas_call(bwd_kernel, out_shape=(jax.ShapeDtypeStruct(q.shape, BF),...]
    all_gather x2 -> x0, waiting for transfers between devices: 88.8 us -> none  [attend(): kv = lax.all_gather(qkv[:, q_w:].reshape(n_t, 2, sp, kv_w), 'ctx', axis=0)]
    psum x1 -> x0, blocking collectives: 42.9 us -> none  [on_device(): lax.psum(jnp.stack([jnp.concatenate(gains0), jnp.concatenate(gains1)]), (...]
    reduce_scatter x2 -> x0, waiting for transfers between devices: 39.4 us -> none  [attend_back(): lax.psum_scatter(dkv, 'ctx', scatter_dimension=0).astype(F32)]
    ppermute x19 -> x15, starting transfers between devices: 2.53 us -> 34.4 us  [swap(): return lax.ppermute(value, 'section', [(0, 1), (1, 0)])]
    unnamed x238 -> x144, local copies, waits for them, and re-layouts: 41.4 us -> 18.8 us
  transfers between devices with their start and end apart: 31 -> 30, of which waited for: 8 -> 0; matrix products, arithmetic and copies ran while one was open for 17% -> 17% of each run, Pallas kernels for 28% -> 59%
where the time goes in v3:
time: 1120 us
  Pallas kernels  777 us (69%)
  matrix products  187 us (17%)
  starting transfers between devices  55.2 us (5%)
  other arithmetic  43.1 us (4%)
  local copies, waits for them, and re-layouts  33.6 us (3%)
  between operations  16.1 us (1%)
    pallas_call x12, Pallas kernels, call(): pl.pallas_call(kernel, out_shape=out_shape, in_specs=[vm] * len(operands)...  777 us
    dot_general x13, matrix products, nn(): lax.dot_general(a, b, (((1,), (0,)), ((), ())), preferred_element_type=F32)  78.8 us
    dot_general x10, matrix products, nt(): lax.dot_general(a, b, (((1,), (1,)), ((), ())), preferred_element_type=F32)  64 us
    dot_general x10, matrix products, tn(): lax.dot_general(a, b, (((0,), (0,)), ((), ())), preferred_element_type=F32)  34.8 us
    ppermute x15, starting transfers between devices, swap(): return lax.ppermute(value, 'section', [(0, 1), (1, 0)])  34.4 us
  transfers between devices with their start and end apart: 30, of which 0 were waited for; matrix products, arithmetic and copies ran while one was open for 17% of the time, Pallas kernels for 59%

profile of v3, /device:TPU:0, one launch (start us, length us, event | category | flops | bytes accessed | tf_op | source)
XLA Modules:
  0.0 1116.2 jit_solution(18011415232893434493)
XLA Ops:
  12.2 1.8 fusion.29
  21.5 2.1 all-gather.2
  27.5 4.3 fusion.51
  33.5 31.0 %shard_map.239 = bf16[4,2,128,1536]{3,2,1,0:T(8,128)(2,1)S(1)} custom-call(bf16[2,128,1536]{2,1,0:T(8,128)(2,1)S(1)} %get-tuple-element.123.h, f32[1,1536]{1,0:T(1,128)S(1)} %get-tuple-element.150.gain.refs_2_), custom_call_target="tpu_custom_call" | custom-call | tf_op jit(solution)/shard_map/pallas_call | solution.py:343
  64.5 1.7 copy-done.11
  69.1 8.3 fusion.2
  77.4 4.7 fusion.15
  82.1 63.0 %shard_map.240 = (bf16[4,2,128,384]{3,2,1,0:T(8,128)(2,1)S(1)}, bf16[2,4,96,512]{3,2,1,0:T(8,128)(2,1)S(1)}, f32[2,4,1,512]{3,2,1,0:T(1,128)S(1)}, bf16[4,2,512,384]{3,2,1,0:T(8,128)(2,1)}) custom-call(bf16[4,2,128,768]{3,2,1,0:T(8,128)(2,1)S(1)} %bitcast.228), custom_call_target="tpu_custom_call" | custom-call | tf_op jit(solution)/shard_map/pallas_call | solution.py:343
  148.0 5.0 convolution_convert_fusion.3
  153.0 34.4 %shard_map.241 = (f32[2,128,1536]{2,1,0:T(8,128)S(1)}, bf16[4,2,128,1536]{3,2,1,0:T(8,128)(2,1)}) custom-call(bf16[4,2,128,1536]{3,2,1,0:T(8,128)(2,1)} %bitcast.271, f32[2,128,1536]{2,1,0:T(8,128)S(1)} %get-tuple-element.122.h.refs_1_, f32[1,1536]{1,0:T(1,128)S(1)} %get-tuple-element.149.gain.refs_2_), custom_call_target="tpu_custom_call" | custom-call | tf_op jit(solution)/shard_map/pallas_call | solution.py:343
  188.5 8.3 fusion.21
  196.8 10.4 multiply_convert_fusion.3
  207.1 7.7 convolution_convert_fusion.5
  214.8 34.1 %shard_map.242 = (f32[2,128,1536]{2,1,0:T(8,128)S(1)}, bf16[4,2,128,1536]{3,2,1,0:T(8,128)(2,1)}) custom-call(bf16[4,2,128,1536]{3,2,1,0:T(8,128)(2,1)} %bitcast.272, f32[2,128,1536]{2,1,0:T(8,128)S(1)} %copy-done.8, f32[1,1536]{1,0:T(1,128)S(1)} %get-tuple-element.148.gain.refs_2_), custom_call_target="tpu_custom_call" | custom-call | tf_op jit(solution)/shard_map/pallas_call | solution.py:343
  249.0 8.5 fusion
  258.4 45.7 %shard_map.243 = (bf16[4,2,128,384]{3,2,1,0:T(8,128)(2,1)S(1)}, bf16[2,4,96,512]{3,2,1,0:T(8,128)(2,1)S(1)}, f32[2,4,1,512]{3,2,1,0:T(1,128)S(1)}, bf16[4,2,512,...) custom-call(bf16[4,2,128,768]{3,2,1,0:T(8,128)(2,1)S(1)} %bitcast.230, bf16[2,128,1536]{2,1,0:T(8,128)(2,1)S(1)} %get-tuple-element.121.refs_1_), custom_call_target="tpu_custom_call" | custom-call | tf_op jit(solution)/shard_map/pallas_call | solution.py:343
  304.0 5.0 convolution_convert_fusion.2
  309.1 33.9 %shard_map.244 = (f32[2,128,1536]{2,1,0:T(8,128)S(1)}, bf16[4,2,128,1536]{3,2,1,0:T(8,128)(2,1)}) custom-call(bf16[4,2,128,1536]{3,2,1,0:T(8,128)(2,1)} %bitcast.270, f32[2,128,1536]{2,1,0:T(8,128)S(1)} %get-tuple-element.56.h.refs_1_, f32[1,1536]{1,0:T(1,128)S(1)} %get-tuple-element.147.gain.refs_2_), custom_call_target="tpu_custom_call" | custom-call | tf_op jit(solution)/shard_map/pallas_call | solution.py:343
  343.0 6.8 fusion.27
  349.9 7.0 fusion.24
  357.0 8.2 multiply_convert_fusion.1
  365.2 3.6 fusion.54
  370.1 28.7 %collective-permute-start.5 = (bf16[512,1536]{1,0:T(8,128)(2,1)}, bf16[512,1536]{1,0:T(8,128)(2,1)}, u32[]{:S(2)}, u32[]{:S(2)}) collective-permute-start(bf16[512,1536]{1,0:T(8,128)(2,1)} %dynamic-slice_convert_fusion.3), channel_id=1, source_target_pairs={{0,16},{16,0},{1,17},{17,1},{2,18},{18,2},{3,19},{19,3},{4,20},{20... | collective-permute-start | bytes 4718600 | tf_op jit(solution)/shard_map/ppermute | solution.py:971
  398.9 3.5 fusion.52
  402.7 1.8 collective-permute-start.2
  404.5 3.6 fusion.53
  408.4 6.9 convolution_convert_fusion.4
  415.3 5.5 fusion.26
  420.9 7.7 add_convert_fusion.1
  428.6 1.7 add_convert_fusion.7
  430.3 1.8 add_convert_fusion.6
  432.1 96.9 %shard_map.245 = (f32[2,128,1536]{2,1,0:T(8,128)S(1)}, f32[1,1536]{1,0:T(1,128)S(1)}, bf16[2,8,48,1024]{3,2,1,0:T(8,128)(2,1)S(1)}, bf16[2,8,48,1024]{3,2,1,0:T(8,128)(2,1)}, bf16[4,2,128,1536]{3,2,1,0:T(8,128)(2,1)}) custom-call(bf16[4,2,128,1536]{3,2,1,0:T(8,128)(2,1)} %bitcast.275, f32[2,128,1536]{2,1,0:T(8,128)} %copy-done.10, ...), custom_call_target="tpu_custom_call" | custom-call | tf_op jit(solution)/shard_map/pallas_call | solution.py:343
  529.1 4.3 convolution_convert_fusion.8
  533.4 63.2 %shard_map.246 = (bf16[4,2,128,768]{3,2,1,0:T(8,128)(2,1)}, bf16[2,128,1536]{2,1,0:T(8,128)(2,1)S(1)}) custom-call(bf16[4,2,128,768]{3,2,1,0:T(8,128)(2,1)} %bitcast.231, bf16[4,2,512,384]{3,2,1,0:T(8,128)(2,1)} %get-tuple-element.53.refs_1_, bf16[4,2,128,384]{3,2,1,0:T(8,128)(2,1)S(1)} %bitcast.253, bf16[2,4,96,512]{3,2,1,0:T(8,128)(2,1)} %copy-done.19, ...), custom_call_target="tpu_custom_call" | custom-call | tf_op jit(solution)/shard_map/pallas_call | solution.py:343
  599.0 2.7 convolution_bitcast_fusion.1
  603.9 3.1 collective-permute-start.22
  607.0 5.7 convolution_convert_fusion.1
  612.8 2.5 collective-permute-start.20
  615.2 3.0 add_convert_fusion.5
  620.7 102.9 %shard_map.247 = (bf16[2,128,1536]{2,1,0:T(8,128)(2,1)S(1)}, f32[1,1536]{1,0:T(1,128)S(1)}, bf16[2,8,32,1536]{3,2,1,0:T(8,128)(2,1)}, bf16[2,3,32,1536]{3,2,1,0:...) custom-call(bf16[4,2,128,1536]{3,2,1,0:T(8,128)(2,1)} %bitcast.267, ...), custom_call_target="tpu_custom_call" | custom-call | tf_op jit(solution)/shard_map/pallas_call | solution.py:343
  723.7 5.6 fusion.57
  733.5 8.6 multiply_convert_fusion
  742.1 5.3 fusion.56
  747.4 3.5 fusion.55
  752.1 5.5 fusion.20
  757.6 9.5 add_convert_fusion
  767.1 1.8 add_convert_fusion.3
  768.9 1.7 add_convert_fusion.4
  770.6 97.3 %shard_map.248 = (f32[2,128,1536]{2,1,0:T(8,128)S(1)}, f32[1,1536]{1,0:T(1,128)S(1)}, bf16[2,8,48,1024]{3,2,1,0:T(8,128)(2,1)S(1)}, bf16[2,8,48,1024]{3,2,1,0:T(8,128)(2,1)}, bf16[4,2,128,1536]{3,2,1,0:T(8,128)(2,1)}) custom-call(bf16[4,2,128,1536]{3,2,1,0:T(8,128)(2,1)} %bitcast.276, f32[2,128,1536]{2,1,0:T(8,128)} %copy-done.7, ...), custom_call_target="tpu_custom_call" | custom-call | tf_op jit(solution)/shard_map/pallas_call | solution.py:343
  868.0 4.6 convolution_convert_fusion.7
  872.6 61.1 %shard_map.249 = bf16[4,2,128,768]{3,2,1,0:T(8,128)(2,1)} custom-call(bf16[4,2,128,768]{3,2,1,0:T(8,128)(2,1)} %bitcast.229, bf16[4,2,512,384]{3,2,1,0:T(8,128)(2,1)} %get-tuple-element.63.refs_1_, bf16[4,2,128,384]{3,2,1,0:T(8,128)(2,1)S(1)} %bitcast.252, bf16[2,4,96,512]{3,2,1,0:T(8,128)(2,1)S(1)} %copy-done.18, ...), custom_call_target="tpu_custom_call" | custom-call | tf_op jit(solution)/shard_map/pallas_call | solution.py:343
  933.7 4.2 convolution_bitcast_fusion
  941.7 4.0 add_convert_fusion.2
  945.7 5.6 convolution_convert_fusion
  953.2 113.8 %shard_map.250 = (f32[2,128,1536]{2,1,0:T(8,128)}, f32[8,1536]{1,0:T(8,128)S(1)}, bf16[2,8,32,1536]{3,2,1,0:T(8,128)(2,1)}, bf16[2,3,32,1536]{3,2,1,0:T(8,128)(2,1)S(1)}, bf16[2,6,64,768]{3,2,1,0:T(8,128)(2,1)S(1)}) custom-call(bf16[4,2,128,1536]{3,2,1,0:T(8,128)(2,1)} %bitcast.274, f32[2,128,1536]{2,1,0:T(8,128)} %copy-done.2, f32[1,1536]{1,0:T(1,128)S(1)} %copy-done.21, ...), custom_call_target="tpu_custom_call" | custom-call | tf_op jit(solution)/shard_map/pallas_call | solution.py:343
  1069.2 2.2 collective-permute-start.16
  1074.6 4.6 fusion.17
  1079.3 2.0 collective-permute-start.18
  1083.9 4.2 collective-permute-start.24
  1088.1 4.5 fusion.16
  1093.9 1.8 fusion.35
  1096.7 1.7 copy-done.24
  1101.3 3.2 slice_bitcast_fusion.18
  1104.5 4.9 fusion.18
  (261 shorter events, 57.8 us)
Async XLA Ops:
  7.2 61.8 %all-gather.17.cloned.1.call-start = ((), (), s32[]{:S(2)}) async-start(), calls=%async_computation.4 | async-start | bytes 14155776 | tf_op jit(solution)/shard_map/all_gather | solution.py:1025
  15.6 132.5 %all-gather.9.cloned.1.call-start = ((), (), s32[]{:S(2)}) async-start(), calls=%async_computation | async-start | bytes 3538944 | tf_op jit(solution)/shard_map/all_gather | solution.py:1025
  16.3 172.2 %all-gather.11.cloned.1.call-start = ((), (), s32[]{:S(2)}) async-start(), calls=%async_computation.1 | async-start | bytes 9437184 | tf_op jit(solution)/shard_map/all_gather | solution.py:1025
  17.1 179.7 %all-gather.13.cloned.1.call-start = ((), (), s32[]{:S(2)}) async-start(), calls=%async_computation.2 | async-start | bytes 9437184 | tf_op jit(solution)/shard_map/all_gather | solution.py:1025
  17.6 189.5 %all-gather.15.cloned.1.call-start = ((), (), s32[]{:S(2)}) async-start(), calls=%async_computation.3 | async-start | bytes 9437184 | tf_op jit(solution)/shard_map/all_gather | solution.py:1025
  18.6 13.3 %collective-permute-start = (bf16[2,128,768]{2,1,0:T(8,128)(2,1)}, bf16[2,128,768]{2,1,0:T(8,128)(2,1)}, u32[]{:S(2)}, u32[]{:S(2)}) collective-permute-start(bf16[2,128,768]{2,1,0:T(8,128)(2,1)} %get-tuple-element.144), channel_id=1, source_target_pairs={{0,16},{16,0},{1,17},{17,1},{2,18},{18,2},{3,19},{19,3},{4,20},{20... | collective-permute-start | bytes 1179656 | tf_op jit(solution)/shard_map/ppermute | solution.py:971
  19.9 46.3 %collective-permute-start.1 = (bf16[2,128,768]{2,1,0:T(8,128)(2,1)}, bf16[2,128,768]{2,1,0:T(8,128)(2,1)}, u32[]{:S(2)}, u32[]{:S(2)}) collective-permute-start(bf16[2,128,768]{2,1,0:T(8,128)(2,1)} %get-tuple-element.140), channel_id=1, source_target_pairs={{0,16},{16,0},{1,17},{17,1},{2,18},{18,2},{3,19},{19,3},{4,20},{20... | collective-permute-start | bytes 1179656 | tf_op jit(solution)/shard_map/ppermute | solution.py:971
  25.1 6.7 copy-start.5
  25.3 6.5 copy-start.3
  33.3 33.0 %copy-start.36 = (bf16[2,128,768]{2,1,0:T(8,128)(2,1)S(1)}, bf16[2,128,768]{2,1,0:T(8,128)(2,1)}, u32[]{:S(2)}) copy-start(bf16[2,128,768]{2,1,0:T(8,128)(2,1)} %get-tuple-element.139) | copy-start | bytes 1179652
  33.5 119.5 %copy-start.2 = (f32[2,128,1536]{2,1,0:T(8,128)}, f32[2,128,1536]{2,1,0:T(8,128)S(1)}, u32[]{:S(2)}) copy-start(f32[2,128,1536]{2,1,0:T(8,128)S(1)} %get-tuple-element.122.h.refs_1_) | copy-start | bytes 4718596
  69.0 8.3 copy-start.22
  69.0 8.3 copy-start.37
  69.0 8.3 copy-start.40
  69.0 8.3 copy-start.44
  207.1 7.7 copy-start.8
  248.9 60.1 %copy-start.9 = (f32[2,128,1536]{2,1,0:T(8,128)}, f32[2,128,1536]{2,1,0:T(8,128)S(1)}, u32[]{:S(2)}) copy-start(f32[2,128,1536]{2,1,0:T(8,128)S(1)} %get-tuple-element.56.h.refs_1_) | copy-start | bytes 4718596
  248.9 8.5 copy-start.23
  249.0 8.5 copy-start.25
  258.3 50.7 %copy-start.1 = (bf16[1024,768]{1,0:T(8,128)(2,1)}, bf16[1024,768]{1,0:T(8,128)(2,1)S(1)}, u32[]{:S(2)}) copy-start(bf16[1024,768]{1,0:T(8,128)(2,1)S(1)} %fusion.13) | copy-start | bytes 4718596
  304.0 5.0 copy-start.19
  343.0 6.9 copy-start.10
  343.0 6.9 copy-start.51
  343.0 13.9 %slice-start.6 = ((s8[6291456]{0:T(1024)(128)(4,1)}), s8[4194304]{0:T(1024)(128)(4,1)S(1)}, s32[]{:S(2)}) async-start(s8[6291456]{0:T(1024)(128)(4,1)} %bitcast.292), calls=%async_computation.11 | async-start | bytes 8388608
  349.9 7.1 slice-start.7
  349.9 7.0 copy-start.50
  368.8 33.6 %copy-start.27 = (f32[1024,1536]{1,0:T(8,128)}, f32[1024,1536]{1,0:T(8,128)S(1)}, u32[]{:S(2)}) copy-start(f32[1024,1536]{1,0:T(8,128)S(1)} %fusion.54) | copy-start | bytes 18874372
  368.8 30.1 %copy-start.58 = (bf16[1024,1024]{1,0:T(8,128)(2,1)S(1)}, bf16[1024,1024]{1,0:T(8,128)(2,1)}, u32[]{:S(2)}) copy-start(bf16[1024,1024]{1,0:T(8,128)(2,1)} %get-tuple-element.127) | copy-start | bytes 6291460
  370.1 242.6 %collective-permute-start.5 = (bf16[512,1536]{1,0:T(8,128)(2,1)}, bf16[512,1536]{1,0:T(8,128)(2,1)}, u32[]{:S(2)}, u32[]{:S(2)}) collective-permute-start(bf16[512,1536]{1,0:T(8,128)(2,1)} %dynamic-slice_convert_fusion.3), channel_id=1, source_target_pairs={{0,16},{16,0},{1,17},{17,1},{2,18},{18,2},{3,19},{19,3},{4,20},{20... | collective-permute-start | bytes 4718600 | tf_op jit(solution)/shard_map/ppermute | solution.py:971
  402.7 25.9 %collective-permute-start.2 = (bf16[768,1024]{1,0:T(8,128)(2,1)S(1)}, bf16[768,1024]{1,0:T(8,128)(2,1)S(1)}, u32[]{:S(2)}, u32[]{:S(2)}) collective-permute-start(bf16[768,1024]{1,0:T(8,128)(2,1)S(1)} %dynamic-slice_convert_fusion.5), channel_id=1, source_target_pairs={{0,16},{16,0},{1,17},{17,1},{2,18},{18,2},{3,19},{19,3},{4,20},{20... | collective-permute-start | bytes 4718600 | tf_op jit(solution)/shard_map/ppermute | solution.py:971
  408.1 7.2 slice-start.2
  408.4 7.0 slice-start.3
  408.4 21.9 %collective-permute-start.3 = (bf16[768,1024]{1,0:T(8,128)(2,1)S(1)}, bf16[768,1024]{1,0:T(8,128)(2,1)S(1)}, u32[]{:S(2)}, u32[]{:S(2)}) collective-permute-start(bf16[768,1024]{1,0:T(8,128)(2,1)S(1)} %dynamic-slice_convert_fusion.4), channel_id=1, source_target_pairs={{0,16},{16,0},{1,17},{17,1},{2,18},{18,2},{3,19},{19,3},{4,20},{20... | collective-permute-start | bytes 4718600 | tf_op jit(solution)/shard_map/ppermute | solution.py:971
  432.1 97.0 %copy-start.52 = (bf16[2,384,1536]{2,1,0:T(8,128)(2,1)S(1)}, bf16[2,384,1536]{2,1,0:T(8,128)(2,1)}, u32[]{:S(2)}) copy-start(bf16[2,384,1536]{2,1,0:T(8,128)(2,1)} %all-gather.9.cloned.1.call-done) | copy-start | bytes 7077892
  596.9 21.4 %collective-permute-start.4 = (bf16[2,128,768]{2,1,0:T(8,128)(2,1)S(1)}, bf16[2,128,768]{2,1,0:T(8,128)(2,1)S(1)}, u32[]{:S(2)}, u32[]{:S(2)}) collective-permute-start(bf16[2,128,768]{2,1,0:T(8,128)(2,1)S(1)} %get-tuple-element.134), channel_id=1, source_target_pairs={{0,16},{16,0},{1,17},{17,1},{2,18},{18,2},{3,19},{19,3},{4,20},{20... | collective-permute-start | bytes 1179656 | tf_op jit(solution)/shard_map/ppermute | solution.py:971
  601.8 17.6 %collective-permute-start.7 = (bf16[768,768]{1,0:T(8,128)(2,1)S(1)}, bf16[768,768]{1,0:T(8,128)(2,1)S(1)}, u32[]{:S(2)}, u32[]{:S(2)}) collective-permute-start(bf16[768,768]{1,0:T(8,128)(2,1)S(1)} %dynamic-slice_convert_fusion.7), channel_id=1, source_target_pairs={{0,16},{16,0},{1,17},{17,1},{2,18},{18,2},{3,19},{19,3},{4,20},{20... | collective-permute-start | bytes 3538952 | tf_op jit(solution)/shard_map/ppermute | solution.py:971
  601.9 13.3 %slice-start = ((s8[6291456]{0:T(1024)(128)(4,1)}), s8[4194304]{0:T(1024)(128)(4,1)S(1)}, s32[]{:S(2)}) async-start(s8[6291456]{0:T(1024)(128)(4,1)} %bitcast.265), calls=%async_computation.5 | async-start | bytes 8388608
  603.4 15.9 %collective-permute-start.6 = (bf16[192,1536]{1,0:T(8,128)(2,1)S(1)}, bf16[192,1536]{1,0:T(8,128)(2,1)S(1)}, u32[]{:S(2)}, u32[]{:S(2)}) collective-permute-start(bf16[192,1536]{1,0:T(8,128)(2,1)S(1)} %dynamic-slice_convert_fusion.9), channel_id=1, source_target_pairs={{0,16},{16,0},{1,17},{17,1},{2,18},{18,2},{3,19},{19,3},{4,20},{20... | collective-permute-start | bytes 1769480 | tf_op jit(solution)/shard_map/ppermute | solution.py:971
  603.9 468.1 %collective-permute-start.22 = (bf16[768,1024]{1,0:T(8,128)(2,1)S(1)}, bf16[768,1024]{1,0:T(8,128)(2,1)}, u32[]{:S(2)}, u32[]{:S(2)}) collective-permute-start(bf16[768,1024]{1,0:T(8,128)(2,1)S(1)} %bitcast.277), channel_id=1, source_target_pairs={{0,16},{1,17},{2,18},{3,19},{4,20},{5,21},{6,22},{7,23},{8,24},{9,... | collective-permute-start | bytes 4718600 | tf_op jit(solution)/shard_map/ppermute | solution.py:1162
  607.0 8.2 slice-start.1
  612.8 466.5 %collective-permute-start.20 = (bf16[768,1024]{1,0:T(8,128)(2,1)S(1)}, bf16[768,1024]{1,0:T(8,128)(2,1)}, u32[]{:S(2)}, u32[]{:S(2)}) collective-permute-start(bf16[768,1024]{1,0:T(8,128)(2,1)S(1)} %bitcast.242), channel_id=1, source_target_pairs={{0,16},{1,17},{2,18},{3,19},{4,20},{5,21},{6,22},{7,23},{8,24},{9,... | collective-permute-start | bytes 4718600 | tf_op jit(solution)/shard_map/ppermute | solution.py:1162
  620.7 103.0 %copy-start.56 = (bf16[1024,1024]{1,0:T(8,128)(2,1)S(1)}, bf16[1024,1024]{1,0:T(8,128)(2,1)}, u32[]{:S(2)}) copy-start(bf16[1024,1024]{1,0:T(8,128)(2,1)} %get-tuple-element.155) | copy-start | bytes 6291460
  723.6 9.8 copy-start.57
  723.6 9.8 copy-start.60
  733.5 206.8 %collective-permute-start.10 = (bf16[512,1536]{1,0:T(8,128)(2,1)}, bf16[512,1536]{1,0:T(8,128)(2,1)}, u32[]{:S(2)}, u32[]{:S(2)}) collective-permute-start(bf16[512,1536]{1,0:T(8,128)(2,1)} %dynamic-slice_convert_fusion), channel_id=1, source_target_pairs={{0,16},{16,0},{1,17},{17,1},{2,18},{18,2},{3,19},{19,3},{4,20},{20... | collective-permute-start | bytes 4718600 | tf_op jit(solution)/shard_map/ppermute | solution.py:971
  733.5 8.6 copy-start.47
  742.1 5.3 copy-start.59
  742.1 10.0 slice-start.4
  751.5 15.6 %collective-permute-start.9 = (bf16[768,1024]{1,0:T(8,128)(2,1)S(1)}, bf16[768,1024]{1,0:T(8,128)(2,1)S(1)}, u32[]{:S(2)}, u32[]{:S(2)}) collective-permute-start(bf16[768,1024]{1,0:T(8,128)(2,1)S(1)} %dynamic-slice_convert_fusion.1), channel_id=1, source_target_pairs={{0,16},{16,0},{1,17},{17,1},{2,18},{18,2},{3,19},{19,3},{4,20},{20... | collective-permute-start | bytes 4718600 | tf_op jit(solution)/shard_map/ppermute | solution.py:971
  752.0 16.8 %collective-permute-start.8 = (bf16[768,1024]{1,0:T(8,128)(2,1)S(1)}, bf16[768,1024]{1,0:T(8,128)(2,1)S(1)}, u32[]{:S(2)}, u32[]{:S(2)}) collective-permute-start(bf16[768,1024]{1,0:T(8,128)(2,1)S(1)} %dynamic-slice_convert_fusion.2), channel_id=1, source_target_pairs={{0,16},{16,0},{1,17},{17,1},{2,18},{18,2},{3,19},{19,3},{4,20},{20... | collective-permute-start | bytes 4718600 | tf_op jit(solution)/shard_map/ppermute | solution.py:971
  872.6 61.1 %copy-start.12 = (bf16[4,2,128,1536]{3,2,1,0:T(8,128)(2,1)S(1)}, bf16[4,2,128,1536]{3,2,1,0:T(8,128)(2,1)}, u32[]{:S(2)}) copy-start(bf16[4,2,128,1536]{3,2,1,0:T(8,128)(2,1)} %copy-done.11) | copy-start | bytes 9437188
  938.1 14.8 %collective-permute-start.12 = (bf16[768,768]{1,0:T(8,128)(2,1)S(1)}, bf16[768,768]{1,0:T(8,128)(2,1)S(1)}, u32[]{:S(2)}, u32[]{:S(2)}) collective-permute-start(bf16[768,768]{1,0:T(8,128)(2,1)S(1)} %dynamic-slice_convert_fusion.6), channel_id=1, source_target_pairs={{0,16},{16,0},{1,17},{17,1},{2,18},{18,2},{3,19},{19,3},{4,20},{20... | collective-permute-start | bytes 3538952 | tf_op jit(solution)/shard_map/ppermute | solution.py:971
  939.7 11.6 %collective-permute-start.11 = (bf16[192,1536]{1,0:T(8,128)(2,1)S(1)}, bf16[192,1536]{1,0:T(8,128)(2,1)S(1)}, u32[]{:S(2)}, u32[]{:S(2)}) collective-permute-start(bf16[192,1536]{1,0:T(8,128)(2,1)S(1)} %dynamic-slice_convert_fusion.8), channel_id=1, source_target_pairs={{0,16},{16,0},{1,17},{17,1},{2,18},{18,2},{3,19},{19,3},{4,20},{20... | collective-permute-start | bytes 1769480 | tf_op jit(solution)/shard_map/ppermute | solution.py:971
  940.3 5.4 copy-start.35
  940.3 133.1 %collective-permute-start.21 = (bf16[768,1024]{1,0:T(8,128)(2,1)S(1)}, bf16[768,1024]{1,0:T(8,128)(2,1)}, u32[]{:S(2)}, u32[]{:S(2)}) collective-permute-start(bf16[768,1024]{1,0:T(8,128)(2,1)S(1)} %bitcast.279), channel_id=1, source_target_pairs={{16,0},{17,1},{18,2},{19,3},{20,4},{21,5},{22,6},{23,7},{24,8},{25... | collective-permute-start | bytes 4718600 | tf_op jit(solution)/shard_map/ppermute | solution.py:1161
  951.3 132.5 %collective-permute-start.19 = (bf16[768,1024]{1,0:T(8,128)(2,1)S(1)}, bf16[768,1024]{1,0:T(8,128)(2,1)S(1)}, u32[]{:S(2)}, u32[]{:S(2)}) collective-permute-start(bf16[768,1024]{1,0:T(8,128)(2,1)S(1)} %bitcast.244), channel_id=1, source_target_pairs={{16,0},{17,1},{18,2},{19,3},{20,4},{21,5},{22,6},{23,7},{24,8},{25... | collective-permute-start | bytes 4718600 | tf_op jit(solution)/shard_map/ppermute | solution.py:1161
  1067.0 2.2 collective-permute-start.14
  1069.2 26.4 %collective-permute-start.16 = (bf16[768,768]{1,0:T(8,128)(2,1)S(1)}, bf16[768,768]{1,0:T(8,128)(2,1)S(1)}, u32[]{:S(2)}, u32[]{:S(2)}) collective-permute-start(bf16[768,768]{1,0:T(8,128)(2,1)S(1)} %bitcast.246), channel_id=1, source_target_pairs={{0,16},{1,17},{2,18},{3,19},{4,20},{5,21},{6,22},{7,23},{8,24},{9,... | collective-permute-start | bytes 3538952 | tf_op jit(solution)/shard_map/ppermute | solution.py:1162
  1072.0 23.6 %collective-permute-start.15 = (bf16[768,768]{1,0:T(8,128)(2,1)S(1)}, bf16[768,768]{1,0:T(8,128)(2,1)S(1)}, u32[]{:S(2)}, u32[]{:S(2)}) collective-permute-start(bf16[768,768]{1,0:T(8,128)(2,1)S(1)} %bitcast.248), channel_id=1, source_target_pairs={{16,0},{17,1},{18,2},{19,3},{20,4},{21,5},{22,6},{23,7},{24,8},{25... | collective-permute-start | bytes 3538952 | tf_op jit(solution)/shard_map/ppermute | solution.py:1161
  1073.3 7.9 collective-permute-start.13
  1079.3 13.3 %collective-permute-start.18 = (bf16[192,1536]{1,0:T(8,128)(2,1)S(1)}, bf16[192,1536]{1,0:T(8,128)(2,1)S(1)}, u32[]{:S(2)}, u32[]{:S(2)}) collective-permute-start(bf16[192,1536]{1,0:T(8,128)(2,1)S(1)} %bitcast.254), channel_id=1, source_target_pairs={{0,16},{1,17},{2,18},{3,19},{4,20},{5,21},{6,22},{7,23},{8,24},{9,... | collective-permute-start | bytes 1769480 | tf_op jit(solution)/shard_map/ppermute | solution.py:1162
  1081.2 12.6 %collective-permute-start.17 = (bf16[192,1536]{1,0:T(8,128)(2,1)S(1)}, bf16[192,1536]{1,0:T(8,128)(2,1)S(1)}, u32[]{:S(2)}, u32[]{:S(2)}) collective-permute-start(bf16[192,1536]{1,0:T(8,128)(2,1)S(1)} %bitcast.256), channel_id=1, source_target_pairs={{16,0},{17,1},{18,2},{19,3},{20,4},{21,5},{22,6},{23,7},{24,8},{25... | collective-permute-start | bytes 1769480 | tf_op jit(solution)/shard_map/ppermute | solution.py:1161
  1083.9 20.7 %collective-permute-start.24 = (bf16[512,1536]{1,0:T(8,128)(2,1)}, bf16[512,1536]{1,0:T(8,128)(2,1)}, u32[]{:S(2)}, u32[]{:S(2)}) collective-permute-start(bf16[512,1536]{1,0:T(8,128)(2,1)} %bitcast.108), channel_id=1, source_target_pairs={{0,16},{1,17},{2,18},{3,19},{4,20},{5,21},{6,22},{7,23},{8,24},{9,... | collective-permute-start | bytes 4718600 | tf_op jit(solution)/shard_map/ppermute | solution.py:1162
  1092.6 12.0 %collective-permute-start.23 = (bf16[512,1536]{1,0:T(8,128)(2,1)}, bf16[512,1536]{1,0:T(8,128)(2,1)}, u32[]{:S(2)}, u32[]{:S(2)}) collective-permute-start(bf16[512,1536]{1,0:T(8,128)(2,1)} %bitcast.106), channel_id=1, source_target_pairs={{16,0},{17,1},{18,2},{19,3},{20,4},{21,5},{22,6},{23,7},{24,8},{25... | collective-permute-start | bytes 4718600 | tf_op jit(solution)/shard_map/ppermute | solution.py:1161
  (35 other events, 98.5 us)
Sparse Core Ops, SparseCore 0:
  15.7 24.5 all-gather.16
  41.8 12.1 all-gather.8
  55.5 17.9 all-gather.10
  74.9 17.9 all-gather.12
  94.2 17.9 all-gather.14

commit v4 on v3

--- a/solution.py
+++ b/solution.py
@@ -369,7 +369,7 @@
         v = h[j, at].astype(F32)
         full[t, j, at] = (v * inverse_rms(v) * gain[...]).astype(BF)
 
-    run_exchange(h.shape[1], None, finish, full, None, None, None, sems)
+    run_exchange(h.shape[1], None, finish, full, None, None, None, sems, turns=True)
 
 
 def norm_gather(h, gain):
@@ -404,6 +404,25 @@
     )
 
 
+def chain_kernel(count, *refs):
+    zs, outs, gots = refs[:count], refs[count : 2 * count], refs[2 * count : 3 * count]
+    chain = Chain(zs, gots, outs, refs[3 * count :])
+    greet(tensor=False, line=True)
+    for time in range(chain.slots):
+        chain.slot(time)
+    chain.drain()
+
+
+def chain_sum(zs):
+    return call(
+        functools.partial(chain_kernel, len(zs)),
+        tuple(jax.ShapeDtypeStruct(z.shape, BF) for z in zs),
+        chain_scratch(zs),
+        13,
+        *zs,
+    )
+
+
 def line_sum(own, rows, sems):
     c, _, has_left, has_right = ctx_ends()
     sides = ((has_left, has_right, c + 1, 0), (has_right, has_left, c - 1, 1))
@@ -449,10 +468,10 @@
     full = take(1)[0] if kind != 2 else None
     got, held, s0, s1, rows, gs, gr = take(7)
     z_got = take(count)
-    z_sems = take(4)
+    z_sems = take(4) if count else None
     ga = take(2) if kind != 2 else None
     line = take(3) if kind == 2 else None
-    chain = Chain(zs, z_got, z_out, z_sems)
+    chain = Chain(zs, z_got, z_out, z_sems) if count else None
     rows[0] = jnp.zeros_like(rows[0])
 
     def finish(j, at, term):
@@ -490,7 +509,7 @@
         dgain[...] = total
 
 
-def back(part, h, gain, g, kind, zs, others=None):
+def back(part, h, gain, g, kind, ident, zs, others=None):
     wide, full, row, narrow = shapes_of(h)
     _, sp, d = h.shape
     row = jax.ShapeDtypeStruct((8, d), F32) if kind == 2 else row
@@ -500,7 +519,7 @@
         pltpu.VMEM((4, 8, d), F32),
         pltpu.SemaphoreType.DMA((2,)),
         pltpu.SemaphoreType.DMA((2,)),
-    ] + chain_scratch(zs)
+    ] + (chain_scratch(zs) if zs else [])
     if kind != 2:
         out += (full,)
         scratch += gather_scratch(sp)
@@ -512,7 +531,7 @@
         ]
     operands = (part, h, gain, g) + (() if others is None else (others,)) + tuple(zs)
     res = call(
-        functools.partial(back_kernel, kind, len(zs)), out, scratch, 5 + kind, *operands
+        functools.partial(back_kernel, kind, len(zs)), out, scratch, ident, *operands
     )
     return res[0], res[1], res[2 : 2 + len(zs)], res[2 + len(zs) :]
 
@@ -1095,23 +1114,17 @@
         part = nt(dqkv, wcat2[layer][:, :qkv_w]).astype(BF)
         return part.reshape(n_t, 2, sp, d), dqkv, more
 
-    def exchange(*grads):
-        out = []
-        for g in grads:
-            size = g.shape[0] // 2
-            give = lax.dynamic_slice_in_dim(g, (1 - sec) * size, size, 0).astype(BF)
-            keep = lax.dynamic_slice_in_dim(g, sec * size, size, 0)
-            out.append((keep, swap(give)))
-        return out
-
-    def terms(halves):
-        return [(keep + got.astype(F32)).astype(BF) for keep, got in halves]
+    def halve(*grads):
+        return [lax.psum_scatter(g, "section", scatter_dimension=0, tiled=True) for g in grads]
+
+    def grad(left, right):
+        return tn(left, right).astype(BF)
 
     def cut(size, term):
         return term.reshape(2, -1, size, term.shape[1])
 
-    def tie(x, others):
-        return lax.optimization_barrier((x, others))
+    def tie(*values):
+        return lax.optimization_barrier(values)
 
     flat = lambda v: v.reshape(rows, d)
     a0, a1, m0, m1 = gain_of(0, 0), gain_of(1, 0), gain_of(0, 1), gain_of(1, 1)
@@ -1130,38 +1143,50 @@
     y_part, mlp1 = feed(n2_1, 1)
 
     gm1 = flat(att1[5])
-    def backward(layer, gm, g, h, h2, n1, n2, att, mlp, kind, a_gain, m_gain, others, *more):
-        part, dgate, dup = feed_back(gm, layer, mlp)
-        wide = exchange(tn(n2, dgate), tn(n2, dup))
-        down = exchange(tn(mlp[2], gm))
-        zs = [cut(48, v) for v in terms(wide)]
-        dh2, dm, wide, (full,) = back(part, h2, m_gain, g, 0, zs)
-        ga = flat(full)
-        out = exchange(tn(att[2], ga))
-        part, dqkv, more = attend_back(ga, layer, att, *more)
-        rest = terms(down + out + exchange(tn(n1, dqkv)))
-        zs = [cut(size, v) for size, v in zip((32, 32, 64), rest)]
-        if others is not None:
-            others = jnp.concatenate([dm, *others], 0)
-        dh, da, rest, full = back(part, h, a_gain, dh2, kind, zs, others)
-        grads = [z.reshape(-1, z.shape[-1]) for z in (rest[0], *wide, *rest[1:])]
-        return dh, full, (da, dm), grads, more
-
-    g0, full, gains1, grads1, (y,) = backward(
-        1, gm1, g_own.astype(F32), h1, h2_1, n1_1, n2_1, att1, mlp1, 1, a1, m1,
-        None, y_part, h2_1,
-    )
-    dh0, _, (gains, _), grads0, _ = backward(
-        0, flat(full[0]), g0.astype(F32), h0, h2_0, n1_0, n2_0, att0, mlp0, 2, a0, m0, gains1
-    )
+    def joined(zs):
+        return [z.reshape(-1, z.shape[-1]) for z in zs]
+
+    part, dgate, dup = feed_back(gm1, 1, mlp1)
+    raw = (grad(n2_1, dgate), grad(n2_1, dup), grad(mlp1[2], gm1))
+    part, raw = tie(part, raw)
+    wide1, down1 = halve(*raw[:2]), halve(raw[2])
+    dh2_1, dm1, _, (full,) = back(part, h2_1, m1, g_own.astype(F32), 0, 5, ())
+    ga = flat(full)
+    part, dqkv, (y,) = attend_back(ga, 1, att1, y_part, h2_1)
+    raw = (grad(att1[2], ga), grad(n1_1, dqkv))
+    part, raw, wide1 = tie(part, raw, wide1)
+    rest1 = down1 + halve(*raw)
+    zs = [cut(48, v) for v in wide1]
+    g0, da1, wide1, (full,) = back(part, h1, a1, dh2_1, 1, 6, zs)
+    gm0 = flat(full)
+    part, dgate, dup = feed_back(gm0, 0, mlp0)
+    raw = (grad(n2_0, dgate), grad(n2_0, dup), grad(mlp0[2], gm0))
+    part, raw, rest1 = tie(part, raw, rest1)
+    wide0 = halve(*raw)
+    zs = [cut(size, v) for size, v in zip((32, 32, 64), rest1)]
+    dh2_0, dm0, rest1, (full,) = back(part, h2_0, m0, g0.astype(F32), 0, 7, zs)
+    ga = flat(full)
+    part, dqkv, _ = attend_back(ga, 0, att0)
+    raw = (grad(att0[2], ga), grad(n1_0, dqkv))
+    part, raw, wide0 = tie(part, raw, wide0)
+    rest0 = halve(*raw)
+    zs = [cut(size, v) for size, v in zip((48, 48, 32), wide0)]
+    others = jnp.concatenate([dm0, da1, dm1], 0)
+    dh0, gains, wide0, _ = back(part, h0, a0, dh2_0, 2, 8, zs, others)
+    rest0, dh0, gains = tie(rest0, dh0, gains)
+    rest0 = chain_sum([cut(size, v) for size, v in zip((32, 64), rest0)])
+    wide1, rest1, wide0, rest0 = joined(wide1), joined(rest1), joined(wide0), joined(rest0)
+    y, dh0, gains, wide1, rest1, wide0, rest0 = tie(y, dh0, gains, wide1, rest1, wide0, rest0)
+    grads1 = (rest1[0], *wide1, *rest1[1:])
+    grads0 = (wide0[2], *wide0[:2], *rest0)
     gains = gains + swap(gains)
     gain_own = lax.dynamic_slice_in_dim(gains, 2 * sec, 2, 0)
 
     def to_owner(r0, r1):
-        got0 = lax.ppermute(r0, "section", [(1, 0)])
-        got1 = lax.ppermute(r1, "section", [(0, 1)])
+        got = swap(jnp.where(first, r1, r0))
+        keep = jnp.where(first, r0, r1)
         return jnp.where(
-            first, jnp.concatenate([r0, got0], 0), jnp.concatenate([got1, r1], 0)
+            first, jnp.concatenate([keep, got], 0), jnp.concatenate([got, keep], 0)
         ).astype(F32)
 
     gd, gg, gu, go, gqkv = (to_owner(a, b) for a, b in zip(grads0, grads1))

time: 1120 us -> 1010 us (0.902)
  Pallas kernels: 777 us -> 697 us
  starting transfers between devices: 55.2 us -> 9.45 us
  matrix products: 187 us -> 201 us
    pallas_call x12 -> x13, Pallas kernels: 777 us -> 697 us  [call(): pl.pallas_call(kernel, out_shape=out_shape, in_specs=[vm] * len(operands)...]
    ppermute x15 -> x10, starting transfers between devices: 34.4 us -> 8.68 us  [swap(): return lax.ppermute(value, 'section', [(0, 1), (1, 0)])]
    ppermute x10 -> x0, starting transfers between devices: 20.5 us -> none  [the longest x5 13.9 us: to_owner(): got1 = lax.ppermute(r1, 'section', [(0, 1)])]
    dot_general x10, matrix products: 34.8 us -> 52.8 us  [tn(): lax.dot_general(a, b, (((0,), (0,)), ((), ())), preferred_element_type=F32)]
    convert_element_type x17 -> x7, other arithmetic: 34.9 us -> 19.2 us  [the longest x5 16.3 us: to_owner(): return jnp.where(first, jnp.concatenate([keep, got], 0), jnp.concatenate(...]
    unnamed x144 -> x182, local copies, waits for them, and re-layouts: 18.8 us -> 26.6 us
  transfers between devices with their start and end apart: 30 -> 25, of which waited for: 0 -> 0; matrix products, arithmetic and copies ran while one was open for 17% -> 17% of each run, Pallas kernels for 59% -> 53%
where the time goes in v4:
time: 1010 us; the launch traced here: 1000 us
  Pallas kernels  697 us (69%)
  matrix products  201 us (20%)
  local copies, waits for them, and re-layouts  37 us (4%)
  other arithmetic  33.1 us (3%)
  between operations  16.1 us (2%)
    pallas_call x13, Pallas kernels, call(): pl.pallas_call(kernel, out_shape=out_shape, in_specs=[vm] * len(operands)...  697 us
    dot_general x13, matrix products, nn(): lax.dot_general(a, b, (((1,), (0,)), ((), ())), preferred_element_type=F32)  75.9 us
    dot_general x10, matrix products, nt(): lax.dot_general(a, b, (((1,), (1,)), ((), ())), preferred_element_type=F32)  63.5 us
    dot_general x10, matrix products, tn(): lax.dot_general(a, b, (((0,), (0,)), ((), ())), preferred_element_type=F32)  52.8 us
    unnamed x182, local copies, waits for them, and re-layouts  26.6 us
  transfers between devices with their start and end apart: 25, of which 0 were waited for; matrix products, arithmetic and copies ran while one was open for 17% of the time, Pallas kernels for 53%

profile of v4, /device:TPU:0, one launch (start us, length us, event | category | flops | bytes accessed | tf_op | source)
XLA Modules:
  0.0 1001.0 jit_solution(15680804547410661625)
XLA Ops:
  7.2 1.6 copy.66
  12.2 1.8 fusion.31
  14.1 1.5 fusion.33
  21.4 1.9 all-gather.2
  23.6 1.4 fusion.43
  27.4 4.3 fusion.53
  33.4 19.4 %shard_map.239 = bf16[4,2,128,1536]{3,2,1,0:T(8,128)(2,1)S(1)} custom-call(bf16[2,128,1536]{2,1,0:T(8,128)(2,1)S(1)} %get-tuple-element.201.h, f32[1,1536]{1,0:T(1,128)S(1)} %get-tuple-element.238.gain.refs_2_), custom_call_target="tpu_custom_call" | custom-call | tf_op jit(solution)/shard_map/pallas_call | solution.py:343
  52.8 1.7 copy-done.14
  56.0 1.6 fusion.46
  57.6 8.1 fusion.2
  65.7 4.7 fusion.15
  70.4 55.0 %shard_map.240 = (bf16[4,2,128,384]{3,2,1,0:T(8,128)(2,1)S(1)}, bf16[2,4,96,512]{3,2,1,0:T(8,128)(2,1)S(1)}, f32[2,4,1,512]{3,2,1,0:T(1,128)S(1)}, bf16[4,2,512,384]{3,2,1,0:T(8,128)(2,1)}) custom-call(bf16[4,2,128,768]{3,2,1,0:T(8,128)(2,1)S(1)} %bitcast.228), custom_call_target="tpu_custom_call" | custom-call | tf_op jit(solution)/shard_map/pallas_call | solution.py:343
  127.5 5.0 convolution_convert_fusion.3
  132.5 34.9 %shard_map.241 = (f32[2,128,1536]{2,1,0:T(8,128)S(1)}, bf16[4,2,128,1536]{3,2,1,0:T(8,128)(2,1)}) custom-call(bf16[4,2,128,1536]{3,2,1,0:T(8,128)(2,1)} %bitcast.259, f32[2,128,1536]{2,1,0:T(8,128)S(1)} %get-tuple-element.200.h.refs_1_, f32[1,1536]{1,0:T(1,128)S(1)} %get-tuple-element.237.gain.refs_2_), custom_call_target="tpu_custom_call" | custom-call | tf_op jit(solution)/shard_map/pallas_call | solution.py:343
  167.5 8.8 fusion.23
  176.3 10.4 %multiply_convert_fusion.3 = (bf16[1024,1024]{1,0:T(8,128)(2,1)}, f32[1024,1024]{1,0:T(8,128)}) fusion(f32[1024,1024]{1,0:T(8,128)} %fusion.23, bf16[1024,1536]{1,0:T(8,128)(2,1)} %bitcast.287, bf16[2,1536,1024]{2,1,0:T(8,128)(2,1)} %all-gather.13.cloned.1.call-done), kind=kOutput, calls=%fused_computation.21 | convolution fusion | flops 3227516928 | bytes 16777216 | tf_op jit(solution)/shard_map/dot_general | solution.py:20
  186.6 7.6 convolution_convert_fusion.11
  194.2 34.1 %shard_map.242 = (f32[2,128,1536]{2,1,0:T(8,128)S(1)}, bf16[4,2,128,1536]{3,2,1,0:T(8,128)(2,1)}) custom-call(bf16[4,2,128,1536]{3,2,1,0:T(8,128)(2,1)} %bitcast.260, f32[2,128,1536]{2,1,0:T(8,128)S(1)} %get-tuple-element.90.h.refs_1_, f32[1,1536]{1,0:T(1,128)S(1)} %get-tuple-element.236.gain.refs_2_), custom_call_target="tpu_custom_call" | custom-call | tf_op jit(solution)/shard_map/pallas_call | solution.py:343
  228.3 8.5 fusion
  238.0 46.1 %shard_map.243 = (bf16[4,2,128,384]{3,2,1,0:T(8,128)(2,1)S(1)}, bf16[2,4,96,512]{3,2,1,0:T(8,128)(2,1)S(1)}, f32[2,4,1,512]{3,2,1,0:T(1,128)S(1)}, bf16[4,2,512,...) custom-call(bf16[4,2,128,768]{3,2,1,0:T(8,128)(2,1)S(1)} %bitcast.230, bf16[2,128,1536]{2,1,0:T(8,128)(2,1)S(1)} %copy-done.16), custom_call_target="tpu_custom_call" | custom-call | tf_op jit(solution)/shard_map/pallas_call | solution.py:343
  284.1 3.5 convolution_convert_fusion.2
  287.6 34.1 %shard_map.244 = (f32[2,128,1536]{2,1,0:T(8,128)S(1)}, bf16[4,2,128,1536]{3,2,1,0:T(8,128)(2,1)}) custom-call(bf16[4,2,128,1536]{3,2,1,0:T(8,128)(2,1)} %bitcast.258, f32[2,128,1536]{2,1,0:T(8,128)S(1)} %get-tuple-element.95.h.refs_1_, f32[1,1536]{1,0:T(1,128)S(1)} %get-tuple-element.235.gain.refs_2_), custom_call_target="tpu_custom_call" | custom-call | tf_op jit(solution)/shard_map/pallas_call | solution.py:343
  321.8 7.4 fusion.29
  329.2 5.0 fusion.26
  334.3 8.1 multiply_convert_fusion.1
  343.8 5.3 convolution_convert_fusion.10
  349.1 7.7 convolution_convert_fusion.9
  356.7 7.6 convolution_convert_fusion.8
  364.4 6.1 fusion.28
  370.5 6.9 add_convert_fusion.1
  379.0 34.7 %shard_map.245 = (f32[2,128,1536]{2,1,0:T(8,128)S(1)}, f32[1,1536]{1,0:T(1,128)S(1)}, bf16[4,2,128,1536]{3,2,1,0:T(8,128)(2,1)}) custom-call(bf16[4,2,128,1536]{3,2,1,0:T(8,128)(2,1)} %bitcast.255, f32[2,128,1536]{2,1,0:T(8,128)S(1)} %get-tuple-element.98.refs_1_.refs_10_, f32[1,1536]{1,0:T(1,128)S(1)} %get-tuple-element.235.gain.refs_2_, ...), custom_call_target="tpu_custom_call" | custom-call | tf_op jit(solution)/shard_map/pallas_call | solution.py:343
  413.7 4.6 convolution_convert_fusion.14
  418.5 4.8 convolution_convert_fusion.7
  423.3 46.6 %shard_map.246 = (bf16[4,2,128,768]{3,2,1,0:T(8,128)(2,1)}, bf16[2,128,1536]{2,1,0:T(8,128)(2,1)S(1)}) custom-call(bf16[4,2,128,768]{3,2,1,0:T(8,128)(2,1)} %bitcast.231, bf16[4,2,512,384]{3,2,1,0:T(8,128)(2,1)} %get-tuple-element.92.refs_1_, bf16[4,2,128,384]{3,2,1,0:T(8,128)(2,1)S(1)} %bitcast.248, bf16[2,4,96,512]{3,2,1,0:T(8,128)(2,1)} %copy-done.32, ...), custom_call_target="tpu_custom_call" | custom-call | tf_op jit(solution)/shard_map/pallas_call | solution.py:343
  469.8 2.4 fusion.19
  472.3 6.6 convolution_convert_fusion.1
  478.8 3.9 bitcast_convert_fusion.1
  482.9 78.4 %shard_map.247 = (bf16[2,128,1536]{2,1,0:T(8,128)(2,1)S(1)}, f32[1,1536]{1,0:T(1,128)S(1)}, bf16[2,8,48,1024]{3,2,1,0:T(8,128)(2,1)S(1)}, bf16[2,8,48,1024]{3,2,1,0:T(8,128)(2,1)S(1)}, bf16[4,2,128,1536]{3,2,1,0:T(8,128)(2,1)}) custom-call(bf16[4,2,128,1536]{3,2,1,0:T(8,128)(2,1)} %bitcast.262, f32[2,128,1536]{2,1,0:T(8,128)} %copy-done.12, ...), custom_call_target="tpu_custom_call" | custom-call | tf_op jit(solution)/shard_map/pallas_call | solution.py:343
  563.6 6.8 convolution_convert_fusion.4
  570.4 11.4 %multiply_convert_fusion = (bf16[1024,1024]{1,0:T(8,128)(2,1)}, bf16[1024,1024]{1,0:T(8,128)(2,1)S(1)}) fusion(f32[1024,1024]{1,0:T(8,128)} %fusion.23, f32[1024,1024]{1,0:T(8,128)} %get-tuple-element.244, bf16[1024,1536]{1,0:T(8,128)(2,1)} %bitcast.294, bf16[2,1024,1536]{2,1,0:T(8,128)(2,1)} %all-gather.15.cloned.1.call-done), kind=kOutput, calls=%fused_computation.16 | convolution fusion | flops 3235905536 | bytes 18874368 | tf_op jit(solution)/shard_map/dot_general | solution.py:24
  583.1 5.1 convolution_convert_fusion.6
  588.1 7.7 convolution_convert_fusion.5
  595.8 6.1 fusion.22
  601.9 7.0 add_convert_fusion
  613.0 82.6 %shard_map.248 = (f32[2,128,1536]{2,1,0:T(8,128)}, f32[1,1536]{1,0:T(1,128)S(1)}, bf16[2,8,32,1536]{3,2,1,0:T(8,128)(2,1)}, bf16[2,3,32,1536]{3,2,1,0:T(8,128)(2...) custom-call(bf16[4,2,128,1536]{3,2,1,0:T(8,128)(2,1)} %bitcast.254, ...), custom_call_target="tpu_custom_call" | custom-call | tf_op jit(solution)/shard_map/pallas_call | solution.py:343
  695.7 4.1 convolution_convert_fusion.13
  699.9 44.0 %shard_map.249 = bf16[4,2,128,768]{3,2,1,0:T(8,128)(2,1)} custom-call(bf16[4,2,128,768]{3,2,1,0:T(8,128)(2,1)} %bitcast.229, bf16[4,2,512,384]{3,2,1,0:T(8,128)(2,1)} %get-tuple-element.103.refs_1_, bf16[4,2,128,384]{3,2,1,0:T(8,128)(2,1)S(1)} %bitcast.249, bf16[2,4,96,512]{3,2,1,0:T(8,128)(2,1)S(1)} %copy-done.31, ...), custom_call_target="tpu_custom_call" | custom-call | tf_op jit(solution)/shard_map/pallas_call | solution.py:343
  743.9 2.4 fusion.20
  746.4 5.7 convolution_convert_fusion
  752.1 3.9 bitcast_convert_fusion
  756.7 138.3 %shard_map.250 = (f32[2,128,1536]{2,1,0:T(8,128)S(1)}, f32[8,1536]{1,0:T(8,128)S(1)}, bf16[2,8,48,1024]{3,2,1,0:T(8,128)(2,1)S(1)}, bf16[2,8,48,1024]{3,2,1,0:T(8,128)(2,1)}, bf16[2,8,32,1536]{3,2,1,0:T(8,128)(2,1)}) custom-call(bf16[4,2,128,1536]{3,2,1,0:T(8,128)(2,1)} %bitcast.261, f32[2,128,1536]{2,1,0:T(8,128)} %copy-done, f32[1,1536]{1,0:T(1,128)S(1)} %copy-done.36, ...), custom_call_target="tpu_custom_call" | custom-call | tf_op jit(solution)/shard_map/pallas_call | solution.py:343
  898.6 49.0 %shard_map.251 = (bf16[2,3,32,1536]{3,2,1,0:T(8,128)(2,1)S(1)}, bf16[2,6,64,768]{3,2,1,0:T(8,128)(2,1)S(1)}) custom-call(bf16[2,3,32,1536]{3,2,1,0:T(8,128)(2,1)S(1)} %bitcast.253, bf16[2,6,64,768]{3,2,1,0:T(8,128)(2,1)S(1)} %bitcast.245), custom_call_target="tpu_custom_call" | custom-call | tf_op jit(solution)/shard_map/pallas_call | solution.py:343
  947.8 5.4 collective-permute-start.2
  955.6 1.9 select_bitcast_fusion.2
  957.5 2.1 select_bitcast_fusion.1
  966.5 1.7 fusion.37
  968.9 2.2 copy-done.41
  971.0 1.6 slice_bitcast_fusion.19
  972.7 1.5 copy.75
  974.2 3.0 copy.76
  977.1 3.2 slice_bitcast_fusion.18
  980.4 4.8 fusion.16
  985.2 4.7 fusion.17
  989.9 4.4 fusion.18
  (285 shorter events, 42.2 us)
Async XLA Ops:
  7.2 50.4 %all-gather.17.cloned.1.call-start = ((), (), s32[]{:S(2)}) async-start(), calls=%async_computation.24 | async-start | bytes 14155776 | tf_op jit(solution)/shard_map/all_gather | solution.py:1044
  15.6 111.9 %all-gather.9.cloned.1.call-start = ((), (), s32[]{:S(2)}) async-start(), calls=%async_computation.10 | async-start | bytes 3538944 | tf_op jit(solution)/shard_map/all_gather | solution.py:1044
  16.3 151.1 %all-gather.11.cloned.1.call-start = ((), (), s32[]{:S(2)}) async-start(), calls=%async_computation.11 | async-start | bytes 9437184 | tf_op jit(solution)/shard_map/all_gather | solution.py:1044
  17.1 159.2 %all-gather.13.cloned.1.call-start = ((), (), s32[]{:S(2)}) async-start(), calls=%async_computation.12 | async-start | bytes 9437184 | tf_op jit(solution)/shard_map/all_gather | solution.py:1044
  17.7 169.0 %all-gather.15.cloned.1.call-start = ((), (), s32[]{:S(2)}) async-start(), calls=%async_computation.13 | async-start | bytes 9437184 | tf_op jit(solution)/shard_map/all_gather | solution.py:1044
  18.6 13.3 %collective-permute-start = (bf16[2,128,768]{2,1,0:T(8,128)(2,1)}, bf16[2,128,768]{2,1,0:T(8,128)(2,1)}, u32[]{:S(2)}, u32[]{:S(2)}) collective-permute-start(bf16[2,128,768]{2,1,0:T(8,128)(2,1)} %get-tuple-element.232), channel_id=1, source_target_pairs={{0,16},{16,0},{1,17},{17,1},{2,18},{18,2},{3,19},{19,3},{4,20},{20... | collective-permute-start | bytes 1179656 | tf_op jit(solution)/shard_map/ppermute | solution.py:990
  19.9 34.6 %collective-permute-start.1 = (bf16[2,128,768]{2,1,0:T(8,128)(2,1)}, bf16[2,128,768]{2,1,0:T(8,128)(2,1)}, u32[]{:S(2)}, u32[]{:S(2)}) collective-permute-start(bf16[2,128,768]{2,1,0:T(8,128)(2,1)} %get-tuple-element.228), channel_id=1, source_target_pairs={{0,16},{16,0},{1,17},{17,1},{2,18},{18,2},{3,19},{19,3},{4,20},{20... | collective-permute-start | bytes 1179656 | tf_op jit(solution)/shard_map/ppermute | solution.py:990
  20.0 462.7 %reduce-scatter.11.cloned.1.call-start = ((), (), s32[]{:S(2)}) async-start(), calls=%async_computation.14 | async-start | bytes 4718592 | tf_op jit(solution)/shard_map/reduce_scatter | solution.py:1118
  25.0 6.7 copy-start.9
  25.2 6.5 copy-start.3
  26.1 7.1 copy-start.5
  31.8 100.7 %copy-start.37 = (f32[1,1536]{1,0:T(1,128)}, f32[1,1536]{1,0:T(1,128)S(1)}, u32[]{:S(2)}) copy-start(f32[1,1536]{1,0:T(1,128)S(1)} %get-tuple-element.237.gain.refs_2_) | copy-start | bytes 18436
  33.2 21.3 %copy-start.53 = (bf16[2,128,768]{2,1,0:T(8,128)(2,1)S(1)}, bf16[2,128,768]{2,1,0:T(8,128)(2,1)}, u32[]{:S(2)}) copy-start(bf16[2,128,768]{2,1,0:T(8,128)(2,1)} %get-tuple-element.227) | copy-start | bytes 1179652
  33.4 99.1 %copy-start = (f32[2,128,1536]{2,1,0:T(8,128)}, f32[2,128,1536]{2,1,0:T(8,128)S(1)}, u32[]{:S(2)}) copy-start(f32[2,128,1536]{2,1,0:T(8,128)S(1)} %get-tuple-element.200.h.refs_1_) | copy-start | bytes 4718596
  57.6 8.1 copy-start.39
  57.6 8.1 copy-start.54
  57.6 8.1 copy-start.57
  57.6 8.1 copy-start.61
  167.4 26.8 %copy-start.11 = (f32[2,128,1536]{2,1,0:T(8,128)}, f32[2,128,1536]{2,1,0:T(8,128)S(1)}, u32[]{:S(2)}) copy-start(f32[2,128,1536]{2,1,0:T(8,128)S(1)} %get-tuple-element.90.h.refs_1_) | copy-start | bytes 4718596
  228.3 59.3 %copy-start.12 = (f32[2,128,1536]{2,1,0:T(8,128)}, f32[2,128,1536]{2,1,0:T(8,128)S(1)}, u32[]{:S(2)}) copy-start(f32[2,128,1536]{2,1,0:T(8,128)S(1)} %get-tuple-element.95.h.refs_1_) | copy-start | bytes 4718596
  228.3 8.5 copy-start.40
  228.3 8.5 copy-start.42
  236.9 47.3 %copy-start.68 = (bf16[2,384,1536]{2,1,0:T(8,128)(2,1)S(1)}, bf16[2,384,1536]{2,1,0:T(8,128)(2,1)}, u32[]{:S(2)}) copy-start(bf16[2,384,1536]{2,1,0:T(8,128)(2,1)} %all-gather.9.cloned.1.call-done) | copy-start | bytes 7077892
  237.7 49.9 %copy-start.2 = (bf16[1024,768]{1,0:T(8,128)(2,1)}, bf16[1024,768]{1,0:T(8,128)(2,1)S(1)}, u32[]{:S(2)}) copy-start(bf16[1024,768]{1,0:T(8,128)(2,1)S(1)} %fusion.13) | copy-start | bytes 4718596
  284.1 37.6 %slice-start = ((s8[6291456]{0:T(1024)(128)(4,1)}), s8[4194304]{0:T(1024)(128)(4,1)S(1)}, s32[]{:S(2)}) async-start(s8[6291456]{0:T(1024)(128)(4,1)} %bitcast.278), calls=%async_computation.25 | async-start | bytes 8388608
  284.1 37.6 %slice-start.1 = ((s8[6291456]{0:T(1024)(128)(4,1)}), s8[2097152]{0:T(1024)(128)(4,1)S(1)}, s32[]{:S(2)}) async-start(s8[6291456]{0:T(1024)(128)(4,1)} %bitcast.278), calls=%async_computation.26 | async-start | bytes 4194304
  287.6 41.6 %slice-start.4 = ((s8[6291456]{0:T(1024)(128)(4,1)}), s8[2097152]{0:T(1024)(128)(4,1)S(1)}, s32[]{:S(2)}) async-start(s8[6291456]{0:T(1024)(128)(4,1)} %bitcast.282), calls=%async_computation.29 | async-start | bytes 4194304
  321.7 57.3 %copy-start.13 = (f32[2,128,1536]{2,1,0:T(8,128)}, f32[2,128,1536]{2,1,0:T(8,128)S(1)}, u32[]{:S(2)}) copy-start(f32[2,128,1536]{2,1,0:T(8,128)S(1)} %get-tuple-element.98.refs_1_.refs_10_) | copy-start | bytes 4718596
  321.7 7.4 slice-start.5
  321.7 7.4 copy-start.66
  321.8 12.5 %slice-start.2 = ((s8[6291456]{0:T(1024)(128)(4,1)}), s8[4194304]{0:T(1024)(128)(4,1)S(1)}, s32[]{:S(2)}) async-start(s8[6291456]{0:T(1024)(128)(4,1)} %bitcast.280), calls=%async_computation.27 | async-start | bytes 8388608
  329.2 5.1 slice-start.3
  329.2 5.1 copy-start.67
  329.2 5.1 copy-start.73
  364.4 6.1 copy-start.78
  377.4 105.3 %reduce-scatter.13.cloned.1.call-start = ((), (), s32[]{:S(2)}) async-start(), calls=%async_computation.15 | async-start | bytes 4718592 | tf_op jit(solution)/shard_map/reduce_scatter | solution.py:1118
  378.2 230.8 %reduce-scatter.15.cloned.1.call-start = ((), (), s32[]{:S(2)}) async-start(), calls=%async_computation.16 | async-start | bytes 4718592 | tf_op jit(solution)/shard_map/reduce_scatter | solution.py:1118
  378.9 230.0 %reduce-scatter.17.cloned.1.call-start = ((), (), s32[]{:S(2)}) async-start(), calls=%async_computation.17 | async-start | bytes 1769472 | tf_op jit(solution)/shard_map/reduce_scatter | solution.py:1118
  379.0 39.4 %slice-start.6 = ((s8[6291456]{0:T(1024)(128)(4,1)}), s8[4194304]{0:T(1024)(128)(4,1)S(1)}, s32[]{:S(2)}) async-start(s8[6291456]{0:T(1024)(128)(4,1)} %bitcast.284), calls=%async_computation.31 | async-start | bytes 8388608
  423.3 46.6 %copy-start.46 = (bf16[4,2,128,1536]{3,2,1,0:T(8,128)(2,1)S(1)}, bf16[4,2,128,1536]{3,2,1,0:T(8,128)(2,1)}, u32[]{:S(2)}) copy-start(bf16[4,2,128,1536]{3,2,1,0:T(8,128)(2,1)} %get-tuple-element.99) | copy-start | bytes 9437188
  472.3 6.6 copy-start.65
  472.3 6.6 copy-start.70
  482.8 126.1 %reduce-scatter.19.cloned.1.call-start = ((), (), s32[]{:S(2)}) async-start(), calls=%async_computation.18 | async-start | bytes 3538944 | tf_op jit(solution)/shard_map/reduce_scatter | solution.py:1118
  482.8 80.7 %copy-start.76 = (bf16[1024,1024]{1,0:T(8,128)(2,1)S(1)}, bf16[1024,1024]{1,0:T(8,128)(2,1)}, u32[]{:S(2)}) copy-start(bf16[1024,1024]{1,0:T(8,128)(2,1)} %get-tuple-element.243) | copy-start | bytes 6291460
  570.3 185.7 %reduce-scatter.21.cloned.1.call-start = ((), (), s32[]{:S(2)}) async-start(), calls=%async_computation.19 | async-start | bytes 4718592 | tf_op jit(solution)/shard_map/reduce_scatter | solution.py:1118
  570.4 12.7 %copy-start.64 = (bf16[4,2,128,1536]{3,2,1,0:T(8,128)(2,1)S(1)}, bf16[4,2,128,1536]{3,2,1,0:T(8,128)(2,1)}, u32[]{:S(2)}) copy-start(bf16[4,2,128,1536]{3,2,1,0:T(8,128)(2,1)} %get-tuple-element.89) | copy-start | bytes 9437188
  595.8 6.1 copy-start.79
  609.0 147.1 %reduce-scatter.23.cloned.1.call-start = ((), (), s32[]{:S(2)}) async-start(), calls=%async_computation.20 | async-start | bytes 4718592 | tf_op jit(solution)/shard_map/reduce_scatter | solution.py:1118
  609.6 146.5 %reduce-scatter.25.cloned.1.call-start = ((), (), s32[]{:S(2)}) async-start(), calls=%async_computation.21 | async-start | bytes 4718592 | tf_op jit(solution)/shard_map/reduce_scatter | solution.py:1118
  610.3 285.9 %reduce-scatter.27.cloned.1.call-start = ((), (), s32[]{:S(2)}) async-start(), calls=%async_computation.22 | async-start | bytes 1769472 | tf_op jit(solution)/shard_map/reduce_scatter | solution.py:1118
  613.0 82.7 %copy-start.69 = (bf16[2,384,1536]{2,1,0:T(8,128)(2,1)S(1)}, bf16[2,384,1536]{2,1,0:T(8,128)(2,1)}, u32[]{:S(2)}) copy-start(bf16[2,384,1536]{2,1,0:T(8,128)(2,1)} %all-gather.9.cloned.1.call-done) | copy-start | bytes 7077892
  699.9 44.0 %copy-start.29 = (bf16[4,2,128,384]{3,2,1,0:T(8,128)(2,1)S(1)}, bf16[4,2,128,384]{3,2,1,0:T(8,128)(2,1)}, u32[]{:S(2)}) copy-start(bf16[4,2,128,384]{3,2,1,0:T(8,128)(2,1)} %copy-done.28) | copy-start | bytes 2359300
  699.9 44.0 %copy-start.45 = (bf16[4,2,128,1536]{3,2,1,0:T(8,128)(2,1)S(1)}, bf16[4,2,128,1536]{3,2,1,0:T(8,128)(2,1)}, u32[]{:S(2)}) copy-start(bf16[4,2,128,1536]{3,2,1,0:T(8,128)(2,1)} %get-tuple-element.120) | copy-start | bytes 9437188
  746.4 5.8 copy-start.15
  756.1 140.1 %reduce-scatter.29.cloned.1.call-start = ((), (), s32[]{:S(2)}) async-start(), calls=%async_computation.23 | async-start | bytes 3538944 | tf_op jit(solution)/shard_map/reduce_scatter | solution.py:1118
  947.8 15.9 %collective-permute-start.2 = (bf16[2,128,768]{2,1,0:T(8,128)(2,1)S(1)}, bf16[2,128,768]{2,1,0:T(8,128)(2,1)S(1)}, u32[]{:S(2)}, u32[]{:S(2)}) collective-permute-start(bf16[2,128,768]{2,1,0:T(8,128)(2,1)S(1)} %get-tuple-element.222), channel_id=1, source_target_pairs={{0,16},{16,0},{1,17},{17,1},{2,18},{18,2},{3,19},{19,3},{4,20},{20... | collective-permute-start | bytes 1179656 | tf_op jit(solution)/shard_map/ppermute | solution.py:990
  953.7 11.0 %collective-permute-start.3 = (bf16[2,128,768]{2,1,0:T(8,128)(2,1)S(1)}, bf16[2,128,768]{2,1,0:T(8,128)(2,1)S(1)}, u32[]{:S(2)}, u32[]{:S(2)}) collective-permute-start(bf16[2,128,768]{2,1,0:T(8,128)(2,1)S(1)} %select_convert_fusion), channel_id=1, source_target_pairs={{0,16},{16,0},{1,17},{17,1},{2,18},{18,2},{3,19},{19,3},{4,20},{20... | collective-permute-start | bytes 1179656 | tf_op jit(solution)/shard_map/ppermute | solution.py:990
  953.8 8.2 collective-permute-start.4
  954.7 13.5 %collective-permute-start.5 = (bf16[768,768]{1,0:T(8,128)(2,1)S(1)}, bf16[768,768]{1,0:T(8,128)(2,1)S(1)}, u32[]{:S(2)}, u32[]{:S(2)}) collective-permute-start(bf16[768,768]{1,0:T(8,128)(2,1)S(1)} %get-tuple-element.216), channel_id=1, source_target_pairs={{0,16},{16,0},{1,17},{17,1},{2,18},{18,2},{3,19},{19,3},{4,20},{20... | collective-permute-start | bytes 3538952 | tf_op jit(solution)/shard_map/ppermute | solution.py:990
  954.9 11.6 %collective-permute-start.6 = (bf16[192,1536]{1,0:T(8,128)(2,1)S(1)}, bf16[192,1536]{1,0:T(8,128)(2,1)S(1)}, u32[]{:S(2)}, u32[]{:S(2)}) collective-permute-start(bf16[192,1536]{1,0:T(8,128)(2,1)S(1)} %get-tuple-element.220), channel_id=1, source_target_pairs={{0,16},{16,0},{1,17},{17,1},{2,18},{18,2},{3,19},{19,3},{4,20},{20... | collective-permute-start | bytes 1769480 | tf_op jit(solution)/shard_map/ppermute | solution.py:990
  962.0 18.4 %collective-permute-start.7 = (bf16[768,1024]{1,0:T(8,128)(2,1)}, bf16[768,1024]{1,0:T(8,128)(2,1)}, u32[]{:S(2)}, u32[]{:S(2)}) collective-permute-start(bf16[768,1024]{1,0:T(8,128)(2,1)} %get-tuple-element.214), channel_id=1, source_target_pairs={{0,16},{16,0},{1,17},{17,1},{2,18},{18,2},{3,19},{19,3},{4,20},{20... | collective-permute-start | bytes 4718600 | tf_op jit(solution)/shard_map/ppermute | solution.py:990
  963.7 21.5 %collective-permute-start.8 = (bf16[768,1024]{1,0:T(8,128)(2,1)}, bf16[768,1024]{1,0:T(8,128)(2,1)}, u32[]{:S(2)}, u32[]{:S(2)}) collective-permute-start(bf16[768,1024]{1,0:T(8,128)(2,1)} %get-tuple-element.212), channel_id=1, source_target_pairs={{0,16},{16,0},{1,17},{17,1},{2,18},{18,2},{3,19},{19,3},{4,20},{20... | collective-permute-start | bytes 4718600 | tf_op jit(solution)/shard_map/ppermute | solution.py:990
  964.7 25.2 %collective-permute-start.9 = (bf16[512,1536]{1,0:T(8,128)(2,1)}, bf16[512,1536]{1,0:T(8,128)(2,1)}, u32[]{:S(2)}, u32[]{:S(2)}) collective-permute-start(bf16[512,1536]{1,0:T(8,128)(2,1)} %get-tuple-element.210), channel_id=1, source_target_pairs={{0,16},{16,0},{1,17},{17,1},{2,18},{18,2},{3,19},{19,3},{4,20},{20... | collective-permute-start | bytes 4718600 | tf_op jit(solution)/shard_map/ppermute | solution.py:990
  974.2 6.2 copy-start.44
  (49 other events, 126.6 us)
Sparse Core Ops, SparseCore 0:
  15.7 24.5 all-gather.16
  41.8 12.1 all-gather.8
  55.5 17.9 all-gather.10
  74.9 17.9 all-gather.12
  94.2 17.9 all-gather.14
  377.5 36.0 reduce-scatter.10
  416.0 12.0 reduce-scatter.12
  430.4 12.0 reduce-scatter.14
  482.9 43.2 reduce-scatter.16
  570.5 32.3 reduce-scatter.18
  609.1 33.2 reduce-scatter.20
  645.0 12.0 reduce-scatter.22
  659.5 12.0 reduce-scatter.24
  756.2 33.0 reduce-scatter.26
  792.1 11.0 reduce-scatter.28

commit v5 on v4

--- a/solution.py
+++ b/solution.py
@@ -40,10 +40,6 @@
     keys = lax.broadcasted_iota(jnp.int32, (length, length), 0)
     queries = lax.broadcasted_iota(jnp.int32, (length, length), 1)
     return keys <= queries
-
-
-def silu_product(gate, up):
-    return gate * jax.nn.sigmoid(gate) * up
 
 
 MESH = pl.DeviceIdType.MESH
@@ -338,8 +334,19 @@
     return [pltpu.SemaphoreType.DMA((n, 3)), pltpu.SemaphoreType.DMA((n, 3))]
 
 
-def call(kernel, out_shape, scratch, ident, *operands):
+def size_in_vmem(shape, dtype):
+    if len(shape) < 2:
+        return 4096
+    lanes = -(-shape[-1] // 128) * 128
+    rows = -(-shape[-2] // 16) * 16
+    return int(np.prod(shape[:-2])) * rows * lanes * jnp.dtype(dtype).itemsize
+
+
+def call(kernel, out_shape, scratch, ident, *operands, spare=10):
     vm = pl.BlockSpec(memory_space=pltpu.VMEM)
+    held = list(operands) + list(out_shape) + [v for v in scratch if hasattr(v, "memory_space")]
+    total = sum(size_in_vmem(v.shape, v.dtype) for v in held if v.dtype in (BF, F32))
+    limit = min(50 * 2**20, total + spare * 2**20)
     return pl.pallas_call(
         kernel,
         out_shape=out_shape,
@@ -347,7 +354,7 @@
         out_specs=(vm,) * len(out_shape),
         scratch_shapes=scratch,
         compiler_params=pltpu.CompilerParams(
-            collective_id=ident, has_side_effects=True, vmem_limit_bytes=50 * 2**20
+            collective_id=ident, has_side_effects=True, vmem_limit_bytes=limit
         ),
     )(*operands)
 
@@ -531,7 +538,7 @@
         ]
     operands = (part, h, gain, g) + (() if others is None else (others,)) + tuple(zs)
     res = call(
-        functools.partial(back_kernel, kind, len(zs)), out, scratch, ident, *operands
+        functools.partial(back_kernel, kind, len(zs)), out, scratch, ident, *operands, spare=50
     )
     return res[0], res[1], res[2 : 2 + len(zs)], res[2 + len(zs) :]
 
@@ -975,6 +982,155 @@
     )
 
 
+def feed_kernel(fwd, bwd, *refs):
+    refs = list(refs)
+
+    def take(size):
+        out = refs[:size]
+        del refs[:size]
+        return out
+
+    n2, w_gate, w_up, w_down = take(4)
+    gm = take(1)[0] if bwd else None
+    kept = take(2) if bwd and not fwd else None
+    if fwd:
+        y_ref = take(1)[0]
+    if fwd and not bwd:
+        keep = take(2)
+    if bwd:
+        part_ref, dw_gate, dw_up, dw_down = take(4)
+    accs = refs
+    step = pl.program_id(0)
+    last = pl.num_programs(0) - 1
+
+    def gather_up(out, acc, term):
+        @pl.when(step == 0)
+        def _():
+            acc[...] = term
+
+        @pl.when((step > 0) & (step < last))
+        def _():
+            acc[...] += term
+
+        @pl.when(step == last)
+        def _():
+            out[...] = (acc[...] + term).astype(BF)
+
+    if kept is None:
+        x = n2[...]
+        gate, up = nn(x, w_gate[...]), nn(x, w_up[...])
+    else:
+        gate, up = kept[0][...].astype(F32), kept[1][...].astype(F32)
+    sig = jax.nn.sigmoid(gate)
+    silu = gate * sig
+    act = (silu * up).astype(BF)
+    if fwd and not bwd:
+        keep[0][...] = gate.astype(BF)
+        keep[1][...] = up.astype(BF)
+    if fwd:
+        gather_up(y_ref, accs[0], nn(act, w_down[...]))
+    if bwd:
+        g = gm[...]
+        dact = nt(g, w_down[...])
+        dgate = (dact * up * (sig * (1.0 + gate * (1.0 - sig)))).astype(BF)
+        dup = (dact * silu).astype(BF)
+        gather_up(part_ref, accs[-1], nt(dgate, w_gate[...]) + nt(dup, w_up[...]))
+        x = n2[...]
+        dw_gate[...] = tn(x, dgate).astype(BF)
+        dw_up[...] = tn(x, dup).astype(BF)
+        dw_down[...] = tn(act, g).astype(BF)
+
+
+def feed_call(layer, n2, w_gate, w_up, w_down, gm=None, kept=None):
+    fwd, bwd = kept is None, gm is not None
+    rows, d = n2.shape
+    units = w_gate.shape[2]
+    tile = min(512, units)
+    once = pl.BlockSpec((rows, d), lambda i: (0, 0), pipeline_mode=pl.Buffered(1))
+    out_once = pl.BlockSpec((rows, d), lambda i: (0, 0))
+    weight = pl.BlockSpec((None, d, tile), lambda i: (layer, 0, i))
+    weight_down = pl.BlockSpec((None, tile, d), lambda i: (layer, i, 0))
+    col = pl.BlockSpec((d, tile), lambda i: (0, i))
+    row = pl.BlockSpec((tile, d), lambda i: (i, 0))
+    slab = pl.BlockSpec((rows, tile), lambda i: (0, i))
+    operands, in_specs = [n2, w_gate, w_up, w_down], [once, weight, weight, weight_down]
+    out, out_specs = [], []
+    if bwd:
+        operands.append(gm)
+        in_specs.append(once)
+    if bwd and not fwd:
+        operands += kept
+        in_specs += [slab, slab]
+    full = jax.ShapeDtypeStruct((rows, d), BF)
+    if fwd:
+        out.append(full)
+        out_specs.append(out_once)
+    if fwd and not bwd:
+        out += [jax.ShapeDtypeStruct((rows, units), BF)] * 2
+        out_specs += [slab, slab]
+    if bwd:
+        out += [full] + [jax.ShapeDtypeStruct((d, units), BF)] * 2
+        out.append(jax.ShapeDtypeStruct((units, d), BF))
+        out_specs += [out_once, col, col, row]
+    return pl.pallas_call(
+        functools.partial(feed_kernel, fwd, bwd),
+        grid=(units // tile,),
+        in_specs=in_specs,
+        out_specs=out_specs,
+        out_shape=out,
+        scratch_shapes=[pltpu.VMEM((rows, d), F32)] * (fwd + bwd),
+        compiler_params=pltpu.CompilerParams(vmem_limit_bytes=60 * 2**20),
+    )(*operands)
+
+
+def settle_kernel(sec, mine0, mine1, got, *outs):
+    def put(src):
+        at = 0
+        for out in outs:
+            width = out.shape[1]
+            out[...] = src[:, at : at + width].astype(F32)
+            at += width
+
+    other = pl.program_id(0) == 1
+
+    @pl.when(other)
+    def _():
+        put(got)
+
+    @pl.when(jnp.logical_not(other) & (sec[0] == 0))
+    def _():
+        put(mine0)
+
+    @pl.when(jnp.logical_not(other) & (sec[0] == 1))
+    def _():
+        put(mine1)
+
+
+def settle(sec, mine0, mine1, got, widths):
+    rows, width = got.shape
+    tile = 256 if rows % 256 == 0 else rows
+    blocks = rows // tile
+    block = (tile, width)
+    return pl.pallas_call(
+        settle_kernel,
+        grid_spec=pltpu.PrefetchScalarGridSpec(
+            num_scalar_prefetch=1,
+            grid=(2, blocks),
+            in_specs=[
+                pl.BlockSpec(block, lambda p, i, sec: (i * (1 - p) * (1 - sec[0]), 0)),
+                pl.BlockSpec(block, lambda p, i, sec: (i * (1 - p) * sec[0], 0)),
+                pl.BlockSpec(block, lambda p, i, sec: (i * p, 0)),
+            ],
+            out_specs=[
+                pl.BlockSpec((tile, w), lambda p, i, sec: (((p + sec[0]) % 2) * blocks + i, 0))
+                for w in widths
+            ],
+        ),
+        out_shape=[jax.ShapeDtypeStruct((2 * rows, w), F32) for w in widths],
+        compiler_params=pltpu.CompilerParams(vmem_limit_bytes=32 * 2**20),
+    )(sec, mine0, mine1, got)
+
+
 def turn_matrix(heads, total):
     half = HEAD_DIM // 2
     m = np.zeros((total, total), np.float32)
@@ -1048,7 +1204,20 @@
         both(jnp.concatenate([attn_gain, mlp_gain], 0)),
     )
 
+    def gain_of(layer, kind):
+        return gains2[layer, kind : kind + 1]
+
+    def tie(*values):
+        return lax.optimization_barrier(values)
+
+    flat = lambda v: v.reshape(rows, d)
+    a0, a1, m0, m1 = gain_of(0, 0), gain_of(1, 0), gain_of(0, 1), gain_of(1, 1)
+
+    h0 = x_own.astype(F32)
+    n1_0 = flat(norm_gather(x_own, a0))
+
     own = jnp.stack([ctx, 2 * n_ctx - 1 - ctx])
+    n1_0, own = tie(n1_0, own)
     offs = jnp.arange(length, dtype=jnp.int32)
     pos = own[:, None] * length + offs[None, :]
     freq = ROPE_BASE ** (-(jnp.arange(0, HEAD_DIM, 2).astype(F32) / HEAD_DIM))
@@ -1072,14 +1241,11 @@
             t,
             jnp.asarray(spread),
             (((1,), (0,)), ((), ())),
-            precision=lax.Precision.HIGHEST,
+            precision=lax.Precision.HIGH,
             preferred_element_type=F32,
         )
 
     cos_all, sin_all = wide_table(cos_r) + jnp.asarray(plain), wide_table(sin_r)
-
-    def gain_of(layer, kind):
-        return gains2[layer, kind : kind + 1]
 
     def attend(n1, layer, h=None):
         raw = nn(n1, wcat2[layer])
@@ -1090,20 +1256,8 @@
         part = nn(mix, wo2[layer]).astype(BF)
         return part.reshape(n_t, 2, sp, d), (qkv, kv_all, mix, mixt, lse, *full)
 
-    def feed(n2, layer):
-        gate, up = nn(n2, wg2[layer]), nn(n2, wu2[layer])
-        act = silu_product(gate, up).astype(BF)
-        part = nn(act, wd2[layer]).astype(BF)
-        return part.reshape(n_t, 2, sp, d), (gate, up, act)
-
-    def feed_back(gm, layer, kept):
-        gate, up, _ = kept
-        dact = nt(gm, wd2[layer])
-        _, pull = jax.vjp(silu_product, gate, up)
-        dgate, dup = pull(dact)
-        dgate, dup = dgate.astype(BF), dup.astype(BF)
-        part = (nt(dgate, wg2[layer]) + nt(dup, wu2[layer])).astype(BF)
-        return part.reshape(n_t, 2, sp, d), dgate, dup
+    def in_blocks(part):
+        return part.reshape(n_t, 2, sp, d)
 
     def attend_back(ga, layer, kept, *more):
         qkv, kv_all, _, mixt, lse = kept[:5]
@@ -1123,32 +1277,23 @@
     def cut(size, term):
         return term.reshape(2, -1, size, term.shape[1])
 
-    def tie(*values):
-        return lax.optimization_barrier(values)
-
-    flat = lambda v: v.reshape(rows, d)
-    a0, a1, m0, m1 = gain_of(0, 0), gain_of(1, 0), gain_of(0, 1), gain_of(1, 1)
-
-    h0 = x_own.astype(F32)
-    n1_0 = flat(norm_gather(x_own, a0))
     part, att0 = attend(n1_0, 0)
     h2_0, full = sum_norm_gather(part, h0, m0, 0)
     n2_0 = flat(full)
-    part, mlp0 = feed(n2_0, 0)
+    part, *kept0 = feed_call(0, n2_0, wg2, wu2, wd2)
+    part = in_blocks(part)
     h1, full = sum_norm_gather(part, h2_0, a1, 1)
     n1_1 = flat(full)
     part, att1 = attend(n1_1, 1, g_own)
     h2_1, full = sum_norm_gather(part, h1, m1, 2)
     n2_1 = flat(full)
-    y_part, mlp1 = feed(n2_1, 1)
 
     gm1 = flat(att1[5])
     def joined(zs):
         return [z.reshape(-1, z.shape[-1]) for z in zs]
 
-    part, dgate, dup = feed_back(gm1, 1, mlp1)
-    raw = (grad(n2_1, dgate), grad(n2_1, dup), grad(mlp1[2], gm1))
-    part, raw = tie(part, raw)
+    y_part, part, *raw = feed_call(1, n2_1, wg2, wu2, wd2, gm1)
+    y_part, part = in_blocks(y_part), in_blocks(part)
     wide1, down1 = halve(*raw[:2]), halve(raw[2])
     dh2_1, dm1, _, (full,) = back(part, h2_1, m1, g_own.astype(F32), 0, 5, ())
     ga = flat(full)
@@ -1159,8 +1304,8 @@
     zs = [cut(48, v) for v in wide1]
     g0, da1, wide1, (full,) = back(part, h1, a1, dh2_1, 1, 6, zs)
     gm0 = flat(full)
-    part, dgate, dup = feed_back(gm0, 0, mlp0)
-    raw = (grad(n2_0, dgate), grad(n2_0, dup), grad(mlp0[2], gm0))
+    part, *raw = feed_call(0, n2_0, wg2, wu2, wd2, gm0, kept0)
+    part = in_blocks(part)
     part, raw, rest1 = tie(part, raw, rest1)
     wide0 = halve(*raw)
     zs = [cut(size, v) for size, v in zip((32, 32, 64), rest1)]
@@ -1189,15 +1334,17 @@
             first, jnp.concatenate([keep, got], 0), jnp.concatenate([got, keep], 0)
         ).astype(F32)
 
-    gd, gg, gu, go, gqkv = (to_owner(a, b) for a, b in zip(grads0, grads1))
-    half_kv = kv_w // 2
+    gd, gg, gu, go = (to_owner(a, b) for a, b in zip(grads0[:4], grads1[:4]))
+    mine0, mine1 = grads0[4], grads1[4]
+    got = swap(jnp.where(first, mine1, mine0))
+    gq, gk, gv = settle(sec.reshape(1), mine0, mine1, got, (q_w, kv_w // 2, kv_w // 2))
     return (
         from_own(y, BF),
         from_own(dh0, F32),
         gain_own[0:1],
-        gqkv[None, :, :q_w],
-        gqkv[None, :, q_w : q_w + half_kv],
-        gqkv[None, :, q_w + half_kv :],
+        gq[None],
+        gk[None],
+        gv[None],
         go[None],
         gain_own[1:2],
         gg[None],

time: 1010 us -> 960 us (0.950)
  matrix products: 201 us -> 67.2 us
  Pallas kernels: 697 us -> 771 us
    pallas_call x0 -> x4, Pallas kernels: none -> 89.1 us  [the longest x3 86.4 us: feed_call(): pl.pallas_call(functools.partial(feed_kernel, fwd, bwd), grid=(units // t...]
    dot_general x13 -> x7, matrix products: 75.9 us -> 25.6 us  [nn(): lax.dot_general(a, b, (((1,), (0,)), ((), ())), preferred_element_type=F32)]
    dot_general x10 -> x4, matrix products: 63.5 us -> 20.9 us  [nt(): lax.dot_general(a, b, (((1,), (1,)), ((), ())), preferred_element_type=F32)]
    dot_general x10 -> x4, matrix products: 52.8 us -> 12.7 us  [tn(): lax.dot_general(a, b, (((0,), (0,)), ((), ())), preferred_element_type=F32)]
    pallas_call x13, Pallas kernels: 697 us -> 682 us  [call(): pl.pallas_call(kernel, out_shape=out_shape, in_specs=[vm] * len(operands)...]
    unnamed x182 -> x200, local copies, waits for them, and re-layouts: 26.6 us -> 36.2 us
  transfers between devices with their start and end apart: 25 -> 25, of which waited for: 0 -> 1; matrix products, arithmetic and copies ran while one was open for 17% -> 9% of each run, Pallas kernels for 53% -> 59%
where the time goes in v5:
time: 960 us; the launch traced here: 951 us
  Pallas kernels  771 us (80%)
  matrix products  67.2 us (7%)
  local copies, waits for them, and re-layouts  44 us (5%)
  other arithmetic  33.6 us (4%)
  between operations  16.3 us (2%)
  starting transfers between devices  10.2 us (1%)
    pallas_call x13, Pallas kernels, call(): pl.pallas_call(kernel, out_shape=out_shape, in_specs=[vm] * len(operands)...  682 us
    pallas_call x3, Pallas kernels, feed_call(): pl.pallas_call(functools.partial(feed_kernel, fwd, bwd), grid=(units // t...  86.4 us
    unnamed x200, local copies, waits for them, and re-layouts  36.2 us
    dot_general x7, matrix products, nn(): lax.dot_general(a, b, (((1,), (0,)), ((), ())), preferred_element_type=F32)  25.6 us
    dot_general x4, matrix products, nt(): lax.dot_general(a, b, (((1,), (1,)), ((), ())), preferred_element_type=F32)  20.9 us
  transfers between devices with their start and end apart: 25, of which 1 were waited for; matrix products, arithmetic and copies ran while one was open for 9% of the time, Pallas kernels for 59%

profile of v5, /device:TPU:0, one launch (start us, length us, event | category | flops | bytes accessed | tf_op | source)
XLA Modules:
  0.0 951.4 jit_solution(7256391782975635636)
XLA Ops:
  7.2 1.6 copy.61
  12.2 1.9 fusion.15
  14.1 1.5 fusion.17
  21.7 1.9 all-gather.2
  24.7 18.9 %shard_map.239 = bf16[4,2,128,1536]{3,2,1,0:T(8,128)(2,1)S(1)} custom-call(bf16[2,128,1536]{2,1,0:T(8,128)(2,1)S(1)} %get-tuple-element.238.h, f32[1,1536]{1,0:T(1,128)S(1)} %get-tuple-element.266.gain.refs_2_), custom_call_target="tpu_custom_call" | custom-call | tf_op jit(solution)/shard_map/pallas_call | solution.py:350
  43.7 1.7 copy-done.24
  45.5 1.4 fusion.26
  49.7 2.1 reshape.560
  51.8 1.6 maximum_select_fusion.8
  53.3 4.2 fusion.36
  57.6 1.6 fusion.29
  59.2 8.1 fusion.2
  67.3 3.7 fusion.7
  71.1 53.0 %shard_map.240 = (bf16[4,2,128,384]{3,2,1,0:T(8,128)(2,1)S(1)}, bf16[2,4,96,512]{3,2,1,0:T(8,128)(2,1)S(1)}, f32[2,4,1,512]{3,2,1,0:T(1,128)S(1)}, bf16[4,2,512,384]{3,2,1,0:T(8,128)(2,1)S(1)}) custom-call(bf16[4,2,128,768]{3,2,1,0:T(8,128)(2,1)S(1)} %bitcast.168), custom_call_target="tpu_custom_call" | custom-call | tf_op jit(solution)/shard_map/pallas_call | solution.py:350
  124.1 1.6 copy-done.26
  128.0 3.3 convolution_convert_fusion.3
  131.4 31.8 %shard_map.241 = (f32[2,128,1536]{2,1,0:T(8,128)S(1)}, bf16[4,2,128,1536]{3,2,1,0:T(8,128)(2,1)S(1)}) custom-call(bf16[4,2,128,1536]{3,2,1,0:T(8,128)(2,1)S(1)} %bitcast.188, f32[2,128,1536]{2,1,0:T(8,128)S(1)} %get-tuple-element.237.h.refs_1_, f32[1,1536]{1,0:T(1,128)S(1)} %get-tuple-element.265.gain.refs_2_), custom_call_target="tpu_custom_call" | custom-call | tf_op jit(solution)/shard_map/pallas_call | solution.py:350
  163.2 1.6 copy-done.1
  164.8 1.1 copy-done.11
  166.0 17.3 %shard_map.242 = (bf16[1024,1536]{1,0:T(8,128)(2,1)}, bf16[1024,1024]{1,0:T(8,128)(2,1)}, bf16[1024,1024]{1,0:T(8,128)(2,1)}) custom-call(bf16[1024,1536]{1,0:T(8,128)(2,1)} %bitcast.172, bf16[2,1536,1024]{2,1,0:T(8,128)(2,1)} %all-gather.11.cloned.1.call-done.refs_1_, bf16[2,1536,1024]{2,1,0:T(8,128)(2,1)} %all-gather.13.cloned.1.call-done.refs_2_, ...), custom_call_target="tpu_custom_call" | custom-call | tf_op jit(solution)/shard_map/pallas_call | solution.py:1075
  183.3 1.9 copy-done.23
  185.2 32.2 %shard_map.243 = (f32[2,128,1536]{2,1,0:T(8,128)S(1)}, bf16[4,2,128,1536]{3,2,1,0:T(8,128)(2,1)S(1)}) custom-call(bf16[4,2,128,1536]{3,2,1,0:T(8,128)(2,1)S(1)} %bitcast.186, f32[2,128,1536]{2,1,0:T(8,128)S(1)} %copy-done.12, f32[1,1536]{1,0:T(1,128)S(1)} %copy-done.50), custom_call_target="tpu_custom_call" | custom-call | tf_op jit(solution)/shard_map/pallas_call | solution.py:350
  217.5 8.7 fusion
  227.4 45.2 %shard_map.244 = (bf16[4,2,128,384]{3,2,1,0:T(8,128)(2,1)S(1)}, bf16[2,4,96,512]{3,2,1,0:T(8,128)(2,1)S(1)}, f32[2,4,1,512]{3,2,1,0:T(1,128)S(1)}, bf16[4,2,512,...) custom-call(bf16[4,2,128,768]{3,2,1,0:T(8,128)(2,1)S(1)} %bitcast.170, bf16[2,128,1536]{2,1,0:T(8,128)(2,1)S(1)} %copy-done.29), custom_call_target="tpu_custom_call" | custom-call | tf_op jit(solution)/shard_map/pallas_call | solution.py:350
  272.6 1.7 copy-done.28
  274.8 1.8 convolution_convert_fusion.2
  277.0 30.6 %shard_map.245 = (f32[2,128,1536]{2,1,0:T(8,128)S(1)}, bf16[4,2,128,1536]{3,2,1,0:T(8,128)(2,1)S(1)}) custom-call(bf16[4,2,128,1536]{3,2,1,0:T(8,128)(2,1)S(1)} %bitcast.187, f32[2,128,1536]{2,1,0:T(8,128)S(1)} %get-tuple-element.110.h.refs_1_, f32[1,1536]{1,0:T(1,128)S(1)} %copy-done.52), custom_call_target="tpu_custom_call" | custom-call | tf_op jit(solution)/shard_map/pallas_call | solution.py:350
  307.6 1.1 copy-done.14
  308.8 1.7 copy-done.20
  310.4 39.8 %shard_map.246 = (bf16[1024,1536]{1,0:T(8,128)(2,1)}, bf16[1024,1536]{1,0:T(8,128)(2,1)}, bf16[1536,1024]{1,0:T(8,128)(2,1)}, bf16[1536,1024]{1,0:T(8,128)(2,1)}, bf16[1024,1536]{1,0:T(8,128)(2,1)}) custom-call(bf16[1024,1536]{1,0:T(8,128)(2,1)} %bitcast.185, bf16[2,1536,1024]{2,1,0:T(8,128)(2,1)} %all-gather.11.cloned.1.call-done.refs_1_, ...), custom_call_target="tpu_custom_call" | custom-call | tf_op jit(solution)/shard_map/pallas_call | solution.py:1075
  351.8 1.4 copy-done.15
  353.9 34.8 %shard_map.247 = (f32[2,128,1536]{2,1,0:T(8,128)S(1)}, f32[1,1536]{1,0:T(1,128)S(1)}, bf16[4,2,128,1536]{3,2,1,0:T(8,128)(2,1)}) custom-call(bf16[4,2,128,1536]{3,2,1,0:T(8,128)(2,1)} %bitcast.212, f32[2,128,1536]{2,1,0:T(8,128)S(1)} %copy-done.15, f32[1,1536]{1,0:T(1,128)S(1)} %copy-done.53, f32[2,128,1536]{2,1,0:T(8,128)} %get-tuple-element.235.refs_3_), custom_call_target="tpu_custom_call" | custom-call | tf_op jit(solution)/shard_map/pallas_call | solution.py:350
  388.8 4.3 convolution_convert_fusion.7
  393.2 50.7 %shard_map.248 = (bf16[4,2,128,768]{3,2,1,0:T(8,128)(2,1)S(1)}, bf16[2,128,1536]{2,1,0:T(8,128)(2,1)S(1)}) custom-call(bf16[4,2,128,768]{3,2,1,0:T(8,128)(2,1)S(1)} %bitcast.171, bf16[4,2,512,384]{3,2,1,0:T(8,128)(2,1)} %copy-done.28, bf16[4,2,128,384]{3,2,1,0:T(8,128)(2,1)S(1)} %bitcast.202, bf16[2,4,96,512]{3,2,1,0:T(8,128)(2,1)S(1)} %copy-done.44, ...), custom_call_target="tpu_custom_call" | custom-call | tf_op jit(solution)/shard_map/pallas_call | solution.py:350
  444.8 1.1 copy-done.66
  445.9 2.4 fusion.11
  448.4 6.6 convolution_convert_fusion.1
  454.9 3.9 bitcast_convert_fusion
  459.5 77.2 %shard_map.249 = (bf16[2,128,1536]{2,1,0:T(8,128)(2,1)S(1)}, f32[1,1536]{1,0:T(1,128)S(1)}, bf16[2,8,48,1024]{3,2,1,0:T(8,128)(2,1)S(1)}, bf16[2,8,48,1024]{3,2,1,0:T(8,128)(2,1)S(1)}, bf16[4,2,128,1536]{3,2,1,0:T(8,128)(2,1)}) custom-call(bf16[4,2,128,1536]{3,2,1,0:T(8,128)(2,1)} %bitcast.217, f32[2,128,1536]{2,1,0:T(8,128)} %copy-done.13, ...), custom_call_target="tpu_custom_call" | custom-call | tf_op jit(solution)/shard_map/pallas_call | solution.py:350
  539.9 29.3 %shard_map.250 = (bf16[1024,1536]{1,0:T(8,128)(2,1)}, bf16[1536,1024]{1,0:T(8,128)(2,1)}, bf16[1536,1024]{1,0:T(8,128)(2,1)}, bf16[1024,1536]{1,0:T(8,128)(2,1)}) custom-call(bf16[1024,1536]{1,0:T(8,128)(2,1)} %bitcast.173, bf16[2,1536,1024]{2,1,0:T(8,128)(2,1)} %all-gather.11.cloned.1.call-done.refs_1_, ...), custom_call_target="tpu_custom_call" | custom-call | tf_op jit(solution)/shard_map/pallas_call | solution.py:1075
  570.8 2.5 convert_element_type.123.refs_3_
  573.4 77.0 %shard_map.251 = (f32[2,128,1536]{2,1,0:T(8,128)}, f32[1,1536]{1,0:T(1,128)S(1)}, bf16[2,8,32,1536]{3,2,1,0:T(8,128)(2,1)}, bf16[2,3,32,1536]{3,2,1,0:T(8,128)(2...) custom-call(bf16[4,2,128,1536]{3,2,1,0:T(8,128)(2,1)} %bitcast.210, ...), custom_call_target="tpu_custom_call" | custom-call | tf_op jit(solution)/shard_map/pallas_call | solution.py:350
  650.5 4.3 convolution_convert_fusion.6
  655.0 37.9 %shard_map.252 = bf16[4,2,128,768]{3,2,1,0:T(8,128)(2,1)S(1)} custom-call(bf16[4,2,128,768]{3,2,1,0:T(8,128)(2,1)S(1)} %bitcast.169, bf16[4,2,512,384]{3,2,1,0:T(8,128)(2,1)S(1)} %copy-done.27, bf16[4,2,128,384]{3,2,1,0:T(8,128)(2,1)S(1)} %bitcast.203, bf16[2,4,96,512]{3,2,1,0:T(8,128)(2,1)S(1)} %copy-done.40, f32[2,4,1,512]{3,2,1,0:T(1,128)S(1)} %copy-done.55, ...), custom_call_target="tpu_custom_call" | custom-call | tf_op jit(solution)/shard_map/pallas_call | solution.py:350
  692.9 2.4 fusion.12
  695.3 5.7 convolution_convert_fusion
  701.0 3.9 convolution_convert_fusion.4
  705.7 145.5 %shard_map.253 = (f32[2,128,1536]{2,1,0:T(8,128)S(1)}, f32[8,1536]{1,0:T(8,128)S(1)}, bf16[2,8,48,1024]{3,2,1,0:T(8,128)(2,1)S(1)}, bf16[2,8,48,1024]{3,2,1,0:T(8,128)(2,1)}, bf16[2,8,32,1536]{3,2,1,0:T(8,128)(2,1)}) custom-call(bf16[4,2,128,1536]{3,2,1,0:T(8,128)(2,1)} %bitcast.215, f32[2,128,1536]{2,1,0:T(8,128)} %copy-done, ...), custom_call_target="tpu_custom_call" | custom-call | tf_op jit(solution)/shard_map/pallas_call | solution.py:350
  851.3 1.3 copy-done.36
  853.6 47.3 %shard_map.254 = (bf16[2,3,32,1536]{3,2,1,0:T(8,128)(2,1)S(1)}, bf16[2,6,64,768]{3,2,1,0:T(8,128)(2,1)S(1)}) custom-call(bf16[2,3,32,1536]{3,2,1,0:T(8,128)(2,1)S(1)} %bitcast.206, bf16[2,6,64,768]{3,2,1,0:T(8,128)(2,1)S(1)} %bitcast.199), custom_call_target="tpu_custom_call" | custom-call | tf_op jit(solution)/shard_map/pallas_call | solution.py:350
  901.5 1.2 copy-done.78
  903.2 1.9 select_bitcast_fusion
  905.1 5.5 collective-permute-start.9
  910.6 1.9 select_bitcast_fusion.1
  915.7 1.9 select_bitcast_fusion.2
  920.1 1.2 collective-permute-done.3
  921.7 1.3 maximum_select_fusion.4
  923.0 1.7 fusion.20
  924.7 2.8 shard_map.255
  927.5 1.5 copy.69
  928.9 1.5 copy.70
  930.4 4.5 fusion.10
  934.9 4.8 fusion.9
  939.7 4.7 fusion.8
  (283 shorter events, 34.8 us)
Async XLA Ops:
  7.2 52.0 %all-gather.17.cloned.1.call-start = ((), (), s32[]{:S(2)}) async-start(), calls=%async_computation.24 | async-start | bytes 14155776 | tf_op jit(solution)/shard_map/all_gather | solution.py:1200
  15.6 112.5 %all-gather.9.cloned.1.call-start = ((), (), s32[]{:S(2)}) async-start(), calls=%async_computation.10 | async-start | bytes 3538944 | tf_op jit(solution)/shard_map/all_gather | solution.py:1200
  16.3 149.7 %all-gather.11.cloned.1.call-start = ((), (), s32[]{:S(2)}) async-start(), calls=%async_computation.11 | async-start | bytes 9437184 | tf_op jit(solution)/shard_map/all_gather | solution.py:1200
  17.1 148.9 %all-gather.13.cloned.1.call-start = ((), (), s32[]{:S(2)}) async-start(), calls=%async_computation.12 | async-start | bytes 9437184 | tf_op jit(solution)/shard_map/all_gather | solution.py:1200
  17.6 148.3 %all-gather.15.cloned.1.call-start = ((), (), s32[]{:S(2)}) async-start(), calls=%async_computation.13 | async-start | bytes 9437184 | tf_op jit(solution)/shard_map/all_gather | solution.py:1200
  18.3 6.0 collective-permute-start
  19.7 32.0 %collective-permute-start.1 = (bf16[2,128,768]{2,1,0:T(8,128)(2,1)}, bf16[2,128,768]{2,1,0:T(8,128)(2,1)}, u32[]{:S(2)}, u32[]{:S(2)}) collective-permute-start(bf16[2,128,768]{2,1,0:T(8,128)(2,1)} %get-tuple-element.256), channel_id=1, source_target_pairs={{0,16},{16,0},{1,17},{17,1},{2,18},{18,2},{3,19},{19,3},{4,20},{20... | collective-permute-start | bytes 1179656 | tf_op jit(solution)/shard_map/ppermute | solution.py:1146
  19.8 439.0 %reduce-scatter.11.cloned.1.call-start = ((), (), s32[]{:S(2)}) async-start(), calls=%async_computation.14 | async-start | bytes 4718592 | tf_op jit(solution)/shard_map/reduce_scatter | solution.py:1272
  24.7 106.6 %copy-start = (f32[2,128,1536]{2,1,0:T(8,128)}, f32[2,128,1536]{2,1,0:T(8,128)S(1)}, u32[]{:S(2)}) copy-start(f32[2,128,1536]{2,1,0:T(8,128)S(1)} %get-tuple-element.237.h.refs_1_) | copy-start | bytes 4718596
  24.7 20.7 %copy-start.91 = (f32[48]{0:T(128)S(1)}, f32[48]{0:T(128)}, u32[]{:S(2)}) copy-start(f32[48]{0:T(128)} %negate_power_fusion) | copy-start | bytes 580
  46.9 4.8 copy-start.8
  47.2 6.2 copy-start.2
  48.7 8.8 copy-start.5
  59.2 8.1 copy-start.68
  59.2 8.1 copy-start.81
  59.2 8.1 copy-start.83
  59.2 8.1 copy-start.87
  166.0 17.3 %copy-start.12 = (f32[2,128,1536]{2,1,0:T(8,128)S(1)}, f32[2,128,1536]{2,1,0:T(8,128)}, u32[]{:S(2)}) copy-start(f32[2,128,1536]{2,1,0:T(8,128)} %copy-done.11) | copy-start | bytes 4718596
  166.0 17.3 %copy-start.50 = (f32[1,1536]{1,0:T(1,128)S(1)}, f32[1,1536]{1,0:T(1,128)}, u32[]{:S(2)}) copy-start(f32[1,1536]{1,0:T(1,128)} %get-tuple-element.264.gain.refs_2_) | copy-start | bytes 18436
  217.4 8.8 copy-start.64
  217.4 59.6 %copy-start.13 = (f32[2,128,1536]{2,1,0:T(8,128)}, f32[2,128,1536]{2,1,0:T(8,128)S(1)}, u32[]{:S(2)}) copy-start(f32[2,128,1536]{2,1,0:T(8,128)S(1)} %get-tuple-element.110.h.refs_1_) | copy-start | bytes 4718596
  217.5 8.7 copy-start.69
  217.5 8.7 copy-start.70
  217.5 8.7 copy-start.88
  227.1 47.7 %copy-start.92 = (bf16[2,384,1536]{2,1,0:T(8,128)(2,1)S(1)}, bf16[2,384,1536]{2,1,0:T(8,128)(2,1)}, u32[]{:S(2)}) copy-start(bf16[2,384,1536]{2,1,0:T(8,128)(2,1)} %all-gather.9.cloned.1.call-done) | copy-start | bytes 7077892
  350.3 108.6 %reduce-scatter.13.cloned.1.call-start = ((), (), s32[]{:S(2)}) async-start(), calls=%async_computation.15 | async-start | bytes 4718592 | tf_op jit(solution)/shard_map/reduce_scatter | solution.py:1272
  351.0 218.2 %reduce-scatter.15.cloned.1.call-start = ((), (), s32[]{:S(2)}) async-start(), calls=%async_computation.16 | async-start | bytes 4718592 | tf_op jit(solution)/shard_map/reduce_scatter | solution.py:1272
  351.8 217.4 %reduce-scatter.17.cloned.1.call-start = ((), (), s32[]{:S(2)}) async-start(), calls=%async_computation.17 | async-start | bytes 1769472 | tf_op jit(solution)/shard_map/reduce_scatter | solution.py:1272
  353.9 34.8 %copy-start.93 = (bf16[2,384,1536]{2,1,0:T(8,128)(2,1)S(1)}, bf16[2,384,1536]{2,1,0:T(8,128)(2,1)}, u32[]{:S(2)}) copy-start(bf16[2,384,1536]{2,1,0:T(8,128)(2,1)} %all-gather.9.cloned.1.call-done) | copy-start | bytes 7077892
  393.2 52.7 %copy-start.42 = (bf16[4,2,128,384]{3,2,1,0:T(8,128)(2,1)S(1)}, bf16[4,2,128,384]{3,2,1,0:T(8,128)(2,1)}, u32[]{:S(2)}) copy-start(bf16[4,2,128,384]{3,2,1,0:T(8,128)(2,1)} %copy-done.41) | copy-start | bytes 2359300
  393.2 52.7 %copy-start.75 = (bf16[4,2,128,1536]{3,2,1,0:T(8,128)(2,1)S(1)}, bf16[4,2,128,1536]{3,2,1,0:T(8,128)(2,1)}, u32[]{:S(2)}) copy-start(bf16[4,2,128,1536]{3,2,1,0:T(8,128)(2,1)} %get-tuple-element.115) | copy-start | bytes 9437188
  448.3 6.6 copy-start.65
  448.3 6.6 copy-start.67
  458.9 110.4 %reduce-scatter.19.cloned.1.call-start = ((), (), s32[]{:S(2)}) async-start(), calls=%async_computation.18 | async-start | bytes 3538944 | tf_op jit(solution)/shard_map/reduce_scatter | solution.py:1272
  459.5 245.5 %reduce-scatter.21.cloned.1.call-start = ((), (), s32[]{:S(2)}) async-start(), calls=%async_computation.19 | async-start | bytes 4718592 | tf_op jit(solution)/shard_map/reduce_scatter | solution.py:1272
  539.9 29.3 %copy-start.60 = (f32[1,1536]{1,0:T(1,128)}, f32[1,1536]{1,0:T(1,128)S(1)}, u32[]{:S(2)}) copy-start(f32[1,1536]{1,0:T(1,128)S(1)} %get-tuple-element.154) | copy-start | bytes 18436
  569.3 135.8 %reduce-scatter.23.cloned.1.call-start = ((), (), s32[]{:S(2)}) async-start(), calls=%async_computation.20 | async-start | bytes 4718592 | tf_op jit(solution)/shard_map/reduce_scatter | solution.py:1272
  569.9 135.2 %reduce-scatter.25.cloned.1.call-start = ((), (), s32[]{:S(2)}) async-start(), calls=%async_computation.21 | async-start | bytes 4718592 | tf_op jit(solution)/shard_map/reduce_scatter | solution.py:1272
  570.6 280.6 %reduce-scatter.27.cloned.1.call-start = ((), (), s32[]{:S(2)}) async-start(), calls=%async_computation.22 | async-start | bytes 1769472 | tf_op jit(solution)/shard_map/reduce_scatter | solution.py:1272
  573.4 77.1 %copy-start.94 = (bf16[2,384,1536]{2,1,0:T(8,128)(2,1)S(1)}, bf16[2,384,1536]{2,1,0:T(8,128)(2,1)}, u32[]{:S(2)}) copy-start(bf16[2,384,1536]{2,1,0:T(8,128)(2,1)} %all-gather.9.cloned.1.call-done) | copy-start | bytes 7077892
  650.4 4.5 copy-start.17
  650.4 4.4 copy-start.47
  650.4 4.4 copy-start.62
  650.4 4.4 copy-start.4
  650.4 4.4 copy-start.7
  650.5 4.4 copy-start.10
  650.5 4.4 copy-start.27
  654.9 37.9 %copy-start.38 = (bf16[4,2,128,384]{3,2,1,0:T(8,128)(2,1)S(1)}, bf16[4,2,128,384]{3,2,1,0:T(8,128)(2,1)}, u32[]{:S(2)}) copy-start(bf16[4,2,128,384]{3,2,1,0:T(8,128)(2,1)} %copy-done.37) | copy-start | bytes 2359300
  654.9 37.9 %copy-start.74 = (bf16[4,2,128,1536]{3,2,1,0:T(8,128)(2,1)S(1)}, bf16[4,2,128,1536]{3,2,1,0:T(8,128)(2,1)}, u32[]{:S(2)}) copy-start(bf16[4,2,128,1536]{3,2,1,0:T(8,128)(2,1)} %get-tuple-element.143) | copy-start | bytes 9437188
  695.3 5.8 copy-start.25
  705.1 146.2 %reduce-scatter.29.cloned.1.call-start = ((), (), s32[]{:S(2)}) async-start(), calls=%async_computation.23 | async-start | bytes 3538944 | tf_op jit(solution)/shard_map/reduce_scatter | solution.py:1272
  903.2 7.4 copy-start.34
  903.2 7.4 copy-start.79
  905.1 8.5 copy-start.48
  905.1 25.3 %collective-permute-start.9 = (bf16[512,1536]{1,0:T(8,128)(2,1)}, bf16[512,1536]{1,0:T(8,128)(2,1)}, u32[]{:S(2)}, u32[]{:S(2)}) collective-permute-start(bf16[512,1536]{1,0:T(8,128)(2,1)} %get-tuple-element.240), channel_id=1, source_target_pairs={{0,16},{16,0},{1,17},{17,1},{2,18},{18,2},{3,19},{19,3},{4,20},{20... | collective-permute-start | bytes 4718600 | tf_op jit(solution)/shard_map/ppermute | solution.py:1146
  912.5 22.5 %collective-permute-start.8 = (bf16[768,1024]{1,0:T(8,128)(2,1)}, bf16[768,1024]{1,0:T(8,128)(2,1)}, u32[]{:S(2)}, u32[]{:S(2)}) collective-permute-start(bf16[768,1024]{1,0:T(8,128)(2,1)} %get-tuple-element.242), channel_id=1, source_target_pairs={{0,16},{16,0},{1,17},{17,1},{2,18},{18,2},{3,19},{19,3},{4,20},{20... | collective-permute-start | bytes 4718600 | tf_op jit(solution)/shard_map/ppermute | solution.py:1146
  913.7 9.3 collective-permute-start.6
  913.7 4.0 collective-permute-start.4
  914.5 3.8 collective-permute-start.2
  917.7 7.0 collective-permute-start.5
  918.3 3.0 collective-permute-start.3
  921.3 18.4 %collective-permute-start.7 = (bf16[768,1024]{1,0:T(8,128)(2,1)}, bf16[768,1024]{1,0:T(8,128)(2,1)}, u32[]{:S(2)}, u32[]{:S(2)}) collective-permute-start(bf16[768,1024]{1,0:T(8,128)(2,1)} %get-tuple-element.244), channel_id=1, source_target_pairs={{0,16},{16,0},{1,17},{17,1},{2,18},{18,2},{3,19},{19,3},{4,20},{20... | collective-permute-start | bytes 4718600 | tf_op jit(solution)/shard_map/ppermute | solution.py:1146
  930.4 4.5 copy-start.72
  934.9 4.8 copy-start.73
  (58 other events, 120.5 us)
Sparse Core Ops, SparseCore 0:
  15.7 24.5 all-gather.16
  41.8 12.1 all-gather.8
  55.5 17.9 all-gather.10
  74.9 17.9 all-gather.12
  94.2 17.9 all-gather.14
  350.4 39.0 reduce-scatter.10
  391.8 12.0 reduce-scatter.12
  406.2 12.0 reduce-scatter.14
  459.0 45.3 reduce-scatter.16
  507.0 11.0 reduce-scatter.18
  569.4 34.7 reduce-scatter.20
  606.3 12.0 reduce-scatter.22
  620.7 12.0 reduce-scatter.24
  705.2 37.8 reduce-scatter.26
  745.9 11.0 reduce-scatter.28
